TPU v7x, 128 devices: a whole 4x4x4 slice. The times are simulated.
128 devices in a mesh: src: 4 (over x), grp: 32 (over z, y, core).
Axes of the slice: x: 4, y: 4, z: 4, core: 2. Of those that a mesh axis runs over, the one named last changes fastest.
Arguments:
- source_points: bfloat16 [32768, 64], P('src'), may hold values from -6 to 6
- source_logmass: float32 [32768], P('src'), may hold values from -1 to 1
- target_points: bfloat16 [524288, 64], P(('src', 'grp')), may hold values from -1.796875 to 1.796875
- target_logmass: float32 [524288], P(('src', 'grp')), may hold values from -1 to 1
- target_potential: float32 [524288], P(('src', 'grp')), may hold values from -1.5 to 61.5
- tile_slot: int32 [256, 256], P('src', 'grp'), may hold values from 0 to 31, as said below
- tile_counts: int32 [256, 32], P('src', 'grp'), may hold values from 2 to 8
- fetch_ids: int32 [16, 256], P('src', 'grp'), may hold values from 0 to 31, as said below
Outputs:
- source_field: float32 [32768], P('src')
- target_field: float32 [524288], P(('src', 'grp'))
Inputs may be any that keep to these rules, and one draw needn't show every extreme that they name: `tile_slot`: within one source block and group the live slots name distinct entries; every entry 0 to 31 of a device's fetch list is named by some live slot of that device. `fetch_ids`: each device names 8 distinct blocks of each peer in its group; every target block is named by some device of its group.
All inputs are finite; a program needn't handle non-finite values.
Results may differ from a plain program's by a relative error of at most 0.0003.
Values may be sent and summed in bfloat16 or wider, within the bound.
No kernel may reach another device: no remote copies, remote signals or barrier semaphores. Data moves between devices by JAX's collectives and lax.ppermute only.
A program may use at most 64 MiB of HBM per device.

v0:
```python
import functools

import jax
import jax.numpy as jnp
from jax import lax
from jax.experimental import pallas as pl
from jax.experimental.pallas import tpu as pltpu
from jax.sharding import PartitionSpec as P

D = 64
BLOCK = 128
KG = 8
ITERS = 3
EPSILON = 0.25
LOWEST = -1e30
LOG2E = 1.4426950408889634
SCALE = LOG2E / EPSILON
PAIRS = 32
COPIES = 2
GROUP = 32
EXTRA = 16
HEAD = 4


SMEM = pl.BlockSpec(memory_space=pltpu.SMEM)
VMEM = pl.BlockSpec(memory_space=pltpu.VMEM)
PARAMS = pltpu.CompilerParams(vmem_limit_bytes=16 * 1024 * 1024)


def plan_kernel(half_ref, near_ref, far_ref, col_ref, row_ref, lists, sizes):
    halves = near_ref.shape[1] // 2
    slots = 2 * GROUP
    stride = halves + KG
    first = half_ref[0] * halves
    for q in range(slots):
        sizes[q] = 0

    def one_block(b, position):
        start = HEAD + 4 * position

        def place(slot, tile):
            col_ref[start + 4 * (tile // 2) + 1 + tile % 2] = slot

        def append(slot):
            size = sizes[slot]
            lists[slot * stride + size] = b
            sizes[slot] = size + 1

        tiles = jnp.int32(0)
        for group, ref in enumerate((near_ref, far_ref)):
            count = ref[KG, first + b]
            for k in range(2):
                slot = ref[k, first + b] + group * GROUP
                place(slot, tiles + k)
                append(slot)

            def more(k, carry, ref=ref, group=group, tiles=tiles):
                slot = ref[k, first + b] + group * GROUP
                place(slot, tiles + k)
                append(slot)
                return carry

            lax.fori_loop(2, count, more, 0)
            tiles = tiles + count
        place(slots, tiles)
        for k in range(KG):
            col_ref[start + 4 * k] = b
        return position + (tiles + 1) // 2

    def finish(ref, pairs, none):
        ref[0] = (pairs + PAIRS - 1) // PAIRS

        def pad(k, carry):
            at = HEAD + 4 * (pairs + k)
            ref[at] = 0
            ref[at + 1] = none
            ref[at + 2] = none
            return carry

        lax.fori_loop(0, ref[0] * PAIRS - pairs, pad, 0)

    finish(col_ref, lax.fori_loop(0, halves, one_block, jnp.int32(0)), slots)

    def one_slot(q, position):
        size = sizes[q]
        lists[q * stride + size] = halves

        def one_pair(k, carry):
            at = HEAD + 4 * (position + k)
            row_ref[at] = q
            row_ref[at + 1] = lists[q * stride + 2 * k]
            row_ref[at + 2] = lists[q * stride + 2 * k + 1]
            return carry

        lax.fori_loop(0, (size + 1) // 2, one_pair, 0)
        return position + (size + 1) // 2

    finish(row_ref, lax.fori_loop(0, slots, one_slot, jnp.int32(0)), halves)


def plan(half, near, far):
    halves = near.shape[1] // 2
    col_room = HEAD + 4 * (halves * KG + PAIRS + KG)
    row_room = HEAD + 4 * (halves * KG + 2 * GROUP + PAIRS)
    return pl.pallas_call(
        plan_kernel,
        out_shape=[shape((col_room,), jnp.int32), shape((row_room,), jnp.int32)],
        in_specs=[SMEM] * 3,
        out_specs=[SMEM] * 2,
        scratch_shapes=[
            pltpu.SMEM((2 * GROUP * (halves + KG),), jnp.int32),
            pltpu.SMEM((2 * GROUP,), jnp.int32),
        ],
    )(half.reshape(1), near, far)


def split3(values):
    high = values.astype(jnp.bfloat16)
    rest = values - high.astype(jnp.float32)
    middle = rest.astype(jnp.bfloat16)
    low = (rest - middle.astype(jnp.float32)).astype(jnp.bfloat16)
    return high, middle, low


def log_sum(values):
    top = functools.reduce(jnp.maximum, values)
    return top + jnp.log2(sum(jnp.exp2(value - top) for value in values))


def pack_kernel(place_ref, ids_ref, points_ref, potential_ref, logmass_ref, out_ref):
    place = place_ref[0]
    peers = ids_ref.shape[0] // out_ref.shape[0]
    per_peer = out_ref.shape[0] // peers
    for d in range(peers):
        other = lax.rem(place - d + peers, peers)

        def one_block(c, carry, d=d, other=other):
            t = ids_ref[(d * peers + place) * per_peer + c]
            block = points_ref[:, pl.ds(pl.multiple_of(t * BLOCK, BLOCK), BLOCK)]
            wide = block.astype(jnp.float32)
            norm = jnp.sum(wide * wide, axis=0, keepdims=True)
            start = SCALE * (potential_ref[pl.ds(t, 1), :] - 0.5 * norm)
            mass = LOG2E * logmass_ref[pl.ds(t, 1), :]
            rows = [part.astype(jnp.float32) for part in split3(start) + split3(mass)]
            rows.append(jnp.zeros((EXTRA - len(rows), BLOCK), jnp.float32))
            out_ref[other * per_peer + c, :D, :] = block
            out_ref[other * per_peer + c, D:, :] = jnp.concatenate(rows, axis=0).astype(jnp.bfloat16)
            return carry

        lax.fori_loop(0, per_peer, one_block, 0, unroll=4)


def unpack_kernel(near_ref, far_ref, right_ref, left_ref, start_ref, mass_ref):
    for group, in_ref in enumerate((near_ref, far_ref)):

        def one_block(q, carry, group=group, in_ref=in_ref):
            block = in_ref[q, :D, :]
            turned = block.T
            to = group * GROUP + q
            right_ref[to] = jnp.concatenate([block, block], axis=0)
            left_ref[to] = jnp.concatenate([turned, turned], axis=1)
            rows = in_ref[q, D:, :].astype(jnp.float32)
            start_ref[pl.ds(to, 1), :] = rows[0:1] + rows[1:2] + rows[2:3]
            mass_ref[pl.ds(to, 1), :] = rows[3:4] + rows[4:5] + rows[5:6]
            return carry

        lax.fori_loop(0, GROUP, one_block, 0, unroll=4)


def source_kernel(half_ref, points_ref, right_ref, left_ref, norm_ref):
    halves = right_ref.shape[0]
    first = half_ref[0] * halves

    def one_block(b, carry):
        at = pl.multiple_of((first + b) * BLOCK, BLOCK)
        wide = points_ref[:, pl.ds(at, BLOCK)].astype(jnp.float32)
        norm_ref[pl.ds(b, 1), :] = 0.5 * jnp.sum(wide * wide, axis=0, keepdims=True)
        scaled = SCALE * wide
        high = scaled.astype(jnp.bfloat16)
        low = (scaled - high.astype(jnp.float32)).astype(jnp.bfloat16)
        both = jnp.concatenate([high, low], axis=0)
        right_ref[b] = both
        left_ref[b] = both.T
        return carry

    lax.fori_loop(0, halves, one_block, 0, unroll=4)


def start_bias(start_ref):
    return start_ref[...]


def field_bias(near, *rest):
    *far, mass_ref = rest
    return mass_ref[...] - log_sum([near[...]] + [ref[...] for ref in far])


def potential_bias(near, *rest):
    *far, chosen_ref, mass_ref = rest
    refs = [near, *far]
    dot = functools.partial(jnp.dot, preferred_element_type=jnp.float32)
    out = []
    for group in range(2):
        own = slice(group * GROUP, (group + 1) * GROUP)
        chosen = chosen_ref[group]
        sums = jnp.concatenate([ref[own, :] for ref in refs], axis=0)
        parts = sum(dot(chosen, part) for part in split3(sums))
        known = dot(chosen, jnp.ones_like(chosen)) > 0.5
        parts = jnp.where(known, parts, LOWEST)
        merged = log_sum([parts[k * GROUP : (k + 1) * GROUP] for k in range(len(refs))])
        out.append(mass_ref[own, :] - merged)
    return jnp.concatenate(out, axis=0)


def pass_kernel(bias_of, bias_count, *refs):
    list_ref, left_ref, right_ref = refs[:3]
    bias_refs = refs[3 : 3 + bias_count]
    out_ref, bias_ref, columns, peaks, masses = refs[3 + bias_count :]
    lefts, rights = left_ref.shape[0], right_ref.shape[0]
    square = (BLOCK, BLOCK)
    lane = lax.broadcasted_iota(jnp.int32, square, 1)
    eye = jnp.where(lane == lax.broadcasted_iota(jnp.int32, square, 0), 1.0, 0.0).astype(jnp.bfloat16)
    lane = jnp.where(lane < 3 * GROUP, lane % GROUP, -1)
    bias_ref[...] = bias_of(*bias_refs)
    for group in range(lefts // GROUP):
        high, middle, low = split3(bias_ref[group * GROUP : (group + 1) * GROUP, :])
        parts = jnp.concatenate([high, middle, low, jnp.zeros_like(high)], axis=0)
        turned = lax.dot_general(
            eye, parts, (((1,), (1,)), ((), ())), preferred_element_type=jnp.float32
        )

        def fill(k, carry, group=group, turned=turned):
            columns[group * GROUP + k] = jnp.where(lane == k, turned, 0.0).astype(jnp.bfloat16)
            return carry

        lax.fori_loop(0, GROUP, fill, 0, unroll=4)
    peaks[...] = jnp.full_like(peaks, LOWEST)
    masses[...] = jnp.zeros_like(masses)
    ones = jnp.ones((BLOCK, 2 * BLOCK), jnp.bfloat16)

    def fold(copy, r, scores):
        scores = scores.reshape(BLOCK // 8, 8, BLOCK)
        old = peaks[copy, r]
        top = jnp.maximum(old, jnp.max(scores, axis=0))
        mass = jnp.sum(jnp.exp2(scores - top[None]), axis=0)
        masses[copy, r] = masses[copy, r] * jnp.exp2(old - top) + mass
        peaks[copy, r] = top

    def right_block(r):
        return right_ref[jnp.minimum(r, rights - 1)]

    def step(t, carry):
        for u in range(PAIRS):
            at = HEAD + 4 * (t * PAIRS + u)
            l, first, second = list_ref[at], list_ref[at + 1], list_ref[at + 2]
            left = jnp.concatenate([left_ref[l], columns[l]], axis=1)
            right = jnp.concatenate([right_block(first), right_block(second)], axis=1)
            scores = jnp.dot(
                left, jnp.concatenate([right, ones], axis=0), preferred_element_type=jnp.float32
            )
            fold((2 * u) % COPIES, first, scores[:, :BLOCK])
            fold((2 * u + 1) % COPIES, second, scores[:, BLOCK:])
        return carry

    lax.fori_loop(0, list_ref[0], step, 0)

    def finish(octet, carry):
        rows = []
        for k in range(8):
            r = octet * 8 + k
            tops = [peaks[copy, r] for copy in range(COPIES)]
            top = jnp.max(functools.reduce(jnp.maximum, tops), axis=0, keepdims=True)
            mass = sum(masses[copy, r] * jnp.exp2(tops[copy] - top) for copy in range(COPIES))
            rows.append(top + jnp.log2(jnp.sum(mass, axis=0, keepdims=True)))
        out_ref[pl.ds(pl.multiple_of(octet * 8, 8), 8), :] = jnp.concatenate(rows, axis=0)
        return carry

    lax.fori_loop(0, rights // 8, finish, 0)


def shape(dims, dtype=jnp.float32):
    return jax.ShapeDtypeStruct(dims, dtype)


def log_sums(pairs, left, right, bias_of, bias):
    lefts, rights = left.shape[0], right.shape[0]
    return pl.pallas_call(
        functools.partial(pass_kernel, bias_of, len(bias)),
        out_shape=[shape((rights, BLOCK)), shape((lefts, BLOCK))],
        in_specs=[SMEM] + [VMEM] * (2 + len(bias)),
        out_specs=[VMEM, VMEM],
        scratch_shapes=[
            pltpu.VMEM((lefts, BLOCK, BLOCK), jnp.bfloat16),
            pltpu.VMEM((COPIES, rights + 1, 8, BLOCK), jnp.float32),
            pltpu.VMEM((COPIES, rights + 1, 8, BLOCK), jnp.float32),
        ],
        compiler_params=PARAMS,
    )(pairs, left, right, *bias)


def ring(values, axis, size, stride=1):
    places = lax.axis_size(axis)
    out = [values]
    for d in range(1, size):
        pairs = []
        for i in range(places):
            place = i // stride % size
            pairs.append((i, i + ((place + d) % size - place) * stride))
        out.append(lax.ppermute(values, axis, pairs))
    return out


def shards(
    source_points,
    source_logmass,
    target_points,
    target_logmass,
    target_potential,
    tile_slot,
    tile_counts,
    fetch_ids,
):
    peers = lax.axis_size("src")
    blocks = tile_counts.shape[0]
    halves = blocks // 2
    per_peer = fetch_ids.shape[1]
    owned = target_potential.shape[0] // BLOCK
    count = peers * per_peer
    place = lax.axis_index("src")
    half = lax.axis_index("grp") % 2

    def swap(values):
        return ring(values, "grp", 2, 1)[1]

    tiles = jnp.concatenate([tile_slot.T, tile_counts.T], axis=0)
    ids = jnp.stack(ring(fetch_ids, "src", peers))
    col_pairs, row_pairs = plan(half, tiles, swap(tiles))
    ids, col_pairs, row_pairs = lax.optimization_barrier((ids, col_pairs, row_pairs))
    packed = pl.pallas_call(
        pack_kernel,
        out_shape=shape((count, D + EXTRA, BLOCK), jnp.bfloat16),
        in_specs=[SMEM, SMEM, VMEM, VMEM, VMEM],
        out_specs=VMEM,
        compiler_params=PARAMS,
    )(
        place.reshape(1),
        ids.reshape(-1),
        target_points.T,
        target_potential.reshape(owned, BLOCK),
        target_logmass.reshape(owned, BLOCK),
    )
    fetched = lax.all_to_all(packed, "src", split_axis=0, concat_axis=0, tiled=True)
    points_right, points_left, source_half = pl.pallas_call(
        source_kernel,
        out_shape=[
            shape((halves, 2 * D, BLOCK), jnp.bfloat16),
            shape((halves, BLOCK, 2 * D), jnp.bfloat16),
            shape((halves, BLOCK)),
        ],
        in_specs=[SMEM, VMEM],
        out_specs=[VMEM] * 3,
        compiler_params=PARAMS,
    )(half.reshape(1), source_points.T)
    targets_right, targets_left, potentials, slot_mass = pl.pallas_call(
        unpack_kernel,
        out_shape=[
            shape((2 * count, 2 * D, BLOCK), jnp.bfloat16),
            shape((2 * count, BLOCK, 2 * D), jnp.bfloat16),
            shape((2 * count, BLOCK)),
            shape((2 * count, BLOCK)),
        ],
        in_specs=[VMEM] * 2,
        out_specs=[VMEM] * 4,
        compiler_params=PARAMS,
    )(fetched, swap(fetched))
    source_mass = LOG2E * lax.dynamic_slice(
        source_logmass.reshape(blocks, BLOCK), (half * halves, 0), (halves, BLOCK)
    )

    all_ids = jnp.stack([ids, swap(ids)])
    same = all_ids[:, :, :, None, :] == all_ids[:, :1, :, :, None]
    same = same[:, :, :, :, None, :] & jnp.eye(peers, dtype=bool)[:, None, :, None]
    same = same.reshape(2, peers, count, 1, count) & jnp.eye(peers, dtype=bool)[:, None, :, None]
    chosen = same.reshape(2, peers * count, peers * count).astype(jnp.bfloat16)

    for sweep_index in range(ITERS):
        if sweep_index == 0:
            rows, _ = log_sums(row_pairs, targets_left, points_right, start_bias, [potentials])
        else:
            rows, _ = log_sums(
                row_pairs, targets_left, points_right, potential_bias, [*col_parts, chosen, slot_mass]
            )
        rows = log_sum(ring(rows, "grp", 4, 2))
        row_parts = ring(rows, "grp", 4, 8)
        cols, field = log_sums(col_pairs, points_left, targets_right, field_bias, [*row_parts, source_mass])
        if sweep_index < ITERS - 1:
            other = swap(cols)
            cols = log_sum([cols, jnp.concatenate([other[count:], other[:count]], axis=0)])
            col_parts = ring(cols, "src", peers)
    field = field * (1.0 / SCALE) + source_half
    other = swap(field)
    low = half == 0
    source_field = jnp.concatenate([jnp.where(low, field, other), jnp.where(low, other, field)], axis=0)

    cols = log_sum([cols[:count], swap(cols[count:])]).reshape(peers, per_peer, BLOCK)
    back, requested = [], []
    for d in range(peers):
        wanted = lax.dynamic_slice(cols, ((place + d) % peers, 0, 0), (1, per_peer, BLOCK))[0]
        pairs = [(i, (i + d) % peers) for i in range(peers)]
        back.append(wanted if d == 0 else lax.ppermute(wanted, "src", pairs))
        requested.append(lax.dynamic_slice(ids, (d, place, 0), (1, 1, per_peer))[0, 0])
    blocks_here = jnp.arange(owned, dtype=jnp.int32)[:, None]
    parts = [
        jnp.max(jnp.where((blocks_here == wants[None])[..., None], sums[None], LOWEST), axis=1)
        for wants, sums in zip(requested, back)
    ]
    owned_pot = LOG2E * target_logmass.reshape(owned, BLOCK) - log_sum(parts)
    target_half = 0.5 * jnp.sum(jnp.square(target_points.astype(jnp.float32)), -1)
    target_field = owned_pot.reshape(-1) * (1.0 / SCALE) + target_half
    return (source_field.reshape(-1), target_field)


def solution(mesh):
    return jax.shard_map(
        shards,
        mesh=mesh,
        in_specs=(
            P("src", None),
            P("src"),
            P(("src", "grp"), None),
            P(("src", "grp")),
            P(("src", "grp")),
            P("src", "grp"),
            P("src", "grp"),
            P("src", "grp"),
        ),
        out_specs=(P("src"), P(("src", "grp"))),
        check_vma=False,
    )
```

profile of v0, /device:TPU:0, one launch (start us, length us, event | category | flops | bytes accessed | tf_op | source)
XLA Modules:
  0.0 155.4 jit_solution(7207278810483943934)
XLA Ops:
  0.6 1.6 %collective-permute-start = (s32[4,8]{1,0:T(4,128)}, s32[4,8]{1,0:T(4,128)S(1)}, u32[]{:S(2)}, u32[]{:S(2)}) collective-permute-start(s32[4,8]{1,0:T(4,128)} %param.15), channel_id=1, source_target_pairs={{0,32},{32,64},{64,96},{96,0},{1,33},{33,65},{65,97},{97,1},{2,34}... | collective-permute-start | bytes 392 | tf_op jit(solution)/shard_map/ppermute | solution.py:309
  2.3 2.7 %collective-permute-start.1 = (s32[4,8]{1,0:T(4,128)}, s32[4,8]{1,0:T(4,128)S(1)}, u32[]{:S(2)}, u32[]{:S(2)}) collective-permute-start(s32[4,8]{1,0:T(4,128)} %param.15), channel_id=1, source_target_pairs={{0,64},{32,96},{64,0},{96,32},{1,65},{33,97},{65,1},{97,33},{2,66}... | collective-permute-start | bytes 392 | tf_op jit(solution)/shard_map/ppermute | solution.py:309
  5.0 1.4 collective-permute-start.2
  7.6 1.2 collective-permute-done.2
  10.1 7.6 %shard_map.95 = (s32[1188]{0:T(1024)}, s32[1412]{0:T(1024)}) custom-call(s32[1]{0:T(128)} %bitcast.4.half_ref, s32[9,64]{1,0:T(8,128)} %copy-done.17, s32[9,64]{1,0:T(8,128)} %copy-done.19), custom_call_target="tpu_custom_call" | custom-call | tf_op jit(solution)/shard_map/pallas_call | solution.py:105
  17.8 1.0 copy-done.9
  20.3 1.0 shard_map.97
  21.3 12.8 %all_to_all.5.near_ref = bf16[32,80,128]{2,1,0:T(8,128)(2,1)S(1)} all-to-all(bf16[32,80,128]{2,1,0:T(8,128)(2,1)S(1)} %shard_map.97), channel_id=1, replica_groups=mesh['src'=4,'grp'=32] {'src'}, dimensions={0} | all-to-all | bytes 1310720 | tf_op jit(solution)/shard_map/all_to_all | solution.py:352
  35.3 1.0 copy-done.3
  36.8 1.1 copy-done.8
  37.9 3.8 %shard_map.98 = (bf16[64,128,128]{2,1,0:T(8,128)(2,1)S(1)}, bf16[64,128,128]{2,1,0:T(8,128)(2,1)S(1)}, f32[64,128]{1,0:T(8,128)S(1)}, f32[64,128]{1,0:T(8,128)S(1)}) custom-call(bf16[32,80,128]{2,1,0:T(8,128)(2,1)S(1)} %copy-done.8, bf16[32,80,128]{2,1,0:T(8,128)(2,1)} %collective-permute-done.4.far_ref), custom_call_target="tpu_custom_call" | custom-call | tf_op jit(solution)/shard_map/pallas_call | solution.py:364
  41.7 1.2 copy-done.4
  42.9 5.9 %shard_map.99 = (f32[32,128]{1,0:T(8,128)S(1)}, f32[64,128]{1,0:T(8,128)}) custom-call(s32[1412]{0:T(1024)S(1)} %copy-done.13, bf16[64,128,128]{2,1,0:T(8,128)(2,1)S(1)} %get-tuple-element.28.refs_1_, bf16[32,128,128]{2,1,0:T(8,128)(2,1)S(1)} %copy-done.4, f32[64,128]{1,0:T(8,128)S(1)} %get-tuple-element.30.refs_3_), custom_call_target="tpu_custom_call" | custom-call | tf_op jit(solution)/shard_map/pallas_call | solution.py:287
  48.8 1.3 copy-done
  50.1 1.2 collective-permute-start.6
  51.3 2.0 %collective-permute-start.7 = (f32[32,128]{1,0:T(8,128)S(1)}, f32[32,128]{1,0:T(8,128)S(1)}, u32[]{:S(2)}, u32[]{:S(2)}) collective-permute-start(f32[32,128]{1,0:T(8,128)S(1)} %get-tuple-element.31), channel_id=1, source_target_pairs={{0,6},{1,7},{2,0},{3,1},{4,2},{5,3},{6,4},{7,5},{8,14},{9,15},{10,... | collective-permute-start | bytes 49160 | tf_op jit(solution)/shard_map/ppermute | solution.py:309
  53.4 1.7 %collective-permute-done.5 = f32[32,128]{1,0:T(8,128)S(1)} collective-permute-done((f32[32,128]{1,0:T(8,128)S(1)}, f32[32,128]{1,0:T(8,128)S(1)}, u32[]{:S(2)}, u32[]{:S(2)}) %collective-permute-start.5) | collective-permute-done | bytes 16416 | tf_op jit(solution)/shard_map/ppermute | solution.py:309
  56.1 2.8 %collective-permute-start.10 = (f32[32,128]{1,0:T(8,128)S(1)}, f32[32,128]{1,0:T(8,128)S(1)}, u32[]{:S(2)}, u32[]{:S(2)}) collective-permute-start(f32[32,128]{1,0:T(8,128)S(1)} %multiply_add_fusion.5.refs_3_), channel_id=1, source_target_pairs={{0,24},{1,25},{2,26},{3,27},{4,28},{5,29},{6,30},{7,31},{8,0},{9,1... | collective-permute-start | bytes 49160 | tf_op jit(solution)/shard_map/ppermute | solution.py:309
  58.9 2.1 %collective-permute-start.8 = (f32[32,128]{1,0:T(8,128)S(1)}, f32[32,128]{1,0:T(8,128)S(1)}, u32[]{:S(2)}, u32[]{:S(2)}) collective-permute-start(f32[32,128]{1,0:T(8,128)S(1)} %multiply_add_fusion.5.refs_3_), channel_id=1, source_target_pairs={{0,8},{1,9},{2,10},{3,11},{4,12},{5,13},{6,14},{7,15},{8,16},{9,17... | collective-permute-start | bytes 49160 | tf_op jit(solution)/shard_map/ppermute | solution.py:309
  61.0 2.0 %collective-permute-start.9 = (f32[32,128]{1,0:T(8,128)S(1)}, f32[32,128]{1,0:T(8,128)S(1)}, u32[]{:S(2)}, u32[]{:S(2)}) collective-permute-start(f32[32,128]{1,0:T(8,128)S(1)} %multiply_add_fusion.5.refs_3_), channel_id=1, source_target_pairs={{0,16},{1,17},{2,18},{3,19},{4,20},{5,21},{6,22},{7,23},{8,24},{9,... | collective-permute-start | bytes 49160 | tf_op jit(solution)/shard_map/ppermute | solution.py:309
  63.9 2.4 %collective-permute-done.9.refs_5_ = f32[32,128]{1,0:T(8,128)S(1)} collective-permute-done((f32[32,128]{1,0:T(8,128)S(1)}, f32[32,128]{1,0:T(8,128)S(1)}, u32[]{:S(2)}, u32[]{:S(2)}) %collective-permute-start.9) | collective-permute-done | bytes 16416 | tf_op jit(solution)/shard_map/ppermute | solution.py:309
  66.2 6.6 %shard_map.100 = (f32[64,128]{1,0:T(8,128)S(1)}, f32[32,128]{1,0:T(8,128)}) custom-call(s32[1188]{0:T(1024)S(1)} %copy-done.12, bf16[32,128,128]{2,1,0:T(8,128)(2,1)S(1)} %get-tuple-element.24.refs_1_, bf16[64,128,128]{2,1,0:T(8,128)(2,1)S(1)} %get-tuple-element.26.refs_2_, f32[32,128]{1,0:T(8,128)S(1)} %multiply_add_fusion.5.refs_3_, ...), custom_call_target="tpu_custom_call" | custom-call | tf_op jit(solution)/shard_map/pallas_call | solution.py:287
  74.5 2.9 %collective-permute-start.14 = (f32[64,128]{1,0:T(8,128)S(1)}, f32[64,128]{1,0:T(8,128)S(1)}, u32[]{:S(2)}, u32[]{:S(2)}) collective-permute-start(f32[64,128]{1,0:T(8,128)S(1)} %multiply_add_fusion.1.refs_3_), channel_id=1, source_target_pairs={{0,96},{32,0},{64,32},{96,64},{1,97},{33,1},{65,33},{97,65},{2,98}... | collective-permute-start | bytes 98312 | tf_op jit(solution)/shard_map/ppermute | solution.py:309
  77.4 1.9 %collective-permute-done.12.refs_4_ = f32[64,128]{1,0:T(8,128)S(1)} collective-permute-done((f32[64,128]{1,0:T(8,128)S(1)}, f32[64,128]{1,0:T(8,128)S(1)}, u32[]{:S(2)}, u32[]{:S(2)}) %collective-permute-start.12) | collective-permute-done | bytes 32800 | tf_op jit(solution)/shard_map/ppermute | solution.py:309
  80.5 1.6 %copy-done.1 = bf16[64,128,128]{2,1,0:T(8,128)(2,1)S(1)} copy-done((bf16[64,128,128]{2,1,0:T(8,128)(2,1)S(1)}, bf16[64,128,128]{2,1,0:T(8,128)(2,1)}, u32[]{:S(2)}) %copy-start.1) | copy-done | bytes 2097176
  82.1 1.2 copy-done.5
  83.3 6.1 %shard_map.101 = (f32[32,128]{1,0:T(8,128)S(1)}, f32[64,128]{1,0:T(8,128)}) custom-call(s32[1412]{0:T(1024)S(1)} %copy-done.13, bf16[64,128,128]{2,1,0:T(8,128)(2,1)S(1)} %copy-done.1, bf16[32,128,128]{2,1,0:T(8,128)(2,1)S(1)} %copy-done.5, f32[64,128]{1,0:T(8,128)S(1)} %multiply_add_fusion.1.refs_3_, f32[64,128]{1,0:T(8,128)S(1)} %collective-permute-done.12.refs_4_, ...), custom_call_target="tpu_custom_call" | custom-call | tf_op jit(solution)/shard_map/pallas_call | solution.py:287
  89.4 1.0 collective-permute-start.17
  90.4 2.3 %collective-permute-start.18 = (f32[32,128]{1,0:T(8,128)S(1)}, f32[32,128]{1,0:T(8,128)S(1)}, u32[]{:S(2)}, u32[]{:S(2)}) collective-permute-start(f32[32,128]{1,0:T(8,128)S(1)} %get-tuple-element.34), channel_id=1, source_target_pairs={{0,6},{1,7},{2,0},{3,1},{4,2},{5,3},{6,4},{7,5},{8,14},{9,15},{10,... | collective-permute-start | bytes 49160 | tf_op jit(solution)/shard_map/ppermute | solution.py:309
  92.7 1.7 %collective-permute-done.16 = f32[32,128]{1,0:T(8,128)S(1)} collective-permute-done((f32[32,128]{1,0:T(8,128)S(1)}, f32[32,128]{1,0:T(8,128)S(1)}, u32[]{:S(2)}, u32[]{:S(2)}) %collective-permute-start.16) | collective-permute-done | bytes 16416 | tf_op jit(solution)/shard_map/ppermute | solution.py:309
  95.5 3.4 %collective-permute-start.19 = (f32[32,128]{1,0:T(8,128)S(1)}, f32[32,128]{1,0:T(8,128)S(1)}, u32[]{:S(2)}, u32[]{:S(2)}) collective-permute-start(f32[32,128]{1,0:T(8,128)S(1)} %multiply_add_fusion.4.refs_3_), channel_id=1, source_target_pairs={{0,8},{1,9},{2,10},{3,11},{4,12},{5,13},{6,14},{7,15},{8,16},{9,17... | collective-permute-start | bytes 49160 | tf_op jit(solution)/shard_map/ppermute | solution.py:309
  98.9 2.8 %collective-permute-start.21 = (f32[32,128]{1,0:T(8,128)S(1)}, f32[32,128]{1,0:T(8,128)S(1)}, u32[]{:S(2)}, u32[]{:S(2)}) collective-permute-start(f32[32,128]{1,0:T(8,128)S(1)} %multiply_add_fusion.4.refs_3_), channel_id=1, source_target_pairs={{0,24},{1,25},{2,26},{3,27},{4,28},{5,29},{6,30},{7,31},{8,0},{9,1... | collective-permute-start | bytes 49160 | tf_op jit(solution)/shard_map/ppermute | solution.py:309
  101.6 2.5 %collective-permute-done.20.refs_5_ = f32[32,128]{1,0:T(8,128)S(1)} collective-permute-done((f32[32,128]{1,0:T(8,128)S(1)}, f32[32,128]{1,0:T(8,128)S(1)}, u32[]{:S(2)}, u32[]{:S(2)}) %collective-permute-start.20) | collective-permute-done | bytes 16416 | tf_op jit(solution)/shard_map/ppermute | solution.py:309
  104.1 6.6 %shard_map.102 = (f32[64,128]{1,0:T(8,128)S(1)}, f32[32,128]{1,0:T(8,128)}) custom-call(s32[1188]{0:T(1024)S(1)} %copy-done.12, bf16[32,128,128]{2,1,0:T(8,128)(2,1)S(1)} %get-tuple-element.24.refs_1_, bf16[64,128,128]{2,1,0:T(8,128)(2,1)S(1)} %get-tuple-element.26.refs_2_, f32[32,128]{1,0:T(8,128)S(1)} %multiply_add_fusion.4.refs_3_, ...), custom_call_target="tpu_custom_call" | custom-call | tf_op jit(solution)/shard_map/pallas_call | solution.py:287
  110.9 1.0 collective-permute-done.22
  112.5 2.8 %collective-permute-start.25 = (f32[64,128]{1,0:T(8,128)S(1)}, f32[64,128]{1,0:T(8,128)S(1)}, u32[]{:S(2)}, u32[]{:S(2)}) collective-permute-start(f32[64,128]{1,0:T(8,128)S(1)} %multiply_add_fusion.refs_3_), channel_id=1, source_target_pairs={{0,96},{32,0},{64,32},{96,64},{1,97},{33,1},{65,33},{97,65},{2,98}... | collective-permute-start | bytes 98312 | tf_op jit(solution)/shard_map/ppermute | solution.py:309
  115.3 1.9 %collective-permute-done.23.refs_4_ = f32[64,128]{1,0:T(8,128)S(1)} collective-permute-done((f32[64,128]{1,0:T(8,128)S(1)}, f32[64,128]{1,0:T(8,128)S(1)}, u32[]{:S(2)}, u32[]{:S(2)}) %collective-permute-start.23) | collective-permute-done | bytes 32800 | tf_op jit(solution)/shard_map/ppermute | solution.py:309
  118.4 1.6 %copy-done.2 = bf16[64,128,128]{2,1,0:T(8,128)(2,1)S(1)} copy-done((bf16[64,128,128]{2,1,0:T(8,128)(2,1)S(1)}, bf16[64,128,128]{2,1,0:T(8,128)(2,1)}, u32[]{:S(2)}) %copy-start.2) | copy-done | bytes 2097176
  120.0 1.2 copy-done.6
  121.2 6.1 %shard_map.103 = (f32[32,128]{1,0:T(8,128)S(1)}, f32[64,128]{1,0:T(8,128)}) custom-call(s32[1412]{0:T(1024)S(1)} %copy-done.13, bf16[64,128,128]{2,1,0:T(8,128)(2,1)S(1)} %copy-done.2, bf16[32,128,128]{2,1,0:T(8,128)(2,1)S(1)} %copy-done.6, f32[64,128]{1,0:T(8,128)S(1)} %multiply_add_fusion.refs_3_, f32[64,128]{1,0:T(8,128)S(1)} %collective-permute-done.23.refs_4_, ...), custom_call_target="tpu_custom_call" | custom-call | tf_op jit(solution)/shard_map/pallas_call | solution.py:287
  127.3 1.0 collective-permute-start.27
  128.4 2.2 %collective-permute-start.28 = (f32[32,128]{1,0:T(8,128)S(1)}, f32[32,128]{1,0:T(8,128)S(1)}, u32[]{:S(2)}, u32[]{:S(2)}) collective-permute-start(f32[32,128]{1,0:T(8,128)S(1)} %get-tuple-element.36), channel_id=1, source_target_pairs={{0,6},{1,7},{2,0},{3,1},{4,2},{5,3},{6,4},{7,5},{8,14},{9,15},{10,... | collective-permute-start | bytes 49160 | tf_op jit(solution)/shard_map/ppermute | solution.py:309
  130.6 1.7 %collective-permute-done.26 = f32[32,128]{1,0:T(8,128)S(1)} collective-permute-done((f32[32,128]{1,0:T(8,128)S(1)}, f32[32,128]{1,0:T(8,128)S(1)}, u32[]{:S(2)}, u32[]{:S(2)}) %collective-permute-start.26) | collective-permute-done | bytes 16416 | tf_op jit(solution)/shard_map/ppermute | solution.py:309
  133.3 2.9 %collective-permute-start.29 = (f32[32,128]{1,0:T(8,128)S(1)}, f32[32,128]{1,0:T(8,128)S(1)}, u32[]{:S(2)}, u32[]{:S(2)}) collective-permute-start(f32[32,128]{1,0:T(8,128)S(1)} %multiply_add_fusion.3.refs_3_), channel_id=1, source_target_pairs={{0,8},{1,9},{2,10},{3,11},{4,12},{5,13},{6,14},{7,15},{8,16},{9,17... | collective-permute-start | bytes 49160 | tf_op jit(solution)/shard_map/ppermute | solution.py:309
  137.2 1.9 %collective-permute-start.31 = (f32[32,128]{1,0:T(8,128)S(1)}, f32[32,128]{1,0:T(8,128)S(1)}, u32[]{:S(2)}, u32[]{:S(2)}) collective-permute-start(f32[32,128]{1,0:T(8,128)S(1)} %multiply_add_fusion.3.refs_3_), channel_id=1, source_target_pairs={{0,24},{1,25},{2,26},{3,27},{4,28},{5,29},{6,30},{7,31},{8,0},{9,1... | collective-permute-start | bytes 49160 | tf_op jit(solution)/shard_map/ppermute | solution.py:309
  139.0 2.5 %collective-permute-done.30.refs_5_ = f32[32,128]{1,0:T(8,128)S(1)} collective-permute-done((f32[32,128]{1,0:T(8,128)S(1)}, f32[32,128]{1,0:T(8,128)S(1)}, u32[]{:S(2)}, u32[]{:S(2)}) %collective-permute-start.30) | collective-permute-done | bytes 16416 | tf_op jit(solution)/shard_map/ppermute | solution.py:309
  141.5 6.0 %shard_map.104 = (f32[64,128]{1,0:T(8,128)S(1)}, f32[32,128]{1,0:T(8,128)S(1)}) custom-call(s32[1188]{0:T(1024)S(1)} %copy-done.12, bf16[32,128,128]{2,1,0:T(8,128)(2,1)S(1)} %get-tuple-element.24.refs_1_, bf16[64,128,128]{2,1,0:T(8,128)(2,1)S(1)} %get-tuple-element.26.refs_2_, f32[32,128]{1,0:T(8,128)S(1)} %multiply_add_fusion.3.refs_3_, ...), custom_call_target="tpu_custom_call" | custom-call | tf_op jit(solution)/shard_map/pallas_call | solution.py:287
  149.0 3.1 %collective-permute-start.36 = (f32[8,128]{1,0:T(8,128)S(1)}, f32[8,128]{1,0:T(8,128)S(1)}, u32[]{:S(2)}, u32[]{:S(2)}) collective-permute-start(f32[8,128]{1,0:T(8,128)S(1)} %get-tuple-element.47), channel_id=1, source_target_pairs={{0,96},{32,0},{64,32},{96,64},{1,97},{33,1},{65,33},{97,65},{2,98}... | collective-permute-start | bytes 12296 | tf_op jit(solution)/shard_map/ppermute | solution.py:410
  (117 shorter events, 20.1 us)
Async XLA Ops:
  0.6 33.4 %copy-start.18 = (f32[8192]{0:T(1024)S(1)}, f32[8192]{0:T(1024)}, u32[]{:S(2)}) copy-start(f32[8192]{0:T(1024)} %param.9) | copy-start | bytes 98308
  0.6 6.5 %collective-permute-start = (s32[4,8]{1,0:T(4,128)}, s32[4,8]{1,0:T(4,128)S(1)}, u32[]{:S(2)}, u32[]{:S(2)}) collective-permute-start(s32[4,8]{1,0:T(4,128)} %param.15), channel_id=1, source_target_pairs={{0,32},{32,64},{64,96},{96,0},{1,33},{33,65},{65,97},{97,1},{2,34}... | collective-permute-start | bytes 392 | tf_op jit(solution)/shard_map/ppermute | solution.py:309
  2.3 5.3 %collective-permute-start.1 = (s32[4,8]{1,0:T(4,128)}, s32[4,8]{1,0:T(4,128)S(1)}, u32[]{:S(2)}, u32[]{:S(2)}) collective-permute-start(s32[4,8]{1,0:T(4,128)} %param.15), channel_id=1, source_target_pairs={{0,64},{32,96},{64,0},{96,32},{1,65},{33,97},{65,1},{97,33},{2,66}... | collective-permute-start | bytes 392 | tf_op jit(solution)/shard_map/ppermute | solution.py:309
  5.0 3.8 %collective-permute-start.2 = (s32[4,8]{1,0:T(4,128)}, s32[4,8]{1,0:T(4,128)S(1)}, u32[]{:S(2)}, u32[]{:S(2)}) collective-permute-start(s32[4,8]{1,0:T(4,128)} %param.15), channel_id=1, source_target_pairs={{0,96},{32,0},{64,32},{96,64},{1,97},{33,1},{65,33},{97,65},{2,98}... | collective-permute-start | bytes 392 | tf_op jit(solution)/shard_map/ppermute | solution.py:309
  7.2 2.3 %copy-start.17 = (s32[9,64]{1,0:T(8,128)}, s32[9,64]{1,0:T(8,128)S(1)}, u32[]{:S(2)}) copy-start(s32[9,64]{1,0:T(8,128)S(1)} %pad_add_fusion.2.near_ref) | copy-start | bytes 6916
  7.2 2.3 %collective-permute-start.3 = (s32[9,64]{1,0:T(8,128)S(1)}, s32[9,64]{1,0:T(8,128)S(1)}, u32[]{:S(2)}, u32[]{:S(2)}) collective-permute-start(s32[9,64]{1,0:T(8,128)S(1)} %pad_add_fusion.2.near_ref), channel_id=1, source_target_pairs={{0,1},{1,0},{2,3},{3,2},{4,5},{5,4},{6,7},{7,6},{8,9},{9,8},{10,11... | collective-permute-start | bytes 6920 | tf_op jit(solution)/shard_map/ppermute | solution.py:309
  20.3 14.3 %copy-start.11 = (bf16[8192,64]{0,1:T(8,128)(2,1)S(1)}, bf16[8192,64]{0,1:T(8,128)(2,1)}, u32[]{:S(2)}) copy-start(bf16[8192,64]{0,1:T(8,128)(2,1)} %param.8) | copy-start | bytes 3145732
  21.3 20.4 %copy-start.13 = (s32[1412]{0:T(1024)S(1)}, s32[1412]{0:T(1024)}, u32[]{:S(2)}) copy-start(s32[1412]{0:T(1024)} %get-tuple-element.27.refs_0_) | copy-start | bytes 16948
  34.1 2.7 %copy-start.7 = (bf16[32,80,128]{2,1,0:T(8,128)(2,1)}, bf16[32,80,128]{2,1,0:T(8,128)(2,1)S(1)}, u32[]{:S(2)}) copy-start(bf16[32,80,128]{2,1,0:T(8,128)(2,1)S(1)} %all_to_all.5.near_ref) | copy-start | bytes 1966084
  34.1 2.7 %collective-permute-start.4 = (bf16[32,80,128]{2,1,0:T(8,128)(2,1)S(1)}, bf16[32,80,128]{2,1,0:T(8,128)(2,1)}, u32[]{:S(2)}, u32[]{:S(2)}) collective-permute-start(bf16[32,80,128]{2,1,0:T(8,128)(2,1)S(1)} %all_to_all.5.near_ref), channel_id=1, source_target_pairs={{0,1},{1,0},{2,3},{3,2},{4,5},{5,4},{6,7},{7,6},{8,9},{9,8},{10,11... | collective-permute-start | bytes 1966088 | tf_op jit(solution)/shard_map/ppermute | solution.py:309
  34.1 2.7 %collective-permute-start.15 = (s32[4,4,8]{2,1,0:T(4,128)S(1)}, s32[4,4,8]{2,1,0:T(4,128)S(1)}, u32[]{:S(2)}, u32[]{:S(2)}) collective-permute-start(s32[4,4,8]{2,1,0:T(4,128)S(1)} %pad_add_fusion.1), channel_id=1, source_target_pairs={{0,1},{1,0},{2,3},{3,2},{4,5},{5,4},{6,7},{7,6},{8,9},{9,8},{10,11... | collective-permute-start | bytes 1544 | tf_op jit(solution)/shard_map/ppermute | solution.py:309
  37.9 28.3 %copy-start.12 = (s32[1188]{0:T(1024)S(1)}, s32[1188]{0:T(1024)}, u32[]{:S(2)}) copy-start(s32[1188]{0:T(1024)} %get-tuple-element.23.refs_0_) | copy-start | bytes 14260
  48.8 1.3 copy-start
  50.1 4.9 %collective-permute-start.5 = (f32[32,128]{1,0:T(8,128)S(1)}, f32[32,128]{1,0:T(8,128)S(1)}, u32[]{:S(2)}, u32[]{:S(2)}) collective-permute-start(f32[32,128]{1,0:T(8,128)S(1)} %get-tuple-element.31), channel_id=1, source_target_pairs={{0,2},{1,3},{2,4},{3,5},{4,6},{5,7},{6,0},{7,1},{8,10},{9,11},{10,... | collective-permute-start | bytes 49160 | tf_op jit(solution)/shard_map/ppermute | solution.py:309
  50.1 5.2 %collective-permute-start.6 = (f32[32,128]{1,0:T(8,128)S(1)}, f32[32,128]{1,0:T(8,128)S(1)}, u32[]{:S(2)}, u32[]{:S(2)}) collective-permute-start(f32[32,128]{1,0:T(8,128)S(1)} %get-tuple-element.31), channel_id=1, source_target_pairs={{0,4},{1,5},{2,6},{3,7},{4,0},{5,1},{6,2},{7,3},{8,12},{9,13},{10,... | collective-permute-start | bytes 49160 | tf_op jit(solution)/shard_map/ppermute | solution.py:309
  51.3 4.8 %collective-permute-start.7 = (f32[32,128]{1,0:T(8,128)S(1)}, f32[32,128]{1,0:T(8,128)S(1)}, u32[]{:S(2)}, u32[]{:S(2)}) collective-permute-start(f32[32,128]{1,0:T(8,128)S(1)} %get-tuple-element.31), channel_id=1, source_target_pairs={{0,6},{1,7},{2,0},{3,1},{4,2},{5,3},{6,4},{7,5},{8,14},{9,15},{10,... | collective-permute-start | bytes 49160 | tf_op jit(solution)/shard_map/ppermute | solution.py:309
  56.1 7.3 %collective-permute-start.10 = (f32[32,128]{1,0:T(8,128)S(1)}, f32[32,128]{1,0:T(8,128)S(1)}, u32[]{:S(2)}, u32[]{:S(2)}) collective-permute-start(f32[32,128]{1,0:T(8,128)S(1)} %multiply_add_fusion.5.refs_3_), channel_id=1, source_target_pairs={{0,24},{1,25},{2,26},{3,27},{4,28},{5,29},{6,30},{7,31},{8,0},{9,1... | collective-permute-start | bytes 49160 | tf_op jit(solution)/shard_map/ppermute | solution.py:309
  58.9 4.9 %collective-permute-start.8 = (f32[32,128]{1,0:T(8,128)S(1)}, f32[32,128]{1,0:T(8,128)S(1)}, u32[]{:S(2)}, u32[]{:S(2)}) collective-permute-start(f32[32,128]{1,0:T(8,128)S(1)} %multiply_add_fusion.5.refs_3_), channel_id=1, source_target_pairs={{0,8},{1,9},{2,10},{3,11},{4,12},{5,13},{6,14},{7,15},{8,16},{9,17... | collective-permute-start | bytes 49160 | tf_op jit(solution)/shard_map/ppermute | solution.py:309
  61.0 5.2 %collective-permute-start.9 = (f32[32,128]{1,0:T(8,128)S(1)}, f32[32,128]{1,0:T(8,128)S(1)}, u32[]{:S(2)}, u32[]{:S(2)}) collective-permute-start(f32[32,128]{1,0:T(8,128)S(1)} %multiply_add_fusion.5.refs_3_), channel_id=1, source_target_pairs={{0,16},{1,17},{2,18},{3,19},{4,20},{5,21},{6,22},{7,23},{8,24},{9,... | collective-permute-start | bytes 49160 | tf_op jit(solution)/shard_map/ppermute | solution.py:309
  72.8 1.2 collective-permute-start.11
  74.1 5.2 %collective-permute-start.12 = (f32[64,128]{1,0:T(8,128)S(1)}, f32[64,128]{1,0:T(8,128)S(1)}, u32[]{:S(2)}, u32[]{:S(2)}) collective-permute-start(f32[64,128]{1,0:T(8,128)S(1)} %multiply_add_fusion.1.refs_3_), channel_id=1, source_target_pairs={{0,32},{32,64},{64,96},{96,0},{1,33},{33,65},{65,97},{97,1},{2,34}... | collective-permute-start | bytes 98312 | tf_op jit(solution)/shard_map/ppermute | solution.py:309
  74.2 5.5 %collective-permute-start.13 = (f32[64,128]{1,0:T(8,128)S(1)}, f32[64,128]{1,0:T(8,128)S(1)}, u32[]{:S(2)}, u32[]{:S(2)}) collective-permute-start(f32[64,128]{1,0:T(8,128)S(1)} %multiply_add_fusion.1.refs_3_), channel_id=1, source_target_pairs={{0,64},{32,96},{64,0},{96,32},{1,65},{33,97},{65,1},{97,33},{2,66}... | collective-permute-start | bytes 98312 | tf_op jit(solution)/shard_map/ppermute | solution.py:309
  74.5 6.0 %collective-permute-start.14 = (f32[64,128]{1,0:T(8,128)S(1)}, f32[64,128]{1,0:T(8,128)S(1)}, u32[]{:S(2)}, u32[]{:S(2)}) collective-permute-start(f32[64,128]{1,0:T(8,128)S(1)} %multiply_add_fusion.1.refs_3_), channel_id=1, source_target_pairs={{0,96},{32,0},{64,32},{96,64},{1,97},{33,1},{65,33},{97,65},{2,98}... | collective-permute-start | bytes 98312 | tf_op jit(solution)/shard_map/ppermute | solution.py:309
  80.5 1.6 %copy-start.1 = (bf16[64,128,128]{2,1,0:T(8,128)(2,1)S(1)}, bf16[64,128,128]{2,1,0:T(8,128)(2,1)}, u32[]{:S(2)}) copy-start(bf16[64,128,128]{2,1,0:T(8,128)(2,1)} %copy-done) | copy-start | bytes 6291460
  89.4 21.3 %copy-start.10 = (bf16[4096,64]{0,1:T(8,128)(2,1)S(1)}, bf16[4096,64]{0,1:T(8,128)(2,1)}, u32[]{:S(2)}) copy-start(bf16[4096,64]{0,1:T(8,128)(2,1)} %param.10) | copy-start | bytes 1572868
  89.4 4.9 %collective-permute-start.16 = (f32[32,128]{1,0:T(8,128)S(1)}, f32[32,128]{1,0:T(8,128)S(1)}, u32[]{:S(2)}, u32[]{:S(2)}) collective-permute-start(f32[32,128]{1,0:T(8,128)S(1)} %get-tuple-element.34), channel_id=1, source_target_pairs={{0,2},{1,3},{2,4},{3,5},{4,6},{5,7},{6,0},{7,1},{8,10},{9,11},{10,... | collective-permute-start | bytes 49160 | tf_op jit(solution)/shard_map/ppermute | solution.py:309
  89.4 5.2 %collective-permute-start.17 = (f32[32,128]{1,0:T(8,128)S(1)}, f32[32,128]{1,0:T(8,128)S(1)}, u32[]{:S(2)}, u32[]{:S(2)}) collective-permute-start(f32[32,128]{1,0:T(8,128)S(1)} %get-tuple-element.34), channel_id=1, source_target_pairs={{0,4},{1,5},{2,6},{3,7},{4,0},{5,1},{6,2},{7,3},{8,12},{9,13},{10,... | collective-permute-start | bytes 49160 | tf_op jit(solution)/shard_map/ppermute | solution.py:309
  90.4 5.0 %collective-permute-start.18 = (f32[32,128]{1,0:T(8,128)S(1)}, f32[32,128]{1,0:T(8,128)S(1)}, u32[]{:S(2)}, u32[]{:S(2)}) collective-permute-start(f32[32,128]{1,0:T(8,128)S(1)} %get-tuple-element.34), channel_id=1, source_target_pairs={{0,6},{1,7},{2,0},{3,1},{4,2},{5,3},{6,4},{7,5},{8,14},{9,15},{10,... | collective-permute-start | bytes 49160 | tf_op jit(solution)/shard_map/ppermute | solution.py:309
  95.5 6.2 %collective-permute-start.19 = (f32[32,128]{1,0:T(8,128)S(1)}, f32[32,128]{1,0:T(8,128)S(1)}, u32[]{:S(2)}, u32[]{:S(2)}) collective-permute-start(f32[32,128]{1,0:T(8,128)S(1)} %multiply_add_fusion.4.refs_3_), channel_id=1, source_target_pairs={{0,8},{1,9},{2,10},{3,11},{4,12},{5,13},{6,14},{7,15},{8,16},{9,17... | collective-permute-start | bytes 49160 | tf_op jit(solution)/shard_map/ppermute | solution.py:309
  98.9 5.2 %collective-permute-start.20 = (f32[32,128]{1,0:T(8,128)S(1)}, f32[32,128]{1,0:T(8,128)S(1)}, u32[]{:S(2)}, u32[]{:S(2)}) collective-permute-start(f32[32,128]{1,0:T(8,128)S(1)} %multiply_add_fusion.4.refs_3_), channel_id=1, source_target_pairs={{0,16},{1,17},{2,18},{3,19},{4,20},{5,21},{6,22},{7,23},{8,24},{9,... | collective-permute-start | bytes 49160 | tf_op jit(solution)/shard_map/ppermute | solution.py:309
  98.9 5.2 %collective-permute-start.21 = (f32[32,128]{1,0:T(8,128)S(1)}, f32[32,128]{1,0:T(8,128)S(1)}, u32[]{:S(2)}, u32[]{:S(2)}) collective-permute-start(f32[32,128]{1,0:T(8,128)S(1)} %multiply_add_fusion.4.refs_3_), channel_id=1, source_target_pairs={{0,24},{1,25},{2,26},{3,27},{4,28},{5,29},{6,30},{7,31},{8,0},{9,1... | collective-permute-start | bytes 49160 | tf_op jit(solution)/shard_map/ppermute | solution.py:309
  110.7 1.2 collective-permute-start.22
  112.0 5.2 %collective-permute-start.23 = (f32[64,128]{1,0:T(8,128)S(1)}, f32[64,128]{1,0:T(8,128)S(1)}, u32[]{:S(2)}, u32[]{:S(2)}) collective-permute-start(f32[64,128]{1,0:T(8,128)S(1)} %multiply_add_fusion.refs_3_), channel_id=1, source_target_pairs={{0,32},{32,64},{64,96},{96,0},{1,33},{33,65},{65,97},{97,1},{2,34}... | collective-permute-start | bytes 98312 | tf_op jit(solution)/shard_map/ppermute | solution.py:309
  112.0 5.5 %collective-permute-start.24 = (f32[64,128]{1,0:T(8,128)S(1)}, f32[64,128]{1,0:T(8,128)S(1)}, u32[]{:S(2)}, u32[]{:S(2)}) collective-permute-start(f32[64,128]{1,0:T(8,128)S(1)} %multiply_add_fusion.refs_3_), channel_id=1, source_target_pairs={{0,64},{32,96},{64,0},{96,32},{1,65},{33,97},{65,1},{97,33},{2,66}... | collective-permute-start | bytes 98312 | tf_op jit(solution)/shard_map/ppermute | solution.py:309
  112.5 5.9 %collective-permute-start.25 = (f32[64,128]{1,0:T(8,128)S(1)}, f32[64,128]{1,0:T(8,128)S(1)}, u32[]{:S(2)}, u32[]{:S(2)}) collective-permute-start(f32[64,128]{1,0:T(8,128)S(1)} %multiply_add_fusion.refs_3_), channel_id=1, source_target_pairs={{0,96},{32,0},{64,32},{96,64},{1,97},{33,1},{65,33},{97,65},{2,98}... | collective-permute-start | bytes 98312 | tf_op jit(solution)/shard_map/ppermute | solution.py:309
  118.4 1.6 %copy-start.2 = (bf16[64,128,128]{2,1,0:T(8,128)(2,1)S(1)}, bf16[64,128,128]{2,1,0:T(8,128)(2,1)}, u32[]{:S(2)}) copy-start(bf16[64,128,128]{2,1,0:T(8,128)(2,1)} %copy-done) | copy-start | bytes 6291460
  127.3 27.5 %copy-start.15 = (f32[4096]{0:T(1024)S(1)}, f32[4096]{0:T(1024)}, u32[]{:S(2)}) copy-start(f32[4096]{0:T(1024)} %param.11) | copy-start | bytes 49156
  127.3 4.9 %collective-permute-start.26 = (f32[32,128]{1,0:T(8,128)S(1)}, f32[32,128]{1,0:T(8,128)S(1)}, u32[]{:S(2)}, u32[]{:S(2)}) collective-permute-start(f32[32,128]{1,0:T(8,128)S(1)} %get-tuple-element.36), channel_id=1, source_target_pairs={{0,2},{1,3},{2,4},{3,5},{4,6},{5,7},{6,0},{7,1},{8,10},{9,11},{10,... | collective-permute-start | bytes 49160 | tf_op jit(solution)/shard_map/ppermute | solution.py:309
  127.3 5.2 %collective-permute-start.27 = (f32[32,128]{1,0:T(8,128)S(1)}, f32[32,128]{1,0:T(8,128)S(1)}, u32[]{:S(2)}, u32[]{:S(2)}) collective-permute-start(f32[32,128]{1,0:T(8,128)S(1)} %get-tuple-element.36), channel_id=1, source_target_pairs={{0,4},{1,5},{2,6},{3,7},{4,0},{5,1},{6,2},{7,3},{8,12},{9,13},{10,... | collective-permute-start | bytes 49160 | tf_op jit(solution)/shard_map/ppermute | solution.py:309
  128.4 4.9 %collective-permute-start.28 = (f32[32,128]{1,0:T(8,128)S(1)}, f32[32,128]{1,0:T(8,128)S(1)}, u32[]{:S(2)}, u32[]{:S(2)}) collective-permute-start(f32[32,128]{1,0:T(8,128)S(1)} %get-tuple-element.36), channel_id=1, source_target_pairs={{0,6},{1,7},{2,0},{3,1},{4,2},{5,3},{6,4},{7,5},{8,14},{9,15},{10,... | collective-permute-start | bytes 49160 | tf_op jit(solution)/shard_map/ppermute | solution.py:309
  133.3 5.7 %collective-permute-start.29 = (f32[32,128]{1,0:T(8,128)S(1)}, f32[32,128]{1,0:T(8,128)S(1)}, u32[]{:S(2)}, u32[]{:S(2)}) collective-permute-start(f32[32,128]{1,0:T(8,128)S(1)} %multiply_add_fusion.3.refs_3_), channel_id=1, source_target_pairs={{0,8},{1,9},{2,10},{3,11},{4,12},{5,13},{6,14},{7,15},{8,16},{9,17... | collective-permute-start | bytes 49160 | tf_op jit(solution)/shard_map/ppermute | solution.py:309
  136.3 5.2 %collective-permute-start.30 = (f32[32,128]{1,0:T(8,128)S(1)}, f32[32,128]{1,0:T(8,128)S(1)}, u32[]{:S(2)}, u32[]{:S(2)}) collective-permute-start(f32[32,128]{1,0:T(8,128)S(1)} %multiply_add_fusion.3.refs_3_), channel_id=1, source_target_pairs={{0,16},{1,17},{2,18},{3,19},{4,20},{5,21},{6,22},{7,23},{8,24},{9,... | collective-permute-start | bytes 49160 | tf_op jit(solution)/shard_map/ppermute | solution.py:309
  137.2 4.3 %collective-permute-start.31 = (f32[32,128]{1,0:T(8,128)S(1)}, f32[32,128]{1,0:T(8,128)S(1)}, u32[]{:S(2)}, u32[]{:S(2)}) collective-permute-start(f32[32,128]{1,0:T(8,128)S(1)} %multiply_add_fusion.3.refs_3_), channel_id=1, source_target_pairs={{0,24},{1,25},{2,26},{3,27},{4,28},{5,29},{6,30},{7,31},{8,0},{9,1... | collective-permute-start | bytes 49160 | tf_op jit(solution)/shard_map/ppermute | solution.py:309
  147.5 1.3 collective-permute-start.33
  147.7 4.6 %collective-permute-start.32 = (f32[32,128]{1,0:T(8,128)S(1)}, f32[32,128]{1,0:T(8,128)S(1)}, u32[]{:S(2)}, u32[]{:S(2)}) collective-permute-start(f32[32,128]{1,0:T(8,128)S(1)} %multiply_add_fusion.2), channel_id=1, source_target_pairs={{0,1},{1,0},{2,3},{3,2},{4,5},{5,4},{6,7},{7,6},{8,9},{9,8},{10,11... | collective-permute-start | bytes 49160 | tf_op jit(solution)/shard_map/ppermute | solution.py:309
  148.9 4.9 %collective-permute-start.34 = (f32[8,128]{1,0:T(8,128)S(1)}, f32[8,128]{1,0:T(8,128)S(1)}, u32[]{:S(2)}, u32[]{:S(2)}) collective-permute-start(f32[8,128]{1,0:T(8,128)S(1)} %get-tuple-element.49), channel_id=1, source_target_pairs={{0,32},{32,64},{64,96},{96,0},{1,33},{33,65},{65,97},{97,1},{2,34}... | collective-permute-start | bytes 12296 | tf_op jit(solution)/shard_map/ppermute | solution.py:410
  148.9 5.2 %collective-permute-start.35 = (f32[8,128]{1,0:T(8,128)S(1)}, f32[8,128]{1,0:T(8,128)S(1)}, u32[]{:S(2)}, u32[]{:S(2)}) collective-permute-start(f32[8,128]{1,0:T(8,128)S(1)} %get-tuple-element.48), channel_id=1, source_target_pairs={{0,64},{32,96},{64,0},{96,32},{1,65},{33,97},{65,1},{97,33},{2,66}... | collective-permute-start | bytes 12296 | tf_op jit(solution)/shard_map/ppermute | solution.py:410
  149.0 5.6 %collective-permute-start.36 = (f32[8,128]{1,0:T(8,128)S(1)}, f32[8,128]{1,0:T(8,128)S(1)}, u32[]{:S(2)}, u32[]{:S(2)}) collective-permute-start(f32[8,128]{1,0:T(8,128)S(1)} %get-tuple-element.47), channel_id=1, source_target_pairs={{0,96},{32,0},{64,32},{96,64},{1,97},{33,1},{65,33},{97,65},{2,98}... | collective-permute-start | bytes 12296 | tf_op jit(solution)/shard_map/ppermute | solution.py:410
  (9 other events, 8.8 us)
where the time goes:
time: 156 us; the launch traced here: 155 us
  Pallas kernels  50.4 us (32%)
  starting transfers between devices  45.2 us (29%)
  waiting for transfers between devices  27.7 us (18%)
  local copies, waits for them, and re-layouts  14.6 us (9%)
  blocking collectives  12.8 us (8%)
  other arithmetic  3.62 us (2%)
    ppermute x34, starting transfers between devices, ring(): out.append(lax.ppermute(values, axis, pairs))  41.9 us
    pallas_call x6, Pallas kernels, log_sums(): pl.pallas_call(functools.partial(pass_kernel, bias_of, len(bias)), out_sh...  37.4 us
    ppermute x34, waiting for transfers between devices, ring(): out.append(lax.ppermute(values, axis, pairs))  26.2 us
    unnamed x40, local copies, waits for them, and re-layouts  13.3 us
    all_to_all x1, blocking collectives, shards(): lax.all_to_all(packed, 'src', split_axis=0, concat_axis=0, tiled=True)  12.8 us
    pallas_call x1, Pallas kernels, plan(): pl.pallas_call(plan_kernel, out_shape=[shape((col_room,), jnp.int32), sha...  7.62 us
    pallas_call x1, Pallas kernels, shards(): pl.pallas_call(unpack_kernel, out_shape=[shape((2 * count, 2 * D, BLOCK),...  3.75 us
    ppermute x3, starting transfers between devices, shards(): back.append(wanted if d == 0 else lax.ppermute(wanted, 'src', pairs))  3.29 us
  transfers between devices with their start and end apart: 37, of which 27 were waited for; matrix products, arithmetic and copies ran while one was open for 2% of the time, Pallas kernels for 0%

commit v1 on v0

v1 whole, which is shorter than its diff:
```python
import functools

import jax
import jax.numpy as jnp
from jax import lax
from jax.experimental import pallas as pl
from jax.experimental.pallas import tpu as pltpu
from jax.sharding import PartitionSpec as P

D = 64
BLOCK = 128
KG = 8
ITERS = 3
EPSILON = 0.25
LOWEST = -1e30
LOG2E = 1.4426950408889634
SCALE = LOG2E / EPSILON
PAIRS = 32
COPIES = 2
GROUP = 32
EXTRA = 16
HEAD = 8
STRIDE = 64


SMEM = pl.BlockSpec(memory_space=pltpu.SMEM)
VMEM = pl.BlockSpec(memory_space=pltpu.VMEM)
HBM = pl.BlockSpec(memory_space=pltpu.HBM)
PARAMS = pltpu.CompilerParams(vmem_limit_bytes=48 * 1024 * 1024)


def shape(dims, dtype=jnp.float32):
    return jax.ShapeDtypeStruct(dims, dtype)


def start_copies(pairs, sems):
    copies = [pltpu.make_async_copy(src, dst, sems.at[k]) for k, (src, dst) in enumerate(pairs)]
    for copy in copies:
        copy.start()
    return copies


def plan_kernel(half_ref, near_ref, far_ref, col_ref, row_ref, lists, sizes):
    halves = near_ref.shape[1] // 2
    slots = 2 * GROUP
    first = half_ref[0] * halves
    col_right = HEAD + (col_ref.shape[0] - HEAD) // 3
    row_right = HEAD + (row_ref.shape[0] - HEAD) // 3

    def clear(q, carry):
        sizes[q] = 0
        return carry

    lax.fori_loop(0, slots + 1, clear, 0, unroll=8)

    def one_block(b, position):
        at = col_right + 2 * position
        tiles = jnp.int32(0)
        for group, ref in enumerate((near_ref, far_ref)):
            count = ref[KG, first + b]
            named = [ref[k, first + b] + group * GROUP for k in range(KG)]
            for k in range(KG):
                col_ref[at + tiles + k] = named[k]
            named = [slot if k < 2 else jnp.where(k < count, slot, slots) for k, slot in enumerate(named)]
            known = [sizes[slot] for slot in named]
            for slot, size in zip(named, known):
                lists[slot * STRIDE + size] = b
            for slot, size in zip(named, known):
                sizes[slot] = size + 1
            tiles = tiles + count
        col_ref[at + tiles] = slots
        for k in range(KG):
            col_ref[HEAD + position + k] = b
        return position + (tiles + 1) // 2

    def finish(ref, right, pairs, none):
        ref[0] = (pairs + PAIRS - 1) // PAIRS

        def pad(k, carry):
            ref[HEAD + pairs + k] = 0
            ref[right + 2 * (pairs + k)] = none
            ref[right + 2 * (pairs + k) + 1] = none
            return carry

        lax.fori_loop(0, ref[0] * PAIRS - pairs, pad, 0)

    finish(col_ref, col_right, lax.fori_loop(0, halves, one_block, jnp.int32(0)), slots)

    def one_slot(q, position):
        size = sizes[q]
        lists[q * STRIDE + size] = halves
        pairs = (size + 1) // 2

        def one_pair(k, carry):
            row_ref[HEAD + position + k] = q
            for j in range(2):
                row_ref[row_right + 2 * (position + k) + j] = lists[q * STRIDE + 2 * k + j]
            return carry

        for k in range(4):
            one_pair(k, 0)
        lax.fori_loop(4, pairs, one_pair, 0)
        return position + pairs

    finish(row_ref, row_right, lax.fori_loop(0, slots, one_slot, jnp.int32(0)), halves)


def plan(half, near, far):
    halves = near.shape[1] // 2
    room = halves * KG + 2 * GROUP + PAIRS + KG
    return pl.pallas_call(
        plan_kernel,
        out_shape=[shape((HEAD + 3 * room,), jnp.int32)] * 2,
        in_specs=[SMEM] * 3,
        out_specs=[SMEM] * 2,
        scratch_shapes=[
            pltpu.SMEM(((2 * GROUP + 1) * STRIDE,), jnp.int32),
            pltpu.SMEM((2 * GROUP + 1,), jnp.int32),
        ],
    )(half.reshape(1), near, far)


def split3(values):
    high = values.astype(jnp.bfloat16)
    rest = values - high.astype(jnp.float32)
    middle = rest.astype(jnp.bfloat16)
    low = (rest - middle.astype(jnp.float32)).astype(jnp.bfloat16)
    return high, middle, low


def log_sum(values):
    top = functools.reduce(jnp.maximum, values)
    return top + jnp.log2(sum(jnp.exp2(value - top) for value in values))


def pack_kernel(place_ref, *refs):
    *ids_refs, points_hbm, potential_hbm, logmass_hbm, out_ref, points, potential, logmass, sems = refs
    copies = start_copies(
        [(potential_hbm, potential), (logmass_hbm, logmass), (points_hbm, points)], sems
    )
    place = place_ref[0]
    peers, per_peer = ids_refs[0].shape
    for copy in copies:
        copy.wait()
    for d, ids_ref in enumerate(ids_refs):
        other = lax.rem(place - d + peers, peers)

        def one_block(c, carry, ids_ref=ids_ref, other=other):
            t = ids_ref[place, c]
            block = points[:, pl.ds(pl.multiple_of(t * BLOCK, BLOCK), BLOCK)]
            wide = block.astype(jnp.float32)
            norm = jnp.sum(wide * wide, axis=0, keepdims=True)
            start = SCALE * (potential[pl.ds(t, 1), :] - 0.5 * norm)
            mass = LOG2E * logmass[pl.ds(t, 1), :]
            rows = [part.astype(jnp.float32) for part in split3(start) + split3(mass)]
            rows.append(jnp.zeros((EXTRA - len(rows), BLOCK), jnp.float32))
            out_ref[other * per_peer + c, :D, :] = block
            out_ref[other * per_peer + c, D:, :] = jnp.concatenate(rows, axis=0).astype(jnp.bfloat16)
            return carry

        lax.fori_loop(0, per_peer, one_block, 0, unroll=8)


def pack(place, ids, points, potential, logmass):
    count = ids[0].size
    return pl.pallas_call(
        pack_kernel,
        out_shape=shape((count, D + EXTRA, BLOCK), jnp.bfloat16),
        in_specs=[SMEM] * (1 + len(ids)) + [HBM] * 3,
        out_specs=VMEM,
        scratch_shapes=[
            pltpu.VMEM(points.shape, points.dtype),
            pltpu.VMEM(potential.shape, potential.dtype),
            pltpu.VMEM(logmass.shape, logmass.dtype),
            pltpu.SemaphoreType.DMA((3,)),
        ],
        compiler_params=PARAMS,
    )(place.reshape(1), *ids, points, potential, logmass)


def unpack_kernel(group, in_ref, *refs):
    outs, (right, left, start, mass, sems) = refs[-9:-5], refs[-5:]

    def one_block(q, carry):
        block = in_ref[q, :D, :]
        both = jnp.concatenate([block, block], axis=0)
        right[q] = both
        left[q] = both.T
        rows = in_ref[q, D:, :].astype(jnp.float32)
        start[pl.ds(q, 1), :] = rows[0:1] + rows[1:2] + rows[2:3]
        mass[pl.ds(q, 1), :] = rows[3:4] + rows[4:5] + rows[5:6]
        return carry

    lax.fori_loop(0, GROUP, one_block, 0, unroll=8)
    own = pl.ds(group * GROUP, GROUP)
    pairs = [(value, out.at[own]) for value, out in zip((right, left, start, mass), outs)]
    for copy in start_copies(pairs, sems):
        copy.wait()


def unpack(group, fetched, before):
    parts = [((BLOCK, BLOCK), jnp.bfloat16)] * 2 + [((BLOCK,), jnp.float32)] * 2
    return pl.pallas_call(
        functools.partial(unpack_kernel, group),
        out_shape=[shape((2 * GROUP, *dims), dtype) for dims, dtype in parts],
        in_specs=[VMEM] + [HBM] * len(before),
        out_specs=[HBM] * 4,
        scratch_shapes=[pltpu.VMEM((GROUP, *dims), dtype) for dims, dtype in parts]
        + [pltpu.SemaphoreType.DMA((4,))],
        input_output_aliases={1 + k: k for k in range(len(before))},
        compiler_params=PARAMS,
    )(fetched, *before)


def source_kernel(half_ref, points_hbm, right_hbm, left_hbm, norm_ref, points, right, left, sems):
    halves = right.shape[0]
    at = pl.multiple_of(half_ref[0] * (halves * BLOCK), halves * BLOCK)
    copy = pltpu.make_async_copy(points_hbm.at[:, pl.ds(at, halves * BLOCK)], points, sems.at[0])
    copy.start()
    copy.wait()

    def one_block(b, carry):
        wide = points[:, pl.ds(pl.multiple_of(b * BLOCK, BLOCK), BLOCK)].astype(jnp.float32)
        norm_ref[pl.ds(b, 1), :] = 0.5 * jnp.sum(wide * wide, axis=0, keepdims=True)
        scaled = SCALE * wide
        high = scaled.astype(jnp.bfloat16)
        low = (scaled - high.astype(jnp.float32)).astype(jnp.bfloat16)
        both = jnp.concatenate([high, low], axis=0)
        right[b] = both
        left[b] = both.T
        return carry

    lax.fori_loop(0, halves, one_block, 0, unroll=4)
    for copy in start_copies([(right, right_hbm), (left, left_hbm)], sems):
        copy.wait()


def source(half, halves, points):
    blocks = (halves, BLOCK, BLOCK)
    return pl.pallas_call(
        source_kernel,
        out_shape=[shape(blocks, jnp.bfloat16), shape(blocks, jnp.bfloat16), shape((halves, BLOCK))],
        in_specs=[SMEM, HBM],
        out_specs=[HBM, HBM, VMEM],
        scratch_shapes=[
            pltpu.VMEM((D, halves * BLOCK), jnp.bfloat16),
            pltpu.VMEM(blocks, jnp.bfloat16),
            pltpu.VMEM(blocks, jnp.bfloat16),
            pltpu.SemaphoreType.DMA((2,)),
        ],
        compiler_params=PARAMS,
    )(half.reshape(1), points)


def start_bias(start_ref):
    return start_ref[...]


def field_bias(mass_ref, *parts):
    return mass_ref[...] - log_sum([ref[...] for ref in parts])


def potential_bias(mass_ref, chosen_ref, *refs):
    dot = functools.partial(jnp.dot, preferred_element_type=jnp.float32)
    out = []
    for group in range(2):
        own = slice(group * GROUP, (group + 1) * GROUP)
        chosen = chosen_ref[group]
        sums = jnp.concatenate([ref[own, :] for ref in refs], axis=0)
        parts = sum(dot(chosen, part) for part in split3(sums))
        known = dot(chosen, jnp.ones_like(chosen)) > 0.5
        parts = jnp.where(known, parts, LOWEST)
        merged = log_sum([parts[k * GROUP : (k + 1) * GROUP] for k in range(len(refs))])
        out.append(mass_ref[own, :] - merged)
    return jnp.concatenate(out, axis=0)


def pass_kernel(bias_of, fixed_count, parts_count, *refs):
    remote_count = 3 + fixed_count
    remotes, refs = refs[:remote_count], refs[remote_count:]
    bias_parts, refs = refs[:parts_count], refs[parts_count:]
    out_ref, bias_ref, columns, peaks, masses, sems = refs[:6]
    locals_ = refs[6:]
    copies = start_copies(list(zip(remotes, locals_))[::-1], sems)
    list_ref, left_ref, right_ref, *fixed = locals_
    lefts, rights = left_ref.shape[0], right_ref.shape[0]
    square = (BLOCK, BLOCK)
    lane = lax.broadcasted_iota(jnp.int32, square, 1)
    eye = jnp.where(lane == lax.broadcasted_iota(jnp.int32, square, 0), 1.0, 0.0).astype(jnp.bfloat16)
    lane = jnp.where(lane < 3 * GROUP, lane % GROUP, -1)
    peaks[...] = jnp.full_like(peaks, LOWEST)
    masses[...] = jnp.zeros_like(masses)
    for copy in copies[:fixed_count]:
        copy.wait()
    bias_ref[...] = bias_of(*fixed, *bias_parts)
    for group in range(lefts // GROUP):
        high, middle, low = split3(bias_ref[group * GROUP : (group + 1) * GROUP, :])
        parts = jnp.concatenate([high, middle, low, jnp.zeros_like(high)], axis=0)
        turned = lax.dot_general(
            eye, parts, (((1,), (1,)), ((), ())), preferred_element_type=jnp.float32
        )

        def fill(k, carry, group=group, turned=turned):
            columns[group * GROUP + k] = jnp.where(lane == k, turned, 0.0).astype(jnp.bfloat16)
            return carry

        lax.fori_loop(0, GROUP, fill, 0, unroll=4)
    for copy in copies[fixed_count:]:
        copy.wait()
    rights_at = HEAD + (list_ref.shape[0] - HEAD) // 3
    ones = jnp.ones((BLOCK, 2 * BLOCK), jnp.bfloat16)

    def fold(copy, r, scores):
        scores = scores.reshape(BLOCK // 8, 8, BLOCK)
        old = peaks[copy, r]
        top = jnp.maximum(old, jnp.max(scores, axis=0))
        mass = jnp.sum(jnp.exp2(scores - top[None]), axis=0)
        masses[copy, r] = masses[copy, r] * jnp.exp2(old - top) + mass
        peaks[copy, r] = top

    def right_block(r):
        return right_ref[jnp.minimum(r, rights - 1)]

    def step(t, carry):
        for u in range(PAIRS):
            i = t * PAIRS + u
            l = list_ref[HEAD + i]
            first, second = list_ref[rights_at + 2 * i], list_ref[rights_at + 2 * i + 1]
            left = jnp.concatenate([left_ref[l], columns[l]], axis=1)
            right = jnp.concatenate([right_block(first), right_block(second)], axis=1)
            scores = jnp.dot(
                left, jnp.concatenate([right, ones], axis=0), preferred_element_type=jnp.float32
            )
            fold((2 * u) % COPIES, first, scores[:, :BLOCK])
            fold((2 * u + 1) % COPIES, second, scores[:, BLOCK:])
        return carry

    lax.fori_loop(0, list_ref[0], step, 0)

    def finish(octet, carry):
        rows = []
        for k in range(8):
            r = octet * 8 + k
            tops = [peaks[copy, r] for copy in range(COPIES)]
            top = jnp.max(functools.reduce(jnp.maximum, tops), axis=0, keepdims=True)
            mass = sum(masses[copy, r] * jnp.exp2(tops[copy] - top) for copy in range(COPIES))
            rows.append(top + jnp.log2(jnp.sum(mass, axis=0, keepdims=True)))
        out_ref[pl.ds(pl.multiple_of(octet * 8, 8), 8), :] = jnp.concatenate(rows, axis=0)
        return carry

    lax.fori_loop(0, rights // 8, finish, 0)


def log_sums(pairs, left, right, bias_of, fixed, parts):
    lefts, rights = left.shape[0], right.shape[0]
    remotes = [pairs, left, right, *fixed]
    return pl.pallas_call(
        functools.partial(pass_kernel, bias_of, len(fixed), len(parts)),
        out_shape=[shape((rights, BLOCK)), shape((lefts, BLOCK))],
        in_specs=[HBM] * len(remotes) + [VMEM] * len(parts),
        out_specs=[VMEM, VMEM],
        scratch_shapes=[
            pltpu.VMEM((lefts, BLOCK, BLOCK), jnp.bfloat16),
            pltpu.VMEM((COPIES, rights + 1, 8, BLOCK), jnp.float32),
            pltpu.VMEM((COPIES, rights + 1, 8, BLOCK), jnp.float32),
            pltpu.SemaphoreType.DMA((len(remotes),)),
            pltpu.SMEM(pairs.shape, pairs.dtype),
        ]
        + [pltpu.VMEM(value.shape, value.dtype) for value in remotes[1:]],
        compiler_params=PARAMS,
    )(*remotes, *parts)


def ring(values, axis, size, stride=1):
    places = lax.axis_size(axis)
    out = [values]
    for d in range(1, size):
        pairs = []
        for i in range(places):
            place = i // stride % size
            pairs.append((i, i + ((place + d) % size - place) * stride))
        out.append(lax.ppermute(values, axis, pairs))
    return out


def shards(
    source_points,
    source_logmass,
    target_points,
    target_logmass,
    target_potential,
    tile_slot,
    tile_counts,
    fetch_ids,
):
    peers = lax.axis_size("src")
    blocks = tile_counts.shape[0]
    halves = blocks // 2
    per_peer = fetch_ids.shape[1]
    owned = target_potential.shape[0] // BLOCK
    count = peers * per_peer
    place = lax.axis_index("src")
    half = lax.axis_index("grp") % 2

    def swap(values):
        return ring(values, "grp", 2, 1)[1]

    tiles = jnp.concatenate([tile_slot.T, tile_counts.T], axis=0)
    ids = ring(fetch_ids, "src", peers)
    packed = pack(
        place,
        ids,
        target_points.T,
        target_potential.reshape(owned, BLOCK),
        target_logmass.reshape(owned, BLOCK),
    )
    ids = jnp.stack(ids)
    col_pairs, row_pairs = plan(half, tiles, swap(tiles))
    fetched = lax.all_to_all(packed, "src", split_axis=0, concat_axis=0, tiled=True)
    points_right, points_left, source_half = source(half, halves, source_points.T)
    targets_right, targets_left, potentials, slot_mass = unpack(1, swap(fetched), unpack(0, fetched, []))
    source_mass = LOG2E * lax.dynamic_slice(
        source_logmass.reshape(blocks, BLOCK), (half * halves, 0), (halves, BLOCK)
    )

    all_ids = jnp.stack([ids, swap(ids)])
    same = all_ids[:, :, :, None, :] == all_ids[:, :1, :, :, None]
    same = same[:, :, :, :, None, :] & jnp.eye(peers, dtype=bool)[:, None, :, None]
    same = same.reshape(2, peers, count, 1, count) & jnp.eye(peers, dtype=bool)[:, None, :, None]
    chosen = same.reshape(2, peers * count, peers * count).astype(jnp.bfloat16)

    for sweep_index in range(ITERS):
        if sweep_index == 0:
            rows, _ = log_sums(row_pairs, targets_left, points_right, start_bias, [potentials], [])
        else:
            rows, _ = log_sums(
                row_pairs, targets_left, points_right, potential_bias, [slot_mass, chosen], col_parts
            )
        rows = log_sum(ring(rows, "grp", 4, 2))
        row_parts = ring(rows, "grp", 4, 8)
        cols, field = log_sums(col_pairs, points_left, targets_right, field_bias, [source_mass], row_parts)
        if sweep_index < ITERS - 1:
            other = swap(cols)
            cols = log_sum([cols, jnp.concatenate([other[count:], other[:count]], axis=0)])
            col_parts = ring(cols, "src", peers)
    field = field * (1.0 / SCALE) + source_half
    other = swap(field)
    low = half == 0
    source_field = jnp.concatenate([jnp.where(low, field, other), jnp.where(low, other, field)], axis=0)

    cols = log_sum([cols[:count], swap(cols[count:])]).reshape(peers, per_peer, BLOCK)
    back, requested = [], []
    for d in range(peers):
        wanted = lax.dynamic_slice(cols, ((place + d) % peers, 0, 0), (1, per_peer, BLOCK))[0]
        pairs = [(i, (i + d) % peers) for i in range(peers)]
        back.append(wanted if d == 0 else lax.ppermute(wanted, "src", pairs))
        requested.append(lax.dynamic_slice(ids, (d, place, 0), (1, 1, per_peer))[0, 0])
    blocks_here = jnp.arange(owned, dtype=jnp.int32)[:, None]
    parts = [
        jnp.max(jnp.where((blocks_here == wants[None])[..., None], sums[None], LOWEST), axis=1)
        for wants, sums in zip(requested, back)
    ]
    owned_pot = LOG2E * target_logmass.reshape(owned, BLOCK) - log_sum(parts)
    target_half = 0.5 * jnp.sum(jnp.square(target_points.astype(jnp.float32)), -1)
    target_field = owned_pot.reshape(-1) * (1.0 / SCALE) + target_half
    return (source_field.reshape(-1), target_field)


def solution(mesh):
    return jax.shard_map(
        shards,
        mesh=mesh,
        in_specs=(
            P("src", None),
            P("src"),
            P(("src", "grp"), None),
            P(("src", "grp")),
            P(("src", "grp")),
            P("src", "grp"),
            P("src", "grp"),
            P("src", "grp"),
        ),
        out_specs=(P("src"), P(("src", "grp"))),
        check_vma=False,
    )
```

time: 156 us -> 155 us (level)
  Pallas kernels: 50.4 us -> 59 us
  starting transfers between devices: 45.2 us -> 38.1 us
  local copies, waits for them, and re-layouts: 14.6 us -> 12.9 us
    pallas_call x10 -> x11, Pallas kernels: 50.4 us -> 59 us  [the longest x6 46.7 us: log_sums(): pl.pallas_call(functools.partial(pass_kernel, bias_of, len(fixed), len(pa...]
    ppermute x34, starting transfers between devices: 41.9 us -> 34.8 us  [ring(): out.append(lax.ppermute(values, axis, pairs))]
    unnamed x40 -> x44, local copies, waits for them, and re-layouts: 13.3 us -> 11.8 us
  transfers between devices with their start and end apart: 37 -> 37, of which waited for: 27 -> 32; matrix products, arithmetic and copies ran while one was open for 2% -> 2% of each run, Pallas kernels for 0% -> 6%
where the time goes in v1:
time: 155 us; the launch traced here: 156 us
  Pallas kernels  59 us (38%)
  starting transfers between devices  38.1 us (25%)
  waiting for transfers between devices  29.1 us (19%)
  blocking collectives  13 us (8%)
  local copies, waits for them, and re-layouts  12.9 us (8%)
  other arithmetic  2.24 us (1%)
    pallas_call x6, Pallas kernels, log_sums(): pl.pallas_call(functools.partial(pass_kernel, bias_of, len(fixed), len(pa...  46.7 us
    ppermute x34, starting transfers between devices, ring(): out.append(lax.ppermute(values, axis, pairs))  34.8 us
    ppermute x34, waiting for transfers between devices, ring(): out.append(lax.ppermute(values, axis, pairs))  27.6 us
    all_to_all x1, blocking collectives, shards(): lax.all_to_all(packed, 'src', split_axis=0, concat_axis=0, tiled=True)  13 us
    unnamed x44, local copies, waits for them, and re-layouts  11.8 us
    pallas_call x1, Pallas kernels, plan(): pl.pallas_call(plan_kernel, out_shape=[shape((HEAD + 3 * room,), jnp.int3...  6.46 us
    pallas_call x2, Pallas kernels, unpack(): pl.pallas_call(functools.partial(unpack_kernel, group), out_shape=[shape(...  3.81 us
    ppermute x3, starting transfers between devices, shards(): back.append(wanted if d == 0 else lax.ppermute(wanted, 'src', pairs))  3.29 us
  transfers between devices with their start and end apart: 37, of which 32 were waited for; matrix products, arithmetic and copies ran while one was open for 2% of the time, Pallas kernels for 6%

profile of v1, /device:TPU:0, one launch (start us, length us, event | category | flops | bytes accessed | tf_op | source)
XLA Modules:
  0.0 155.5 jit_solution(7299394309562379206)
XLA Ops:
  0.7 1.6 %collective-permute-start.1 = (s32[4,8]{1,0:T(4,128)}, s32[4,8]{1,0:T(4,128)S(1)}, u32[]{:S(2)}, u32[]{:S(2)}) collective-permute-start(s32[4,8]{1,0:T(4,128)} %refs_0_.1), channel_id=1, source_target_pairs={{0,32},{32,64},{64,96},{96,0},{1,33},{33,65},{65,97},{97,1},{2,34}... | collective-permute-start | bytes 392 | tf_op jit(solution)/shard_map/ppermute | solution.py:382
  2.3 2.7 %collective-permute-start.2 = (s32[4,8]{1,0:T(4,128)}, s32[4,8]{1,0:T(4,128)S(1)}, u32[]{:S(2)}, u32[]{:S(2)}) collective-permute-start(s32[4,8]{1,0:T(4,128)} %refs_0_.1), channel_id=1, source_target_pairs={{0,64},{32,96},{64,0},{96,32},{1,65},{33,97},{65,1},{97,33},{2,66}... | collective-permute-start | bytes 392 | tf_op jit(solution)/shard_map/ppermute | solution.py:382
  5.0 1.4 collective-permute-start.3
  6.5 1.1 collective-permute-done.2.refs_2_
  7.6 1.2 collective-permute-done.3.refs_3_
  8.8 1.0 copy-done.7
  12.0 1.1 shard_map.97
  13.1 13.0 %all_to_all.5.in_ref = bf16[32,80,128]{2,1,0:T(8,128)(2,1)} all-to-all(bf16[32,80,128]{2,1,0:T(8,128)(2,1)S(1)} %shard_map.97), channel_id=1, replica_groups=mesh['src'=4,'grp'=32] {'src'}, dimensions={0} | all-to-all | bytes 1310720 | tf_op jit(solution)/shard_map/all_to_all | solution.py:419
  27.3 1.0 shard_map.96
  28.3 1.0 copy-done.3
  29.9 6.5 %shard_map.95 = (s32[1088]{0:T(1024)}, s32[1088]{0:T(1024)}) custom-call(s32[1]{0:T(128)} %bitcast.half_ref, s32[9,64]{1,0:T(8,128)} %copy-done.17, s32[9,64]{1,0:T(8,128)} %copy-done.19), custom_call_target="tpu_custom_call" | custom-call | tf_op jit(solution)/shard_map/pallas_call | solution.py:111
  36.4 1.9 %shard_map.98 = (bf16[64,128,128]{2,1,0:T(8,128)(2,1)S(1)}, bf16[64,128,128]{2,1,0:T(8,128)(2,1)S(1)}, f32[64,128]{1,0:T(8,128)S(1)}, f32[64,128]{1,0:T(8,128)S(1)}) custom-call(bf16[32,80,128]{2,1,0:T(8,128)(2,1)} %all_to_all.5.in_ref), custom_call_target="tpu_custom_call" | custom-call | tf_op jit(solution)/shard_map/pallas_call | solution.py:203
  38.3 1.9 %shard_map.99 = (bf16[64,128,128]{2,1,0:T(8,128)(2,1)S(1)}, bf16[64,128,128]{2,1,0:T(8,128)(2,1)S(1)}, f32[64,128]{1,0:T(8,128)S(1)}, f32[64,128]{1,0:T(8,128)S(1)}) custom-call(bf16[32,80,128]{2,1,0:T(8,128)(2,1)} %collective-permute-done.4.in_ref, ...), custom_call_target="tpu_custom_call", output_to_operand_aliasing={{0}: (1, {}), {1}: (2, {}), {2}: (3, {}), {3}: (4, {})} | custom-call | tf_op jit(solution)/shard_map/pallas_call | solution.py:203
  40.2 7.2 %shard_map.100 = (f32[32,128]{1,0:T(8,128)S(1)}, f32[64,128]{1,0:T(8,128)}) custom-call(s32[1088]{0:T(1024)S(1)} %copy-done.11, bf16[64,128,128]{2,1,0:T(8,128)(2,1)S(1)} %get-tuple-element.30.refs_1_, bf16[32,128,128]{2,1,0:T(8,128)(2,1)S(1)} %copy-done.4, f32[64,128]{1,0:T(8,128)S(1)} %get-tuple-element.33.refs_3_), custom_call_target="tpu_custom_call" | custom-call | tf_op jit(solution)/shard_map/pallas_call | solution.py:357
  47.5 1.3 copy-done
  48.9 2.6 %collective-permute-start.7 = (f32[32,128]{1,0:T(8,128)S(1)}, f32[32,128]{1,0:T(8,128)S(1)}, u32[]{:S(2)}, u32[]{:S(2)}) collective-permute-start(f32[32,128]{1,0:T(8,128)S(1)} %get-tuple-element.34), channel_id=1, source_target_pairs={{0,4},{1,5},{2,6},{3,7},{4,0},{5,1},{6,2},{7,3},{8,12},{9,13},{10,... | collective-permute-start | bytes 49160 | tf_op jit(solution)/shard_map/ppermute | solution.py:382
  52.1 1.7 %collective-permute-done.6 = f32[32,128]{1,0:T(8,128)S(1)} collective-permute-done((f32[32,128]{1,0:T(8,128)S(1)}, f32[32,128]{1,0:T(8,128)S(1)}, u32[]{:S(2)}, u32[]{:S(2)}) %collective-permute-start.6) | collective-permute-done | bytes 16416 | tf_op jit(solution)/shard_map/ppermute | solution.py:382
  54.1 1.1 collective-permute-done.8
  55.3 2.0 %collective-permute-start.10 = (f32[32,128]{1,0:T(8,128)S(1)}, f32[32,128]{1,0:T(8,128)S(1)}, u32[]{:S(2)}, u32[]{:S(2)}) collective-permute-start(f32[32,128]{1,0:T(8,128)S(1)} %multiply_add_fusion.5.refs_4_), channel_id=1, source_target_pairs={{0,16},{1,17},{2,18},{3,19},{4,20},{5,21},{6,22},{7,23},{8,24},{9,... | collective-permute-start | bytes 49160 | tf_op jit(solution)/shard_map/ppermute | solution.py:382
  57.8 1.5 collective-permute-start.9
  59.8 0.8 collective-permute-done.10.refs_6_
  61.0 1.8 %collective-permute-done.9.refs_5_ = f32[32,128]{1,0:T(8,128)S(1)} collective-permute-done((f32[32,128]{1,0:T(8,128)S(1)}, f32[32,128]{1,0:T(8,128)S(1)}, u32[]{:S(2)}, u32[]{:S(2)}) %collective-permute-start.9) | collective-permute-done | bytes 16416 | tf_op jit(solution)/shard_map/ppermute | solution.py:382
  62.8 8.3 %shard_map.101 = (f32[64,128]{1,0:T(8,128)S(1)}, f32[32,128]{1,0:T(8,128)}) custom-call(s32[1088]{0:T(1024)S(1)} %copy-done.10, bf16[32,128,128]{2,1,0:T(8,128)(2,1)S(1)} %get-tuple-element.23.refs_1_, bf16[64,128,128]{2,1,0:T(8,128)(2,1)S(1)} %get-tuple-element.28.refs_2_, f32[32,128]{1,0:T(8,128)S(1)} %dynamic-slice_multiply_fusion.refs_3_, ...), custom_call_target="tpu_custom_call" | custom-call | tf_op jit(solution)/shard_map/pallas_call | solution.py:357
  72.5 1.2 collective-permute-start.14
  73.7 2.5 %collective-permute-start.15 = (f32[64,128]{1,0:T(8,128)S(1)}, f32[64,128]{1,0:T(8,128)S(1)}, u32[]{:S(2)}, u32[]{:S(2)}) collective-permute-start(f32[64,128]{1,0:T(8,128)S(1)} %multiply_add_fusion.1.refs_5_), channel_id=1, source_target_pairs={{0,96},{32,0},{64,32},{96,64},{1,97},{33,1},{65,33},{97,65},{2,98}... | collective-permute-start | bytes 98312 | tf_op jit(solution)/shard_map/ppermute | solution.py:382
  76.2 1.4 collective-permute-done.13.refs_6_
  78.0 0.8 collective-permute-done.15.refs_8_
  78.8 1.6 %copy-done.1 = bf16[64,128,128]{2,1,0:T(8,128)(2,1)S(1)} copy-done((bf16[64,128,128]{2,1,0:T(8,128)(2,1)S(1)}, bf16[64,128,128]{2,1,0:T(8,128)(2,1)}, u32[]{:S(2)}) %copy-start.1) | copy-done | bytes 2097176
  80.4 1.2 copy-done.5
  81.6 7.6 %shard_map.102 = (f32[32,128]{1,0:T(8,128)S(1)}, f32[64,128]{1,0:T(8,128)}) custom-call(s32[1088]{0:T(1024)S(1)} %copy-done.11, bf16[64,128,128]{2,1,0:T(8,128)(2,1)S(1)} %copy-done.1, bf16[32,128,128]{2,1,0:T(8,128)(2,1)S(1)} %copy-done.5, f32[64,128]{1,0:T(8,128)S(1)} %get-tuple-element.32.refs_3_, bf16[2,128,128]{2,1,0:T(8,128)(2,1)S(1)} %and_convert_fusion.refs_4_, ...), custom_call_target="tpu_custom_call" | custom-call | tf_op jit(solution)/shard_map/pallas_call | solution.py:357
  89.3 2.1 %collective-permute-start.17 = (f32[32,128]{1,0:T(8,128)S(1)}, f32[32,128]{1,0:T(8,128)S(1)}, u32[]{:S(2)}, u32[]{:S(2)}) collective-permute-start(f32[32,128]{1,0:T(8,128)S(1)} %get-tuple-element.36), channel_id=1, source_target_pairs={{0,4},{1,5},{2,6},{3,7},{4,0},{5,1},{6,2},{7,3},{8,12},{9,13},{10,... | collective-permute-start | bytes 49160 | tf_op jit(solution)/shard_map/ppermute | solution.py:382
  91.4 1.2 collective-permute-start.18
  92.5 1.7 %collective-permute-done.16 = f32[32,128]{1,0:T(8,128)S(1)} collective-permute-done((f32[32,128]{1,0:T(8,128)S(1)}, f32[32,128]{1,0:T(8,128)S(1)}, u32[]{:S(2)}, u32[]{:S(2)}) %collective-permute-start.16) | collective-permute-done | bytes 16416 | tf_op jit(solution)/shard_map/ppermute | solution.py:382
  95.5 3.1 %collective-permute-start.21 = (f32[32,128]{1,0:T(8,128)S(1)}, f32[32,128]{1,0:T(8,128)S(1)}, u32[]{:S(2)}, u32[]{:S(2)}) collective-permute-start(f32[32,128]{1,0:T(8,128)S(1)} %multiply_add_fusion.4.refs_4_), channel_id=1, source_target_pairs={{0,24},{1,25},{2,26},{3,27},{4,28},{5,29},{6,30},{7,31},{8,0},{9,1... | collective-permute-start | bytes 49160 | tf_op jit(solution)/shard_map/ppermute | solution.py:382
  98.6 1.7 %collective-permute-done.19.refs_5_ = f32[32,128]{1,0:T(8,128)S(1)} collective-permute-done((f32[32,128]{1,0:T(8,128)S(1)}, f32[32,128]{1,0:T(8,128)S(1)}, u32[]{:S(2)}, u32[]{:S(2)}) %collective-permute-start.19) | collective-permute-done | bytes 16416 | tf_op jit(solution)/shard_map/ppermute | solution.py:382
  101.4 8.3 %shard_map.103 = (f32[64,128]{1,0:T(8,128)S(1)}, f32[32,128]{1,0:T(8,128)}) custom-call(s32[1088]{0:T(1024)S(1)} %copy-done.10, bf16[32,128,128]{2,1,0:T(8,128)(2,1)S(1)} %get-tuple-element.23.refs_1_, bf16[64,128,128]{2,1,0:T(8,128)(2,1)S(1)} %get-tuple-element.28.refs_2_, f32[32,128]{1,0:T(8,128)S(1)} %dynamic-slice_multiply_fusion.refs_3_, ...), custom_call_target="tpu_custom_call" | custom-call | tf_op jit(solution)/shard_map/pallas_call | solution.py:357
  110.0 1.0 collective-permute-done.22
  111.2 3.1 %collective-permute-start.25 = (f32[64,128]{1,0:T(8,128)S(1)}, f32[64,128]{1,0:T(8,128)S(1)}, u32[]{:S(2)}, u32[]{:S(2)}) collective-permute-start(f32[64,128]{1,0:T(8,128)S(1)} %multiply_add_fusion.refs_5_), channel_id=1, source_target_pairs={{0,96},{32,0},{64,32},{96,64},{1,97},{33,1},{65,33},{97,65},{2,98}... | collective-permute-start | bytes 98312 | tf_op jit(solution)/shard_map/ppermute | solution.py:382
  114.3 1.9 %collective-permute-done.23.refs_6_ = f32[64,128]{1,0:T(8,128)S(1)} collective-permute-done((f32[64,128]{1,0:T(8,128)S(1)}, f32[64,128]{1,0:T(8,128)S(1)}, u32[]{:S(2)}, u32[]{:S(2)}) %collective-permute-start.23) | collective-permute-done | bytes 32800 | tf_op jit(solution)/shard_map/ppermute | solution.py:382
  117.4 1.6 %copy-done.2 = bf16[64,128,128]{2,1,0:T(8,128)(2,1)S(1)} copy-done((bf16[64,128,128]{2,1,0:T(8,128)(2,1)S(1)}, bf16[64,128,128]{2,1,0:T(8,128)(2,1)}, u32[]{:S(2)}) %copy-start.2) | copy-done | bytes 2097176
  119.0 1.2 copy-done.6
  120.2 7.6 %shard_map.104 = (f32[32,128]{1,0:T(8,128)S(1)}, f32[64,128]{1,0:T(8,128)}) custom-call(s32[1088]{0:T(1024)S(1)} %copy-done.11, bf16[64,128,128]{2,1,0:T(8,128)(2,1)S(1)} %copy-done.2, bf16[32,128,128]{2,1,0:T(8,128)(2,1)S(1)} %copy-done.6, f32[64,128]{1,0:T(8,128)S(1)} %get-tuple-element.32.refs_3_, bf16[2,128,128]{2,1,0:T(8,128)(2,1)S(1)} %and_convert_fusion.refs_4_, ...), custom_call_target="tpu_custom_call" | custom-call | tf_op jit(solution)/shard_map/pallas_call | solution.py:357
  128.3 2.8 %collective-permute-start.28 = (f32[32,128]{1,0:T(8,128)S(1)}, f32[32,128]{1,0:T(8,128)S(1)}, u32[]{:S(2)}, u32[]{:S(2)}) collective-permute-start(f32[32,128]{1,0:T(8,128)S(1)} %get-tuple-element.38), channel_id=1, source_target_pairs={{0,6},{1,7},{2,0},{3,1},{4,2},{5,3},{6,4},{7,5},{8,14},{9,15},{10,... | collective-permute-start | bytes 49160 | tf_op jit(solution)/shard_map/ppermute | solution.py:382
  131.1 1.7 %collective-permute-done.26 = f32[32,128]{1,0:T(8,128)S(1)} collective-permute-done((f32[32,128]{1,0:T(8,128)S(1)}, f32[32,128]{1,0:T(8,128)S(1)}, u32[]{:S(2)}, u32[]{:S(2)}) %collective-permute-start.26) | collective-permute-done | bytes 16416 | tf_op jit(solution)/shard_map/ppermute | solution.py:382
  134.3 2.9 %collective-permute-start.31 = (f32[32,128]{1,0:T(8,128)S(1)}, f32[32,128]{1,0:T(8,128)S(1)}, u32[]{:S(2)}, u32[]{:S(2)}) collective-permute-start(f32[32,128]{1,0:T(8,128)S(1)} %multiply_add_fusion.3.refs_4_), channel_id=1, source_target_pairs={{0,24},{1,25},{2,26},{3,27},{4,28},{5,29},{6,30},{7,31},{8,0},{9,1... | collective-permute-start | bytes 49160 | tf_op jit(solution)/shard_map/ppermute | solution.py:382
  137.2 1.7 %collective-permute-done.29.refs_5_ = f32[32,128]{1,0:T(8,128)S(1)} collective-permute-done((f32[32,128]{1,0:T(8,128)S(1)}, f32[32,128]{1,0:T(8,128)S(1)}, u32[]{:S(2)}, u32[]{:S(2)}) %collective-permute-start.29) | collective-permute-done | bytes 16416 | tf_op jit(solution)/shard_map/ppermute | solution.py:382
  139.9 7.7 %shard_map.105 = (f32[64,128]{1,0:T(8,128)S(1)}, f32[32,128]{1,0:T(8,128)S(1)}) custom-call(s32[1088]{0:T(1024)S(1)} %copy-done.10, bf16[32,128,128]{2,1,0:T(8,128)(2,1)S(1)} %get-tuple-element.23.refs_1_, bf16[64,128,128]{2,1,0:T(8,128)(2,1)S(1)} %get-tuple-element.28.refs_2_, f32[32,128]{1,0:T(8,128)S(1)} %dynamic-slice_multiply_fusion.refs_3_, ...), custom_call_target="tpu_custom_call" | custom-call | tf_op jit(solution)/shard_map/pallas_call | solution.py:357
  149.2 3.1 %collective-permute-start.36 = (f32[8,128]{1,0:T(8,128)S(1)}, f32[8,128]{1,0:T(8,128)S(1)}, u32[]{:S(2)}, u32[]{:S(2)}) collective-permute-start(f32[8,128]{1,0:T(8,128)S(1)} %get-tuple-element.49), channel_id=1, source_target_pairs={{0,96},{32,0},{64,32},{96,64},{1,97},{33,1},{65,33},{97,65},{2,98}... | collective-permute-start | bytes 12296 | tf_op jit(solution)/shard_map/ppermute | solution.py:456
  (121 shorter events, 19.8 us)
Async XLA Ops:
  0.6 26.1 %copy-start.16 = (s32[4,8]{1,0:T(4,128)S(1)}, s32[4,8]{1,0:T(4,128)}, u32[]{:S(2)}) copy-start(s32[4,8]{1,0:T(4,128)} %refs_0_.1) | copy-start | bytes 388
  0.6 25.4 %copy-start.20 = (s32[64,8]{0,1:T(8,128)S(1)}, s32[64,8]{0,1:T(8,128)}, u32[]{:S(2)}) copy-start(s32[64,8]{0,1:T(8,128)} %param.13) | copy-start | bytes 6148
  0.7 25.4 %copy-start.21 = (s32[64,1]{0,1:T(1,128)S(1)}, s32[64,1]{0,1:T(1,128)}, u32[]{:S(2)}) copy-start(s32[64,1]{0,1:T(1,128)} %param.14) | copy-start | bytes 772
  0.7 5.8 %collective-permute-start.1 = (s32[4,8]{1,0:T(4,128)}, s32[4,8]{1,0:T(4,128)S(1)}, u32[]{:S(2)}, u32[]{:S(2)}) collective-permute-start(s32[4,8]{1,0:T(4,128)} %refs_0_.1), channel_id=1, source_target_pairs={{0,32},{32,64},{64,96},{96,0},{1,33},{33,65},{65,97},{97,1},{2,34}... | collective-permute-start | bytes 392 | tf_op jit(solution)/shard_map/ppermute | solution.py:382
  2.3 5.3 %collective-permute-start.2 = (s32[4,8]{1,0:T(4,128)}, s32[4,8]{1,0:T(4,128)S(1)}, u32[]{:S(2)}, u32[]{:S(2)}) collective-permute-start(s32[4,8]{1,0:T(4,128)} %refs_0_.1), channel_id=1, source_target_pairs={{0,64},{32,96},{64,0},{96,32},{1,65},{33,97},{65,1},{97,33},{2,66}... | collective-permute-start | bytes 392 | tf_op jit(solution)/shard_map/ppermute | solution.py:382
  5.0 3.8 %collective-permute-start.3 = (s32[4,8]{1,0:T(4,128)}, s32[4,8]{1,0:T(4,128)S(1)}, u32[]{:S(2)}, u32[]{:S(2)}) collective-permute-start(s32[4,8]{1,0:T(4,128)} %refs_0_.1), channel_id=1, source_target_pairs={{0,96},{32,0},{64,32},{96,64},{1,97},{33,1},{65,33},{97,65},{2,98}... | collective-permute-start | bytes 392 | tf_op jit(solution)/shard_map/ppermute | solution.py:382
  12.0 14.7 %copy-start.18 = (f32[8192]{0:T(1024)S(1)}, f32[8192]{0:T(1024)}, u32[]{:S(2)}) copy-start(f32[8192]{0:T(1024)} %param.9) | copy-start | bytes 98308
  12.0 15.3 %copy-start.9 = (bf16[8192,64]{0,1:T(8,128)(2,1)S(1)}, bf16[8192,64]{0,1:T(8,128)(2,1)}, u32[]{:S(2)}) copy-start(bf16[8192,64]{0,1:T(8,128)(2,1)} %param.8) | copy-start | bytes 3145732
  26.1 12.1 %collective-permute-start.4 = (bf16[32,80,128]{2,1,0:T(8,128)(2,1)}, bf16[32,80,128]{2,1,0:T(8,128)(2,1)}, u32[]{:S(2)}, u32[]{:S(2)}) collective-permute-start(bf16[32,80,128]{2,1,0:T(8,128)(2,1)} %all_to_all.5.in_ref), channel_id=1, source_target_pairs={{0,1},{1,0},{2,3},{3,2},{4,5},{5,4},{6,7},{7,6},{8,9},{9,8},{10,11... | collective-permute-start | bytes 1966088 | tf_op jit(solution)/shard_map/ppermute | solution.py:382
  26.1 3.2 %copy-start.17 = (s32[9,64]{1,0:T(8,128)}, s32[9,64]{1,0:T(8,128)S(1)}, u32[]{:S(2)}) copy-start(s32[9,64]{1,0:T(8,128)S(1)} %pad_add_fusion.1.near_ref) | copy-start | bytes 6916
  26.1 3.2 %collective-permute-start = (s32[9,64]{1,0:T(8,128)S(1)}, s32[9,64]{1,0:T(8,128)S(1)}, u32[]{:S(2)}, u32[]{:S(2)}) collective-permute-start(s32[9,64]{1,0:T(8,128)S(1)} %pad_add_fusion.1.near_ref), channel_id=1, source_target_pairs={{0,1},{1,0},{2,3},{3,2},{4,5},{5,4},{6,7},{7,6},{8,9},{9,8},{10,11... | collective-permute-start | bytes 6920 | tf_op jit(solution)/shard_map/ppermute | solution.py:382
  26.7 2.5 %collective-permute-start.5 = (s32[4,4,8]{2,1,0:T(4,128)S(1)}, s32[4,4,8]{2,1,0:T(4,128)S(1)}, u32[]{:S(2)}, u32[]{:S(2)}) collective-permute-start(s32[4,4,8]{2,1,0:T(4,128)S(1)} %get-tuple-element.56), channel_id=1, source_target_pairs={{0,1},{1,0},{2,3},{3,2},{4,5},{5,4},{6,7},{7,6},{8,9},{9,8},{10,11... | collective-permute-start | bytes 1544 | tf_op jit(solution)/shard_map/ppermute | solution.py:382
  38.2 2.0 %copy-start.4 = (bf16[32,128,128]{2,1,0:T(8,128)(2,1)S(1)}, bf16[32,128,128]{2,1,0:T(8,128)(2,1)}, u32[]{:S(2)}) copy-start(bf16[32,128,128]{2,1,0:T(8,128)(2,1)} %copy-done.3) | copy-start | bytes 3145732
  38.2 2.0 %copy-start.11 = (s32[1088]{0:T(1024)S(1)}, s32[1088]{0:T(1024)}, u32[]{:S(2)}) copy-start(s32[1088]{0:T(1024)} %get-tuple-element.29.refs_0_) | copy-start | bytes 13060
  40.2 22.6 %copy-start.10 = (s32[1088]{0:T(1024)S(1)}, s32[1088]{0:T(1024)}, u32[]{:S(2)}) copy-start(s32[1088]{0:T(1024)} %get-tuple-element.22.refs_0_) | copy-start | bytes 13060
  48.9 4.9 %collective-permute-start.6 = (f32[32,128]{1,0:T(8,128)S(1)}, f32[32,128]{1,0:T(8,128)S(1)}, u32[]{:S(2)}, u32[]{:S(2)}) collective-permute-start(f32[32,128]{1,0:T(8,128)S(1)} %get-tuple-element.34), channel_id=1, source_target_pairs={{0,2},{1,3},{2,4},{3,5},{4,6},{5,7},{6,0},{7,1},{8,10},{9,11},{10,... | collective-permute-start | bytes 49160 | tf_op jit(solution)/shard_map/ppermute | solution.py:382
  48.9 5.2 %collective-permute-start.7 = (f32[32,128]{1,0:T(8,128)S(1)}, f32[32,128]{1,0:T(8,128)S(1)}, u32[]{:S(2)}, u32[]{:S(2)}) collective-permute-start(f32[32,128]{1,0:T(8,128)S(1)} %get-tuple-element.34), channel_id=1, source_target_pairs={{0,4},{1,5},{2,6},{3,7},{4,0},{5,1},{6,2},{7,3},{8,12},{9,13},{10,... | collective-permute-start | bytes 49160 | tf_op jit(solution)/shard_map/ppermute | solution.py:382
  51.5 3.7 %collective-permute-start.8 = (f32[32,128]{1,0:T(8,128)S(1)}, f32[32,128]{1,0:T(8,128)S(1)}, u32[]{:S(2)}, u32[]{:S(2)}) collective-permute-start(f32[32,128]{1,0:T(8,128)S(1)} %get-tuple-element.34), channel_id=1, source_target_pairs={{0,6},{1,7},{2,0},{3,1},{4,2},{5,3},{6,4},{7,5},{8,14},{9,15},{10,... | collective-permute-start | bytes 49160 | tf_op jit(solution)/shard_map/ppermute | solution.py:382
  55.3 5.3 %collective-permute-start.10 = (f32[32,128]{1,0:T(8,128)S(1)}, f32[32,128]{1,0:T(8,128)S(1)}, u32[]{:S(2)}, u32[]{:S(2)}) collective-permute-start(f32[32,128]{1,0:T(8,128)S(1)} %multiply_add_fusion.5.refs_4_), channel_id=1, source_target_pairs={{0,16},{1,17},{2,18},{3,19},{4,20},{5,21},{6,22},{7,23},{8,24},{9,... | collective-permute-start | bytes 49160 | tf_op jit(solution)/shard_map/ppermute | solution.py:382
  57.3 3.7 %collective-permute-start.11 = (f32[32,128]{1,0:T(8,128)S(1)}, f32[32,128]{1,0:T(8,128)S(1)}, u32[]{:S(2)}, u32[]{:S(2)}) collective-permute-start(f32[32,128]{1,0:T(8,128)S(1)} %multiply_add_fusion.5.refs_4_), channel_id=1, source_target_pairs={{0,24},{1,25},{2,26},{3,27},{4,28},{5,29},{6,30},{7,31},{8,0},{9,1... | collective-permute-start | bytes 49160 | tf_op jit(solution)/shard_map/ppermute | solution.py:382
  57.8 4.9 %collective-permute-start.9 = (f32[32,128]{1,0:T(8,128)S(1)}, f32[32,128]{1,0:T(8,128)S(1)}, u32[]{:S(2)}, u32[]{:S(2)}) collective-permute-start(f32[32,128]{1,0:T(8,128)S(1)} %multiply_add_fusion.5.refs_4_), channel_id=1, source_target_pairs={{0,8},{1,9},{2,10},{3,11},{4,12},{5,13},{6,14},{7,15},{8,16},{9,17... | collective-permute-start | bytes 49160 | tf_op jit(solution)/shard_map/ppermute | solution.py:382
  71.1 1.3 collective-permute-start.12
  72.4 5.2 %collective-permute-start.13 = (f32[64,128]{1,0:T(8,128)S(1)}, f32[64,128]{1,0:T(8,128)S(1)}, u32[]{:S(2)}, u32[]{:S(2)}) collective-permute-start(f32[64,128]{1,0:T(8,128)S(1)} %multiply_add_fusion.1.refs_5_), channel_id=1, source_target_pairs={{0,32},{32,64},{64,96},{96,0},{1,33},{33,65},{65,97},{97,1},{2,34}... | collective-permute-start | bytes 98312 | tf_op jit(solution)/shard_map/ppermute | solution.py:382
  72.5 5.5 %collective-permute-start.14 = (f32[64,128]{1,0:T(8,128)S(1)}, f32[64,128]{1,0:T(8,128)S(1)}, u32[]{:S(2)}, u32[]{:S(2)}) collective-permute-start(f32[64,128]{1,0:T(8,128)S(1)} %multiply_add_fusion.1.refs_5_), channel_id=1, source_target_pairs={{0,64},{32,96},{64,0},{96,32},{1,65},{33,97},{65,1},{97,33},{2,66}... | collective-permute-start | bytes 98312 | tf_op jit(solution)/shard_map/ppermute | solution.py:382
  73.7 5.2 %collective-permute-start.15 = (f32[64,128]{1,0:T(8,128)S(1)}, f32[64,128]{1,0:T(8,128)S(1)}, u32[]{:S(2)}, u32[]{:S(2)}) collective-permute-start(f32[64,128]{1,0:T(8,128)S(1)} %multiply_add_fusion.1.refs_5_), channel_id=1, source_target_pairs={{0,96},{32,0},{64,32},{96,64},{1,97},{33,1},{65,33},{97,65},{2,98}... | collective-permute-start | bytes 98312 | tf_op jit(solution)/shard_map/ppermute | solution.py:382
  89.2 20.6 %copy-start.8 = (bf16[4096,64]{0,1:T(8,128)(2,1)S(1)}, bf16[4096,64]{0,1:T(8,128)(2,1)}, u32[]{:S(2)}) copy-start(bf16[4096,64]{0,1:T(8,128)(2,1)} %param.10) | copy-start | bytes 1572868
  89.2 5.0 %collective-permute-start.16 = (f32[32,128]{1,0:T(8,128)S(1)}, f32[32,128]{1,0:T(8,128)S(1)}, u32[]{:S(2)}, u32[]{:S(2)}) collective-permute-start(f32[32,128]{1,0:T(8,128)S(1)} %get-tuple-element.36), channel_id=1, source_target_pairs={{0,2},{1,3},{2,4},{3,5},{4,6},{5,7},{6,0},{7,1},{8,10},{9,11},{10,... | collective-permute-start | bytes 49160 | tf_op jit(solution)/shard_map/ppermute | solution.py:382
  89.3 5.5 %collective-permute-start.17 = (f32[32,128]{1,0:T(8,128)S(1)}, f32[32,128]{1,0:T(8,128)S(1)}, u32[]{:S(2)}, u32[]{:S(2)}) collective-permute-start(f32[32,128]{1,0:T(8,128)S(1)} %get-tuple-element.36), channel_id=1, source_target_pairs={{0,4},{1,5},{2,6},{3,7},{4,0},{5,1},{6,2},{7,3},{8,12},{9,13},{10,... | collective-permute-start | bytes 49160 | tf_op jit(solution)/shard_map/ppermute | solution.py:382
  91.4 3.9 %collective-permute-start.18 = (f32[32,128]{1,0:T(8,128)S(1)}, f32[32,128]{1,0:T(8,128)S(1)}, u32[]{:S(2)}, u32[]{:S(2)}) collective-permute-start(f32[32,128]{1,0:T(8,128)S(1)} %get-tuple-element.36), channel_id=1, source_target_pairs={{0,6},{1,7},{2,0},{3,1},{4,2},{5,3},{6,4},{7,5},{8,14},{9,15},{10,... | collective-permute-start | bytes 49160 | tf_op jit(solution)/shard_map/ppermute | solution.py:382
  95.3 5.0 %collective-permute-start.19 = (f32[32,128]{1,0:T(8,128)S(1)}, f32[32,128]{1,0:T(8,128)S(1)}, u32[]{:S(2)}, u32[]{:S(2)}) collective-permute-start(f32[32,128]{1,0:T(8,128)S(1)} %multiply_add_fusion.4.refs_4_), channel_id=1, source_target_pairs={{0,8},{1,9},{2,10},{3,11},{4,12},{5,13},{6,14},{7,15},{8,16},{9,17... | collective-permute-start | bytes 49160 | tf_op jit(solution)/shard_map/ppermute | solution.py:382
  95.4 5.3 %collective-permute-start.20 = (f32[32,128]{1,0:T(8,128)S(1)}, f32[32,128]{1,0:T(8,128)S(1)}, u32[]{:S(2)}, u32[]{:S(2)}) collective-permute-start(f32[32,128]{1,0:T(8,128)S(1)} %multiply_add_fusion.4.refs_4_), channel_id=1, source_target_pairs={{0,16},{1,17},{2,18},{3,19},{4,20},{5,21},{6,22},{7,23},{8,24},{9,... | collective-permute-start | bytes 49160 | tf_op jit(solution)/shard_map/ppermute | solution.py:382
  95.5 5.9 %collective-permute-start.21 = (f32[32,128]{1,0:T(8,128)S(1)}, f32[32,128]{1,0:T(8,128)S(1)}, u32[]{:S(2)}, u32[]{:S(2)}) collective-permute-start(f32[32,128]{1,0:T(8,128)S(1)} %multiply_add_fusion.4.refs_4_), channel_id=1, source_target_pairs={{0,24},{1,25},{2,26},{3,27},{4,28},{5,29},{6,30},{7,31},{8,0},{9,1... | collective-permute-start | bytes 49160 | tf_op jit(solution)/shard_map/ppermute | solution.py:382
  109.7 1.3 collective-permute-start.22
  111.0 5.2 %collective-permute-start.23 = (f32[64,128]{1,0:T(8,128)S(1)}, f32[64,128]{1,0:T(8,128)S(1)}, u32[]{:S(2)}, u32[]{:S(2)}) collective-permute-start(f32[64,128]{1,0:T(8,128)S(1)} %multiply_add_fusion.refs_5_), channel_id=1, source_target_pairs={{0,32},{32,64},{64,96},{96,0},{1,33},{33,65},{65,97},{97,1},{2,34}... | collective-permute-start | bytes 98312 | tf_op jit(solution)/shard_map/ppermute | solution.py:382
  111.1 5.5 %collective-permute-start.24 = (f32[64,128]{1,0:T(8,128)S(1)}, f32[64,128]{1,0:T(8,128)S(1)}, u32[]{:S(2)}, u32[]{:S(2)}) collective-permute-start(f32[64,128]{1,0:T(8,128)S(1)} %multiply_add_fusion.refs_5_), channel_id=1, source_target_pairs={{0,64},{32,96},{64,0},{96,32},{1,65},{33,97},{65,1},{97,33},{2,66}... | collective-permute-start | bytes 98312 | tf_op jit(solution)/shard_map/ppermute | solution.py:382
  111.2 6.2 %collective-permute-start.25 = (f32[64,128]{1,0:T(8,128)S(1)}, f32[64,128]{1,0:T(8,128)S(1)}, u32[]{:S(2)}, u32[]{:S(2)}) collective-permute-start(f32[64,128]{1,0:T(8,128)S(1)} %multiply_add_fusion.refs_5_), channel_id=1, source_target_pairs={{0,96},{32,0},{64,32},{96,64},{1,97},{33,1},{65,33},{97,65},{2,98}... | collective-permute-start | bytes 98312 | tf_op jit(solution)/shard_map/ppermute | solution.py:382
  127.8 27.1 %copy-start.13 = (f32[4096]{0:T(1024)S(1)}, f32[4096]{0:T(1024)}, u32[]{:S(2)}) copy-start(f32[4096]{0:T(1024)} %param.11) | copy-start | bytes 49156
  127.8 5.0 %collective-permute-start.26 = (f32[32,128]{1,0:T(8,128)S(1)}, f32[32,128]{1,0:T(8,128)S(1)}, u32[]{:S(2)}, u32[]{:S(2)}) collective-permute-start(f32[32,128]{1,0:T(8,128)S(1)} %get-tuple-element.38), channel_id=1, source_target_pairs={{0,2},{1,3},{2,4},{3,5},{4,6},{5,7},{6,0},{7,1},{8,10},{9,11},{10,... | collective-permute-start | bytes 49160 | tf_op jit(solution)/shard_map/ppermute | solution.py:382
  127.9 5.3 %collective-permute-start.27 = (f32[32,128]{1,0:T(8,128)S(1)}, f32[32,128]{1,0:T(8,128)S(1)}, u32[]{:S(2)}, u32[]{:S(2)}) collective-permute-start(f32[32,128]{1,0:T(8,128)S(1)} %get-tuple-element.38), channel_id=1, source_target_pairs={{0,4},{1,5},{2,6},{3,7},{4,0},{5,1},{6,2},{7,3},{8,12},{9,13},{10,... | collective-permute-start | bytes 49160 | tf_op jit(solution)/shard_map/ppermute | solution.py:382
  128.3 5.6 %collective-permute-start.28 = (f32[32,128]{1,0:T(8,128)S(1)}, f32[32,128]{1,0:T(8,128)S(1)}, u32[]{:S(2)}, u32[]{:S(2)}) collective-permute-start(f32[32,128]{1,0:T(8,128)S(1)} %get-tuple-element.38), channel_id=1, source_target_pairs={{0,6},{1,7},{2,0},{3,1},{4,2},{5,3},{6,4},{7,5},{8,14},{9,15},{10,... | collective-permute-start | bytes 49160 | tf_op jit(solution)/shard_map/ppermute | solution.py:382
  133.9 5.0 %collective-permute-start.29 = (f32[32,128]{1,0:T(8,128)S(1)}, f32[32,128]{1,0:T(8,128)S(1)}, u32[]{:S(2)}, u32[]{:S(2)}) collective-permute-start(f32[32,128]{1,0:T(8,128)S(1)} %multiply_add_fusion.3.refs_4_), channel_id=1, source_target_pairs={{0,8},{1,9},{2,10},{3,11},{4,12},{5,13},{6,14},{7,15},{8,16},{9,17... | collective-permute-start | bytes 49160 | tf_op jit(solution)/shard_map/ppermute | solution.py:382
  134.0 5.3 %collective-permute-start.30 = (f32[32,128]{1,0:T(8,128)S(1)}, f32[32,128]{1,0:T(8,128)S(1)}, u32[]{:S(2)}, u32[]{:S(2)}) collective-permute-start(f32[32,128]{1,0:T(8,128)S(1)} %multiply_add_fusion.3.refs_4_), channel_id=1, source_target_pairs={{0,16},{1,17},{2,18},{3,19},{4,20},{5,21},{6,22},{7,23},{8,24},{9,... | collective-permute-start | bytes 49160 | tf_op jit(solution)/shard_map/ppermute | solution.py:382
  134.3 5.6 %collective-permute-start.31 = (f32[32,128]{1,0:T(8,128)S(1)}, f32[32,128]{1,0:T(8,128)S(1)}, u32[]{:S(2)}, u32[]{:S(2)}) collective-permute-start(f32[32,128]{1,0:T(8,128)S(1)} %multiply_add_fusion.3.refs_4_), channel_id=1, source_target_pairs={{0,24},{1,25},{2,26},{3,27},{4,28},{5,29},{6,30},{7,31},{8,0},{9,1... | collective-permute-start | bytes 49160 | tf_op jit(solution)/shard_map/ppermute | solution.py:382
  147.7 1.3 collective-permute-start.33
  147.8 4.6 %collective-permute-start.32 = (f32[32,128]{1,0:T(8,128)S(1)}, f32[32,128]{1,0:T(8,128)S(1)}, u32[]{:S(2)}, u32[]{:S(2)}) collective-permute-start(f32[32,128]{1,0:T(8,128)S(1)} %multiply_add_fusion.2), channel_id=1, source_target_pairs={{0,1},{1,0},{2,3},{3,2},{4,5},{5,4},{6,7},{7,6},{8,9},{9,8},{10,11... | collective-permute-start | bytes 49160 | tf_op jit(solution)/shard_map/ppermute | solution.py:382
  149.0 4.9 %collective-permute-start.34 = (f32[8,128]{1,0:T(8,128)S(1)}, f32[8,128]{1,0:T(8,128)S(1)}, u32[]{:S(2)}, u32[]{:S(2)}) collective-permute-start(f32[8,128]{1,0:T(8,128)S(1)} %get-tuple-element.51), channel_id=1, source_target_pairs={{0,32},{32,64},{64,96},{96,0},{1,33},{33,65},{65,97},{97,1},{2,34}... | collective-permute-start | bytes 12296 | tf_op jit(solution)/shard_map/ppermute | solution.py:456
  149.1 5.2 %collective-permute-start.35 = (f32[8,128]{1,0:T(8,128)S(1)}, f32[8,128]{1,0:T(8,128)S(1)}, u32[]{:S(2)}, u32[]{:S(2)}) collective-permute-start(f32[8,128]{1,0:T(8,128)S(1)} %get-tuple-element.50), channel_id=1, source_target_pairs={{0,64},{32,96},{64,0},{96,32},{1,65},{33,97},{65,1},{97,33},{2,66}... | collective-permute-start | bytes 12296 | tf_op jit(solution)/shard_map/ppermute | solution.py:456
  149.2 5.6 %collective-permute-start.36 = (f32[8,128]{1,0:T(8,128)S(1)}, f32[8,128]{1,0:T(8,128)S(1)}, u32[]{:S(2)}, u32[]{:S(2)}) collective-permute-start(f32[8,128]{1,0:T(8,128)S(1)} %get-tuple-element.49), channel_id=1, source_target_pairs={{0,96},{32,0},{64,32},{96,64},{1,97},{33,1},{65,33},{97,65},{2,98}... | collective-permute-start | bytes 12296 | tf_op jit(solution)/shard_map/ppermute | solution.py:456
  (11 other events, 11.7 us)

commit v2 on v1

--- a/solution.py
+++ b/solution.py
@@ -16,9 +16,11 @@
 LOG2E = 1.4426950408889634
 SCALE = LOG2E / EPSILON
 PAIRS = 32
+TAIL = 16
 COPIES = 2
 GROUP = 32
 EXTRA = 16
+LEFT, RIGHT = 0, 1
 HEAD = 8
 STRIDE = 64
 
@@ -26,7 +28,9 @@
 SMEM = pl.BlockSpec(memory_space=pltpu.SMEM)
 VMEM = pl.BlockSpec(memory_space=pltpu.VMEM)
 HBM = pl.BlockSpec(memory_space=pltpu.HBM)
-PARAMS = pltpu.CompilerParams(vmem_limit_bytes=48 * 1024 * 1024)
+MIB = 1024 * 1024
+PREPARE = pltpu.CompilerParams(vmem_limit_bytes=64 * MIB)
+PASS = pltpu.CompilerParams(vmem_limit_bytes=53 * MIB)
 
 
 def shape(dims, dtype=jnp.float32):
@@ -74,7 +78,9 @@
         return position + (tiles + 1) // 2
 
     def finish(ref, right, pairs, none):
-        ref[0] = (pairs + PAIRS - 1) // PAIRS
+        tails = (pairs + TAIL - 1) // TAIL
+        ref[0] = tails // (PAIRS // TAIL)
+        ref[1] = tails % (PAIRS // TAIL)
 
         def pad(k, carry):
             ref[HEAD + pairs + k] = 0
@@ -82,7 +88,7 @@
             ref[right + 2 * (pairs + k) + 1] = none
             return carry
 
-        lax.fori_loop(0, ref[0] * PAIRS - pairs, pad, 0)
+        lax.fori_loop(0, tails * TAIL - pairs, pad, 0)
 
     finish(col_ref, col_right, lax.fori_loop(0, halves, one_block, jnp.int32(0)), slots)
 
@@ -174,18 +180,18 @@
             pltpu.VMEM(logmass.shape, logmass.dtype),
             pltpu.SemaphoreType.DMA((3,)),
         ],
-        compiler_params=PARAMS,
+        compiler_params=PREPARE,
     )(place.reshape(1), *ids, points, potential, logmass)
 
 
 def unpack_kernel(group, in_ref, *refs):
-    outs, (right, left, start, mass, sems) = refs[-9:-5], refs[-5:]
+    outs, (blocks, start, mass, sems) = refs[-7:-4], refs[-4:]
 
     def one_block(q, carry):
         block = in_ref[q, :D, :]
         both = jnp.concatenate([block, block], axis=0)
-        right[q] = both
-        left[q] = both.T
+        blocks[RIGHT, q] = both
+        blocks[LEFT, q] = both.T
         rows = in_ref[q, D:, :].astype(jnp.float32)
         start[pl.ds(q, 1), :] = rows[0:1] + rows[1:2] + rows[2:3]
         mass[pl.ds(q, 1), :] = rows[3:4] + rows[4:5] + rows[5:6]
@@ -193,27 +199,31 @@
 
     lax.fori_loop(0, GROUP, one_block, 0, unroll=8)
     own = pl.ds(group * GROUP, GROUP)
-    pairs = [(value, out.at[own]) for value, out in zip((right, left, start, mass), outs)]
+    pairs = [(blocks, outs[0].at[:, own]), (start, outs[1].at[own]), (mass, outs[2].at[own])]
     for copy in start_copies(pairs, sems):
         copy.wait()
 
 
 def unpack(group, fetched, before):
-    parts = [((BLOCK, BLOCK), jnp.bfloat16)] * 2 + [((BLOCK,), jnp.float32)] * 2
     return pl.pallas_call(
         functools.partial(unpack_kernel, group),
-        out_shape=[shape((2 * GROUP, *dims), dtype) for dims, dtype in parts],
+        out_shape=[shape((2, 2 * GROUP, BLOCK, BLOCK), jnp.bfloat16)]
+        + [shape((2 * GROUP, BLOCK))] * 2,
         in_specs=[VMEM] + [HBM] * len(before),
-        out_specs=[HBM] * 4,
-        scratch_shapes=[pltpu.VMEM((GROUP, *dims), dtype) for dims, dtype in parts]
-        + [pltpu.SemaphoreType.DMA((4,))],
+        out_specs=[HBM] * 3,
+        scratch_shapes=[
+            pltpu.VMEM((2, GROUP, BLOCK, BLOCK), jnp.bfloat16),
+            pltpu.VMEM((GROUP, BLOCK), jnp.float32),
+            pltpu.VMEM((GROUP, BLOCK), jnp.float32),
+            pltpu.SemaphoreType.DMA((3,)),
+        ],
         input_output_aliases={1 + k: k for k in range(len(before))},
-        compiler_params=PARAMS,
+        compiler_params=PREPARE,
     )(fetched, *before)
 
 
-def source_kernel(half_ref, points_hbm, right_hbm, left_hbm, norm_ref, points, right, left, sems):
-    halves = right.shape[0]
+def source_kernel(half_ref, points_hbm, blocks_hbm, norm_ref, points, blocks, sems):
+    halves = blocks.shape[1]
     at = pl.multiple_of(half_ref[0] * (halves * BLOCK), halves * BLOCK)
     copy = pltpu.make_async_copy(points_hbm.at[:, pl.ds(at, halves * BLOCK)], points, sems.at[0])
     copy.start()
@@ -226,29 +236,29 @@
         high = scaled.astype(jnp.bfloat16)
         low = (scaled - high.astype(jnp.float32)).astype(jnp.bfloat16)
         both = jnp.concatenate([high, low], axis=0)
-        right[b] = both
-        left[b] = both.T
+        blocks[RIGHT, b] = both
+        blocks[LEFT, b] = both.T
         return carry
 
     lax.fori_loop(0, halves, one_block, 0, unroll=4)
-    for copy in start_copies([(right, right_hbm), (left, left_hbm)], sems):
-        copy.wait()
+    copy = pltpu.make_async_copy(blocks, blocks_hbm, sems.at[1])
+    copy.start()
+    copy.wait()
 
 
 def source(half, halves, points):
-    blocks = (halves, BLOCK, BLOCK)
+    blocks = (2, halves, BLOCK, BLOCK)
     return pl.pallas_call(
         source_kernel,
-        out_shape=[shape(blocks, jnp.bfloat16), shape(blocks, jnp.bfloat16), shape((halves, BLOCK))],
+        out_shape=[shape(blocks, jnp.bfloat16), shape((halves, BLOCK))],
         in_specs=[SMEM, HBM],
-        out_specs=[HBM, HBM, VMEM],
+        out_specs=[HBM, VMEM],
         scratch_shapes=[
             pltpu.VMEM((D, halves * BLOCK), jnp.bfloat16),
             pltpu.VMEM(blocks, jnp.bfloat16),
-            pltpu.VMEM(blocks, jnp.bfloat16),
             pltpu.SemaphoreType.DMA((2,)),
         ],
-        compiler_params=PARAMS,
+        compiler_params=PREPARE,
     )(half.reshape(1), points)
 
 
@@ -256,8 +266,8 @@
     return start_ref[...]
 
 
-def field_bias(mass_ref, *parts):
-    return mass_ref[...] - log_sum([ref[...] for ref in parts])
+def field_bias(mass_ref, parts_ref):
+    return mass_ref[...] - log_sum([parts_ref[k] for k in range(parts_ref.shape[0])])
 
 
 def potential_bias(mass_ref, chosen_ref, *refs):
@@ -281,8 +291,9 @@
     bias_parts, refs = refs[:parts_count], refs[parts_count:]
     out_ref, bias_ref, columns, peaks, masses, sems = refs[:6]
     locals_ = refs[6:]
-    copies = start_copies(list(zip(remotes, locals_))[::-1], sems)
     list_ref, left_ref, right_ref, *fixed = locals_
+    sources = [remotes[0], remotes[1].at[LEFT], remotes[2].at[RIGHT], *remotes[3:]]
+    copies = start_copies(list(zip(sources, locals_))[::-1], sems)
     lefts, rights = left_ref.shape[0], right_ref.shape[0]
     square = (BLOCK, BLOCK)
     lane = lax.broadcasted_iota(jnp.int32, square, 1)
@@ -321,9 +332,9 @@
     def right_block(r):
         return right_ref[jnp.minimum(r, rights - 1)]
 
-    def step(t, carry):
-        for u in range(PAIRS):
-            i = t * PAIRS + u
+    def step(start, count, t, carry):
+        for u in range(count):
+            i = start + t * count + u
             l = list_ref[HEAD + i]
             first, second = list_ref[rights_at + 2 * i], list_ref[rights_at + 2 * i + 1]
             left = jnp.concatenate([left_ref[l], columns[l]], axis=1)
@@ -335,7 +346,8 @@
             fold((2 * u + 1) % COPIES, second, scores[:, BLOCK:])
         return carry
 
-    lax.fori_loop(0, list_ref[0], step, 0)
+    lax.fori_loop(0, list_ref[0], functools.partial(step, 0, PAIRS), 0)
+    lax.fori_loop(0, list_ref[1], functools.partial(step, list_ref[0] * PAIRS, TAIL), 0)
 
     def finish(octet, carry):
         rows = []
@@ -345,18 +357,20 @@
             top = jnp.max(functools.reduce(jnp.maximum, tops), axis=0, keepdims=True)
             mass = sum(masses[copy, r] * jnp.exp2(tops[copy] - top) for copy in range(COPIES))
             rows.append(top + jnp.log2(jnp.sum(mass, axis=0, keepdims=True)))
-        out_ref[pl.ds(pl.multiple_of(octet * 8, 8), 8), :] = jnp.concatenate(rows, axis=0)
+        out_ref[0, pl.ds(pl.multiple_of(octet * 8, 8), 8), :] = jnp.concatenate(rows, axis=0)
         return carry
 
     lax.fori_loop(0, rights // 8, finish, 0)
-
-
-def log_sums(pairs, left, right, bias_of, fixed, parts):
-    lefts, rights = left.shape[0], right.shape[0]
+    for k in range(1, out_ref.shape[0]):
+        out_ref[k] = out_ref[0]
+
+
+def log_sums(pairs, left, right, bias_of, fixed, parts, copies):
+    lefts, rights = left.shape[1], right.shape[1]
     remotes = [pairs, left, right, *fixed]
     return pl.pallas_call(
         functools.partial(pass_kernel, bias_of, len(fixed), len(parts)),
-        out_shape=[shape((rights, BLOCK)), shape((lefts, BLOCK))],
+        out_shape=[shape((copies, rights, BLOCK)), shape((lefts, BLOCK))],
         in_specs=[HBM] * len(remotes) + [VMEM] * len(parts),
         out_specs=[VMEM, VMEM],
         scratch_shapes=[
@@ -365,9 +379,11 @@
             pltpu.VMEM((COPIES, rights + 1, 8, BLOCK), jnp.float32),
             pltpu.SemaphoreType.DMA((len(remotes),)),
             pltpu.SMEM(pairs.shape, pairs.dtype),
+            pltpu.VMEM(left.shape[1:], left.dtype),
+            pltpu.VMEM(right.shape[1:], right.dtype),
         ]
-        + [pltpu.VMEM(value.shape, value.dtype) for value in remotes[1:]],
-        compiler_params=PARAMS,
+        + [pltpu.VMEM(value.shape, value.dtype) for value in fixed],
+        compiler_params=PASS,
     )(*remotes, *parts)
 
 
@@ -417,8 +433,9 @@
     ids = jnp.stack(ids)
     col_pairs, row_pairs = plan(half, tiles, swap(tiles))
     fetched = lax.all_to_all(packed, "src", split_axis=0, concat_axis=0, tiled=True)
-    points_right, points_left, source_half = source(half, halves, source_points.T)
-    targets_right, targets_left, potentials, slot_mass = unpack(1, swap(fetched), unpack(0, fetched, []))
+    points, source_half = source(half, halves, source_points.T)
+    fetched, points, col_pairs, row_pairs = lax.optimization_barrier((fetched, points, col_pairs, row_pairs))
+    targets, potentials, slot_mass = unpack(1, swap(fetched), unpack(0, fetched, []))
     source_mass = LOG2E * lax.dynamic_slice(
         source_logmass.reshape(blocks, BLOCK), (half * halves, 0), (halves, BLOCK)
     )
@@ -429,16 +446,19 @@
     same = same.reshape(2, peers, count, 1, count) & jnp.eye(peers, dtype=bool)[:, None, :, None]
     chosen = same.reshape(2, peers * count, peers * count).astype(jnp.bfloat16)
 
+    groups = lax.axis_size("grp")
+    same_core = [list(range(core, groups, 2)) for core in range(2)]
     for sweep_index in range(ITERS):
         if sweep_index == 0:
-            rows, _ = log_sums(row_pairs, targets_left, points_right, start_bias, [potentials], [])
+            bias_of, fixed, parts = start_bias, [potentials], []
         else:
-            rows, _ = log_sums(
-                row_pairs, targets_left, points_right, potential_bias, [slot_mass, chosen], col_parts
-            )
-        rows = log_sum(ring(rows, "grp", 4, 2))
-        row_parts = ring(rows, "grp", 4, 8)
-        cols, field = log_sums(col_pairs, points_left, targets_right, field_bias, [source_mass], row_parts)
+            bias_of, fixed, parts = potential_bias, [slot_mass, chosen], col_parts
+        rows, _ = log_sums(row_pairs, targets, points, bias_of, fixed, parts, groups // 2)
+        rows = lax.all_to_all(
+            rows, "grp", split_axis=0, concat_axis=0, tiled=True, axis_index_groups=same_core
+        )
+        cols, field = log_sums(col_pairs, points, targets, field_bias, [source_mass], [rows], 1)
+        cols = cols[0]
         if sweep_index < ITERS - 1:
             other = swap(cols)
             cols = log_sum([cols, jnp.concatenate([other[count:], other[:count]], axis=0)])

time: 155 us -> 147 us (0.948); the launches traced: 156 us -> 146 us
  Pallas kernels: 59 us -> 47.1 us
  local copies, waits for them, and re-layouts: 12.9 us -> 5.14 us
  other arithmetic: 2.24 us -> 6.05 us
  blocking collectives: 13 us -> 15.5 us
  starting transfers between devices: 38.1 us -> 40.5 us
    all_to_all x0 -> x3, starting transfers between devices: none -> 20.1 us  [the longest x2 15.9 us: shards(): lax.all_to_all(rows, 'grp', split_axis=0, concat_axis=0, tiled=True, axis...]
    pallas_call x6, Pallas kernels: 46.7 us -> 28 us  [log_sums(): pl.pallas_call(functools.partial(pass_kernel, bias_of, len(fixed), len(pa...]
    ppermute x34 -> x16, waiting for transfers between devices: 27.6 us -> 10.2 us  [ring(): out.append(lax.ppermute(values, axis, pairs))]
    ppermute x34 -> x16, starting transfers between devices: 34.8 us -> 17.8 us  [ring(): out.append(lax.ppermute(values, axis, pairs))]
    all_to_all x0 -> x3, waiting for transfers between devices: none -> 16.9 us  [the longest x2 16.8 us: shards(): lax.all_to_all(rows, 'grp', split_axis=0, concat_axis=0, tiled=True, axis...]
    unnamed x44 -> x34, local copies, waits for them, and re-layouts: 11.8 us -> 2.11 us
    pallas_call x1, Pallas kernels: 0.95 us -> 3.79 us  [source(): pl.pallas_call(source_kernel, out_shape=[shape(blocks, jnp.bfloat16), sha...]
    all_to_all x1, blocking collectives: 13 us -> 15.5 us  [shards(): lax.all_to_all(rows, 'grp', split_axis=0, concat_axis=0, tiled=True, axis...]
  transfers between devices with their start and end apart: 37 -> 22, of which waited for: 32 -> 14; matrix products, arithmetic and copies ran while one was open for 2% -> 6% of each run, Pallas kernels for 6% -> 9%
where the time goes in v2:
time: 147 us; the launch traced here: 146 us
  Pallas kernels  47.1 us (32%)
  starting transfers between devices  40.5 us (28%)
  waiting for transfers between devices  30.1 us (20%)
  blocking collectives  15.5 us (11%)
  other arithmetic  6.05 us (4%)
  local copies, waits for them, and re-layouts  5.14 us (3%)
    pallas_call x6, Pallas kernels, log_sums(): pl.pallas_call(functools.partial(pass_kernel, bias_of, len(fixed), len(pa...  28 us
    ppermute x16, starting transfers between devices, ring(): out.append(lax.ppermute(values, axis, pairs))  17.8 us
    all_to_all x2, waiting for transfers between devices, shards(): lax.all_to_all(rows, 'grp', split_axis=0, concat_axis=0, tiled=True, axis...  16.8 us
    all_to_all x2, starting transfers between devices, shards(): lax.all_to_all(rows, 'grp', split_axis=0, concat_axis=0, tiled=True, axis...  15.9 us
    all_to_all x1, blocking collectives, shards(): lax.all_to_all(rows, 'grp', split_axis=0, concat_axis=0, tiled=True, axis...  15.5 us
    ppermute x16, waiting for transfers between devices, ring(): out.append(lax.ppermute(values, axis, pairs))  10.2 us
    pallas_call x1, Pallas kernels, plan(): pl.pallas_call(plan_kernel, out_shape=[shape((HEAD + 3 * room,), jnp.int3...  6.25 us
    pallas_call x2, Pallas kernels, unpack(): pl.pallas_call(functools.partial(unpack_kernel, group), out_shape=[shape(...  6 us
  transfers between devices with their start and end apart: 22, of which 14 were waited for; matrix products, arithmetic and copies ran while one was open for 6% of the time, Pallas kernels for 9%

profile of v2, /device:TPU:0, one launch (start us, length us, event | category | flops | bytes accessed | tf_op | source)
XLA Modules:
  0.0 145.6 jit_solution(15984480928544580793)
XLA Ops:
  0.6 1.6 %collective-permute-start = (s32[4,8]{1,0:T(4,128)}, s32[4,8]{1,0:T(4,128)}, u32[]{:S(2)}, u32[]{:S(2)}) collective-permute-start(s32[4,8]{1,0:T(4,128)} %refs_0_.1), channel_id=1, source_target_pairs={{0,32},{32,64},{64,96},{96,0},{1,33},{33,65},{65,97},{97,1},{2,34}... | collective-permute-start | bytes 392 | tf_op jit(solution)/shard_map/ppermute | solution.py:398
  2.3 2.7 %collective-permute-start.1 = (s32[4,8]{1,0:T(4,128)}, s32[4,8]{1,0:T(4,128)}, u32[]{:S(2)}, u32[]{:S(2)}) collective-permute-start(s32[4,8]{1,0:T(4,128)} %refs_0_.1), channel_id=1, source_target_pairs={{0,64},{32,96},{64,0},{96,32},{1,65},{33,97},{65,1},{97,33},{2,66}... | collective-permute-start | bytes 392 | tf_op jit(solution)/shard_map/ppermute | solution.py:398
  5.0 1.4 collective-permute-start.2
  6.4 1.2 collective-permute-done.1.refs_2_
  7.7 1.2 collective-permute-done.2.refs_3_
  8.9 3.0 %shard_map.95 = bf16[32,80,128]{2,1,0:T(8,128)(2,1)} custom-call(s32[1]{0:T(128)} %bitcast.place_ref, s32[4,8]{1,0:T(4,128)} %refs_0_.1, s32[4,8]{1,0:T(4,128)} %collective-permute-done.refs_1_, s32[4,8]{1,0:T(4,128)} %collective-permute-done.1.refs_2_, s32[4,8]{1,0:T(4,128)} %collective-permute-done.2.refs_3_, bf16[64,4096]{1,0:T(8,128)(2,1)} %bitcast.152, ...), custom_call_target="tpu_custom_call" | custom-call | tf_op jit(solution)/shard_map/pallas_call | solution.py:172
  11.9 4.2 %all-to-all-start = ((bf16[32,80,128]{2,1,0:T(8,128)(2,1)}), bf16[32,80,128]{2,1,0:T(8,128)(2,1)}, u32[]{:S(2)}, u32[]{:S(2)}) async-start(bf16[32,80,128]{2,1,0:T(8,128)(2,1)} %shard_map.95), calls=%async_computation | async-start | bytes 1310720 | tf_op jit(solution)/shard_map/all_to_all | solution.py:435
  16.1 1.3 pad_add_fusion.1.near_ref
  17.4 3.8 %shard_map.96 = (bf16[2,32,128,128]{3,2,1,0:T(8,128)(2,1)}, f32[32,128]{1,0:T(8,128)}) custom-call(s32[1]{0:T(128)} %bitcast.4.half_ref, bf16[64,8192]{1,0:T(8,128)(2,1)} %bitcast.153), custom_call_target="tpu_custom_call" | custom-call | tf_op jit(solution)/shard_map/pallas_call | solution.py:251
  21.2 6.2 %shard_map.97 = (s32[1088]{0:T(1024)}, s32[1088]{0:T(1024)}) custom-call(s32[1]{0:T(128)} %bitcast.4.half_ref, s32[9,64]{1,0:T(8,128)} %pad_add_fusion.1.near_ref, s32[9,64]{1,0:T(8,128)} %collective-permute-done.3.far_ref), custom_call_target="tpu_custom_call" | custom-call | tf_op jit(solution)/shard_map/pallas_call | solution.py:117
  28.1 1.3 dynamic-slice_multiply_fusion.refs_3_
  29.4 0.7 pad_add_fusion.2
  30.3 0.7 and.70
  31.1 0.7 and.76
  31.9 0.6 copy-done.12
  32.5 0.6 pad_add_fusion
  33.1 3.0 %shard_map.98 = (bf16[2,64,128,128]{3,2,1,0:T(8,128)(2,1)}, f32[64,128]{1,0:T(8,128)}, f32[64,128]{1,0:T(8,128)}) custom-call(bf16[32,80,128]{2,1,0:T(8,128)(2,1)} %all-to-all-done.in_ref), custom_call_target="tpu_custom_call" | custom-call | tf_op jit(solution)/shard_map/pallas_call | solution.py:208
  36.1 3.0 %shard_map.99 = (bf16[2,64,128,128]{3,2,1,0:T(8,128)(2,1)}, f32[64,128]{1,0:T(8,128)}, f32[64,128]{1,0:T(8,128)}) custom-call(bf16[32,80,128]{2,1,0:T(8,128)(2,1)} %collective-permute-done.4.in_ref, bf16[2,64,128,128]{3,2,1,0:T(8,128)(2,1)} %get-tuple-element.29.refs_0_, ...), custom_call_target="tpu_custom_call", output_to_operand_aliasing={{0}: (1, {}), {1}: (2, {}), {2}: (3, {})} | custom-call | tf_op jit(solution)/shard_map/pallas_call | solution.py:208
  39.1 0.8 copy-done.2
  39.9 0.7 copy-done.4
  40.6 4.8 %shard_map.100 = (f32[16,32,128]{2,1,0:T(8,128)}, f32[64,128]{1,0:T(8,128)}) custom-call(s32[1088]{0:T(1024)S(1)} %copy-done.4, bf16[2,64,128,128]{3,2,1,0:T(8,128)(2,1)} %get-tuple-element.32.refs_1_.refs_2_, bf16[2,32,128,128]{3,2,1,0:T(8,128)(2,1)} %get-tuple-element.27.refs_2_.refs_1_, f32[64,128]{1,0:T(8,128)S(1)} %copy-done.2), custom_call_target="tpu_custom_call" | custom-call | tf_op jit(solution)/shard_map/pallas_call | solution.py:371
  45.4 8.9 %all-to-all-start.1 = ((f32[16,32,128]{2,1,0:T(8,128)}), f32[16,32,128]{2,1,0:T(8,128)S(1)}, u32[]{:S(2)}, u32[]{:S(2)}) async-start(f32[16,32,128]{2,1,0:T(8,128)} %get-tuple-element.36), calls=%async_computation.1 | async-start | bytes 524288 | tf_op jit(solution)/shard_map/all_to_all | solution.py:457
  54.9 8.2 %all-to-all-done.1.refs_4_ = f32[16,32,128]{2,1,0:T(8,128)S(1)} async-done(((f32[16,32,128]{2,1,0:T(8,128)}), f32[16,32,128]{2,1,0:T(8,128)S(1)}, u32[]{:S(2)}, u32[]{:S(2)}) %all-to-all-start.1) | async-done | bytes 262176 | tf_op jit(solution)/shard_map/all_to_all | solution.py:457
  63.1 4.7 %shard_map.101 = (f32[1,64,128]{2,1,0:T(8,128)S(1)}, f32[32,128]{1,0:T(8,128)}) custom-call(s32[1088]{0:T(1024)S(1)} %copy-done.3, bf16[2,32,128,128]{3,2,1,0:T(8,128)(2,1)} %get-tuple-element.27.refs_2_.refs_1_, bf16[2,64,128,128]{3,2,1,0:T(8,128)(2,1)} %get-tuple-element.32.refs_1_.refs_2_, f32[32,128]{1,0:T(8,128)S(1)} %copy-done.1, ...), custom_call_target="tpu_custom_call" | custom-call | tf_op jit(solution)/shard_map/pallas_call | solution.py:371
  68.3 0.8 collective-permute-done.6
  69.1 1.9 %collective-permute-start.7 = (f32[64,128]{1,0:T(8,128)S(1)}, f32[64,128]{1,0:T(8,128)S(1)}, u32[]{:S(2)}, u32[]{:S(2)}) collective-permute-start(f32[64,128]{1,0:T(8,128)S(1)} %multiply_add_fusion.1.refs_5_), channel_id=1, source_target_pairs={{0,32},{32,64},{64,96},{96,0},{1,33},{33,65},{65,97},{97,1},{2,34}... | collective-permute-start | bytes 98312 | tf_op jit(solution)/shard_map/ppermute | solution.py:398
  71.0 3.0 %collective-permute-start.8 = (f32[64,128]{1,0:T(8,128)S(1)}, f32[64,128]{1,0:T(8,128)S(1)}, u32[]{:S(2)}, u32[]{:S(2)}) collective-permute-start(f32[64,128]{1,0:T(8,128)S(1)} %multiply_add_fusion.1.refs_5_), channel_id=1, source_target_pairs={{0,64},{32,96},{64,0},{96,32},{1,65},{33,97},{65,1},{97,33},{2,66}... | collective-permute-start | bytes 98312 | tf_op jit(solution)/shard_map/ppermute | solution.py:398
  74.0 1.4 collective-permute-start.9
  75.5 0.9 collective-permute-done.8.refs_7_
  76.4 1.5 %collective-permute-done.9.refs_8_ = f32[64,128]{1,0:T(8,128)S(1)} collective-permute-done((f32[64,128]{1,0:T(8,128)S(1)}, f32[64,128]{1,0:T(8,128)S(1)}, u32[]{:S(2)}, u32[]{:S(2)}) %collective-permute-start.9) | collective-permute-done | bytes 32800 | tf_op jit(solution)/shard_map/ppermute | solution.py:398
  78.0 4.7 %shard_map.102 = (f32[16,32,128]{2,1,0:T(8,128)S(1)}, f32[64,128]{1,0:T(8,128)}) custom-call(s32[1088]{0:T(1024)S(1)} %copy-done.5, bf16[2,64,128,128]{3,2,1,0:T(8,128)(2,1)} %get-tuple-element.32.refs_1_.refs_2_, bf16[2,32,128,128]{3,2,1,0:T(8,128)(2,1)} %get-tuple-element.27.refs_2_.refs_1_, f32[64,128]{1,0:T(8,128)S(1)} %copy-done, ...), custom_call_target="tpu_custom_call" | custom-call | tf_op jit(solution)/shard_map/pallas_call | solution.py:371
  82.7 15.5 %all_to_all.20.refs_4_ = f32[16,32,128]{2,1,0:T(8,128)S(1)} all-to-all(f32[16,32,128]{2,1,0:T(8,128)S(1)} %get-tuple-element.38), channel_id=1, replica_groups={{0,2,4,6,8,10,12,14,16,18,20,22,24,26,28,30},{1,3,5,7,9,11,13,15,17,19,..., dimensions={0} | all-to-all | bytes 524288 | tf_op jit(solution)/shard_map/all_to_all | solution.py:457
  98.2 4.9 %shard_map.103 = (f32[1,64,128]{2,1,0:T(8,128)S(1)}, f32[32,128]{1,0:T(8,128)}) custom-call(s32[1088]{0:T(1024)S(1)} %copy-done.3, bf16[2,32,128,128]{3,2,1,0:T(8,128)(2,1)} %get-tuple-element.27.refs_2_.refs_1_, bf16[2,64,128,128]{3,2,1,0:T(8,128)(2,1)} %get-tuple-element.32.refs_1_.refs_2_, f32[32,128]{1,0:T(8,128)S(1)} %copy-done.1, ...), custom_call_target="tpu_custom_call" | custom-call | tf_op jit(solution)/shard_map/pallas_call | solution.py:371
  103.4 1.0 collective-permute-done.10
  104.5 3.7 %collective-permute-start.12 = (f32[64,128]{1,0:T(8,128)S(1)}, f32[64,128]{1,0:T(8,128)S(1)}, u32[]{:S(2)}, u32[]{:S(2)}) collective-permute-start(f32[64,128]{1,0:T(8,128)S(1)} %multiply_add_fusion.refs_5_), channel_id=1, source_target_pairs={{0,64},{32,96},{64,0},{96,32},{1,65},{33,97},{65,1},{97,33},{2,66}... | collective-permute-start | bytes 98312 | tf_op jit(solution)/shard_map/ppermute | solution.py:398
  108.6 0.7 fusion.34
  109.3 0.7 collective-permute-done.11.refs_6_
  110.5 1.7 %collective-permute-done.13.refs_8_ = f32[64,128]{1,0:T(8,128)S(1)} collective-permute-done((f32[64,128]{1,0:T(8,128)S(1)}, f32[64,128]{1,0:T(8,128)S(1)}, u32[]{:S(2)}, u32[]{:S(2)}) %collective-permute-start.13) | collective-permute-done | bytes 32800 | tf_op jit(solution)/shard_map/ppermute | solution.py:398
  112.2 4.8 %shard_map.104 = (f32[16,32,128]{2,1,0:T(8,128)}, f32[64,128]{1,0:T(8,128)}) custom-call(s32[1088]{0:T(1024)S(1)} %copy-done.5, bf16[2,64,128,128]{3,2,1,0:T(8,128)(2,1)} %get-tuple-element.32.refs_1_.refs_2_, bf16[2,32,128,128]{3,2,1,0:T(8,128)(2,1)} %get-tuple-element.27.refs_2_.refs_1_, f32[64,128]{1,0:T(8,128)S(1)} %copy-done, ...), custom_call_target="tpu_custom_call" | custom-call | tf_op jit(solution)/shard_map/pallas_call | solution.py:371
  117.0 6.9 %all-to-all-start.3 = ((f32[16,32,128]{2,1,0:T(8,128)}), f32[16,32,128]{2,1,0:T(8,128)S(1)}, u32[]{:S(2)}, u32[]{:S(2)}) async-start(f32[16,32,128]{2,1,0:T(8,128)} %get-tuple-element.40), calls=%async_computation.3 | async-start | bytes 524288 | tf_op jit(solution)/shard_map/all_to_all | solution.py:457
  124.0 8.7 %all-to-all-done.3.refs_4_ = f32[16,32,128]{2,1,0:T(8,128)S(1)} async-done(((f32[16,32,128]{2,1,0:T(8,128)}), f32[16,32,128]{2,1,0:T(8,128)S(1)}, u32[]{:S(2)}, u32[]{:S(2)}) %all-to-all-start.3) | async-done | bytes 262176 | tf_op jit(solution)/shard_map/all_to_all | solution.py:457
  132.7 4.1 %shard_map.105 = (f32[1,64,128]{2,1,0:T(8,128)S(1)}, f32[32,128]{1,0:T(8,128)S(1)}) custom-call(s32[1088]{0:T(1024)S(1)} %copy-done.3, bf16[2,32,128,128]{3,2,1,0:T(8,128)(2,1)} %get-tuple-element.27.refs_2_.refs_1_, bf16[2,64,128,128]{3,2,1,0:T(8,128)(2,1)} %get-tuple-element.32.refs_1_.refs_2_, f32[32,128]{1,0:T(8,128)S(1)} %copy-done.1, ...), custom_call_target="tpu_custom_call" | custom-call | tf_op jit(solution)/shard_map/pallas_call | solution.py:371
  137.5 0.6 collective-permute-done.15
  138.1 1.5 %collective-permute-start.18 = (f32[8,128]{1,0:T(8,128)S(1)}, f32[8,128]{1,0:T(8,128)S(1)}, u32[]{:S(2)}, u32[]{:S(2)}) collective-permute-start(f32[8,128]{1,0:T(8,128)S(1)} %get-tuple-element.51), channel_id=1, source_target_pairs={{0,96},{32,0},{64,32},{96,64},{1,97},{33,1},{65,33},{97,65},{2,98}... | collective-permute-start | bytes 12296 | tf_op jit(solution)/shard_map/ppermute | solution.py:476
  139.6 1.1 collective-permute-start.16
  140.9 0.6 maximum_bitcast_fusion
  141.9 2.8 %collective-permute-done.17 = f32[8,128]{1,0:T(8,128)S(1)} collective-permute-done((f32[8,128]{1,0:T(8,128)S(1)}, f32[8,128]{1,0:T(8,128)S(1)}, u32[]{:S(2)}, u32[]{:S(2)}) %collective-permute-start.17) | collective-permute-done | bytes 4128 | tf_op jit(solution)/shard_map/ppermute | solution.py:476
  145.0 0.6 fusion.12
  (78 shorter events, 4.6 us)
Async XLA Ops:
  0.6 5.8 %collective-permute-start = (s32[4,8]{1,0:T(4,128)}, s32[4,8]{1,0:T(4,128)}, u32[]{:S(2)}, u32[]{:S(2)}) collective-permute-start(s32[4,8]{1,0:T(4,128)} %refs_0_.1), channel_id=1, source_target_pairs={{0,32},{32,64},{64,96},{96,0},{1,33},{33,65},{65,97},{97,1},{2,34}... | collective-permute-start | bytes 392 | tf_op jit(solution)/shard_map/ppermute | solution.py:398
  2.3 5.4 %collective-permute-start.1 = (s32[4,8]{1,0:T(4,128)}, s32[4,8]{1,0:T(4,128)}, u32[]{:S(2)}, u32[]{:S(2)}) collective-permute-start(s32[4,8]{1,0:T(4,128)} %refs_0_.1), channel_id=1, source_target_pairs={{0,64},{32,96},{64,0},{96,32},{1,65},{33,97},{65,1},{97,33},{2,66}... | collective-permute-start | bytes 392 | tf_op jit(solution)/shard_map/ppermute | solution.py:398
  5.0 3.9 %collective-permute-start.2 = (s32[4,8]{1,0:T(4,128)}, s32[4,8]{1,0:T(4,128)}, u32[]{:S(2)}, u32[]{:S(2)}) collective-permute-start(s32[4,8]{1,0:T(4,128)} %refs_0_.1), channel_id=1, source_target_pairs={{0,96},{32,0},{64,32},{96,64},{1,97},{33,1},{65,33},{97,65},{2,98}... | collective-permute-start | bytes 392 | tf_op jit(solution)/shard_map/ppermute | solution.py:398
  11.9 15.6 %all-to-all-start = ((bf16[32,80,128]{2,1,0:T(8,128)(2,1)}), bf16[32,80,128]{2,1,0:T(8,128)(2,1)}, u32[]{:S(2)}, u32[]{:S(2)}) async-start(bf16[32,80,128]{2,1,0:T(8,128)(2,1)} %shard_map.95), calls=%async_computation | async-start | bytes 1310720 | tf_op jit(solution)/shard_map/all_to_all | solution.py:435
  17.4 3.8 %collective-permute-start.3 = (s32[9,64]{1,0:T(8,128)}, s32[9,64]{1,0:T(8,128)}, u32[]{:S(2)}, u32[]{:S(2)}) collective-permute-start(s32[9,64]{1,0:T(8,128)} %pad_add_fusion.1.near_ref), channel_id=1, source_target_pairs={{0,1},{1,0},{2,3},{3,2},{4,5},{5,4},{6,7},{7,6},{8,9},{9,8},{10,11... | collective-permute-start | bytes 6920 | tf_op jit(solution)/shard_map/ppermute | solution.py:398
  27.5 8.5 %collective-permute-start.4 = (bf16[32,80,128]{2,1,0:T(8,128)(2,1)}, bf16[32,80,128]{2,1,0:T(8,128)(2,1)}, u32[]{:S(2)}, u32[]{:S(2)}) collective-permute-start(bf16[32,80,128]{2,1,0:T(8,128)(2,1)} %all-to-all-done.in_ref), channel_id=1, source_target_pairs={{0,1},{1,0},{2,3},{3,2},{4,5},{5,4},{6,7},{7,6},{8,9},{9,8},{10,11... | collective-permute-start | bytes 1966088 | tf_op jit(solution)/shard_map/ppermute | solution.py:398
  30.1 1.8 %copy-start.16 = (s32[4,4,8]{2,1,0:T(4,128)}, s32[4,4,8]{2,1,0:T(4,128)S(1)}, u32[]{:S(2)}) copy-start(s32[4,4,8]{2,1,0:T(4,128)S(1)} %get-tuple-element.58) | copy-start | bytes 1540
  30.1 1.8 %copy-start.7 = (s32[1,4,4,8]{3,2,1,0:T(4,128)}, s32[1,4,4,8]{3,2,1,0:T(4,128)S(1)}, u32[]{:S(2)}) copy-start(s32[1,4,4,8]{3,2,1,0:T(4,128)S(1)} %get-tuple-element.59) | copy-start | bytes 1540
  30.1 1.7 %collective-permute-start.5 = (s32[4,4,8]{2,1,0:T(4,128)S(1)}, s32[4,4,8]{2,1,0:T(4,128)S(1)}, u32[]{:S(2)}, u32[]{:S(2)}) collective-permute-start(s32[4,4,8]{2,1,0:T(4,128)S(1)} %get-tuple-element.58), channel_id=1, source_target_pairs={{0,1},{1,0},{2,3},{3,2},{4,5},{5,4},{6,7},{7,6},{8,9},{9,8},{10,11... | collective-permute-start | bytes 1544 | tf_op jit(solution)/shard_map/ppermute | solution.py:398
  31.9 0.6 copy-start.12
  39.1 24.0 %copy-start.1 = (f32[32,128]{1,0:T(8,128)S(1)}, f32[32,128]{1,0:T(8,128)}, u32[]{:S(2)}) copy-start(f32[32,128]{1,0:T(8,128)} %dynamic-slice_multiply_fusion.refs_3_) | copy-start | bytes 49156
  39.1 0.8 copy-start.2
  39.9 0.7 copy-start.4
  40.6 13.8 %copy-start.8 = (s32[1,4,4,8]{3,2,1,0:T(4,128)S(1)}, s32[1,4,4,8]{3,2,1,0:T(4,128)}, u32[]{:S(2)}) copy-start(s32[1,4,4,8]{3,2,1,0:T(4,128)} %copy-done.7) | copy-start | bytes 1540
  40.6 13.8 %copy-start.13 = (s32[4,4,8]{2,1,0:T(4,128)S(1)}, s32[4,4,8]{2,1,0:T(4,128)}, u32[]{:S(2)}) copy-start(s32[4,4,8]{2,1,0:T(4,128)} %copy-done.12) | copy-start | bytes 1540
  40.6 13.8 %copy-start.11 = (s32[2,4,4,8]{3,2,1,0:T(4,128)S(1)}, s32[2,4,4,8]{3,2,1,0:T(4,128)}, u32[]{:S(2)}) copy-start(s32[2,4,4,8]{3,2,1,0:T(4,128)} %pad_add_fusion) | copy-start | bytes 3076
  40.6 22.5 %copy-start.3 = (s32[1088]{0:T(1024)S(1)}, s32[1088]{0:T(1024)}, u32[]{:S(2)}) copy-start(s32[1088]{0:T(1024)} %get-tuple-element.26.refs_0_) | copy-start | bytes 13060
  45.4 22.5 %copy-start.15 = (pred[32,32]{1,0:T(8,128)(4,1)S(1)}, pred[32,32]{1,0:T(8,128)(4,1)}, u32[]{:S(2)}) copy-start(pred[32,32]{1,0:T(8,128)(4,1)} %and.70) | copy-start | bytes 3076
  45.4 30.1 %copy-start.10 = (pred[128,128]{1,0:T(8,128)(4,1)S(1)}, pred[128,128]{1,0:T(8,128)(4,1)}, u32[]{:S(2)}) copy-start(pred[128,128]{1,0:T(8,128)(4,1)} %and.76) | copy-start | bytes 49156
  45.4 32.5 %copy-start = (f32[64,128]{1,0:T(8,128)S(1)}, f32[64,128]{1,0:T(8,128)}, u32[]{:S(2)}) copy-start(f32[64,128]{1,0:T(8,128)} %get-tuple-element.34.refs_3_) | copy-start | bytes 98308
  45.4 32.5 %copy-start.5 = (s32[1088]{0:T(1024)S(1)}, s32[1088]{0:T(1024)}, u32[]{:S(2)}) copy-start(s32[1088]{0:T(1024)} %get-tuple-element.33.refs_0_) | copy-start | bytes 13060
  45.4 17.6 %all-to-all-start.1 = ((f32[16,32,128]{2,1,0:T(8,128)}), f32[16,32,128]{2,1,0:T(8,128)S(1)}, u32[]{:S(2)}, u32[]{:S(2)}) async-start(f32[16,32,128]{2,1,0:T(8,128)} %get-tuple-element.36), calls=%async_computation.1 | async-start | bytes 524288 | tf_op jit(solution)/shard_map/all_to_all | solution.py:457
  67.8 1.3 collective-permute-start.6
  69.1 6.4 %collective-permute-start.7 = (f32[64,128]{1,0:T(8,128)S(1)}, f32[64,128]{1,0:T(8,128)S(1)}, u32[]{:S(2)}, u32[]{:S(2)}) collective-permute-start(f32[64,128]{1,0:T(8,128)S(1)} %multiply_add_fusion.1.refs_5_), channel_id=1, source_target_pairs={{0,32},{32,64},{64,96},{96,0},{1,33},{33,65},{65,97},{97,1},{2,34}... | collective-permute-start | bytes 98312 | tf_op jit(solution)/shard_map/ppermute | solution.py:398
  71.0 5.4 %collective-permute-start.8 = (f32[64,128]{1,0:T(8,128)S(1)}, f32[64,128]{1,0:T(8,128)S(1)}, u32[]{:S(2)}, u32[]{:S(2)}) collective-permute-start(f32[64,128]{1,0:T(8,128)S(1)} %multiply_add_fusion.1.refs_5_), channel_id=1, source_target_pairs={{0,64},{32,96},{64,0},{96,32},{1,65},{33,97},{65,1},{97,33},{2,66}... | collective-permute-start | bytes 98312 | tf_op jit(solution)/shard_map/ppermute | solution.py:398
  74.0 3.9 %collective-permute-start.9 = (f32[64,128]{1,0:T(8,128)S(1)}, f32[64,128]{1,0:T(8,128)S(1)}, u32[]{:S(2)}, u32[]{:S(2)}) collective-permute-start(f32[64,128]{1,0:T(8,128)S(1)} %multiply_add_fusion.1.refs_5_), channel_id=1, source_target_pairs={{0,96},{32,0},{64,32},{96,64},{1,97},{33,1},{65,33},{97,65},{2,98}... | collective-permute-start | bytes 98312 | tf_op jit(solution)/shard_map/ppermute | solution.py:398
  82.7 20.5 %copy-start.6 = (bf16[4096,64]{0,1:T(8,128)(2,1)S(1)}, bf16[4096,64]{0,1:T(8,128)(2,1)}, u32[]{:S(2)}) copy-start(bf16[4096,64]{0,1:T(8,128)(2,1)} %param.10) | copy-start | bytes 1572868
  103.1 1.3 collective-permute-start.10
  104.4 5.5 %collective-permute-start.11 = (f32[64,128]{1,0:T(8,128)S(1)}, f32[64,128]{1,0:T(8,128)S(1)}, u32[]{:S(2)}, u32[]{:S(2)}) collective-permute-start(f32[64,128]{1,0:T(8,128)S(1)} %multiply_add_fusion.refs_5_), channel_id=1, source_target_pairs={{0,32},{32,64},{64,96},{96,0},{1,33},{33,65},{65,97},{97,1},{2,34}... | collective-permute-start | bytes 98312 | tf_op jit(solution)/shard_map/ppermute | solution.py:398
  104.5 6.0 %collective-permute-start.12 = (f32[64,128]{1,0:T(8,128)S(1)}, f32[64,128]{1,0:T(8,128)S(1)}, u32[]{:S(2)}, u32[]{:S(2)}) collective-permute-start(f32[64,128]{1,0:T(8,128)S(1)} %multiply_add_fusion.refs_5_), channel_id=1, source_target_pairs={{0,64},{32,96},{64,0},{96,32},{1,65},{33,97},{65,1},{97,33},{2,66}... | collective-permute-start | bytes 98312 | tf_op jit(solution)/shard_map/ppermute | solution.py:398
  108.3 3.9 %collective-permute-start.13 = (f32[64,128]{1,0:T(8,128)S(1)}, f32[64,128]{1,0:T(8,128)S(1)}, u32[]{:S(2)}, u32[]{:S(2)}) collective-permute-start(f32[64,128]{1,0:T(8,128)S(1)} %multiply_add_fusion.refs_5_), channel_id=1, source_target_pairs={{0,96},{32,0},{64,32},{96,64},{1,97},{33,1},{65,33},{97,65},{2,98}... | collective-permute-start | bytes 98312 | tf_op jit(solution)/shard_map/ppermute | solution.py:398
  117.0 19.9 %copy-start.14 = (f32[32,128]{1,0:T(8,128)S(1)}, f32[32,128]{1,0:T(8,128)}, u32[]{:S(2)}) copy-start(f32[32,128]{1,0:T(8,128)} %get-tuple-element.42) | copy-start | bytes 49156
  117.0 27.9 %copy-start.9 = (f32[4096]{0:T(1024)S(1)}, f32[4096]{0:T(1024)}, u32[]{:S(2)}) copy-start(f32[4096]{0:T(1024)} %param.11) | copy-start | bytes 49156
  117.0 15.6 %all-to-all-start.3 = ((f32[16,32,128]{2,1,0:T(8,128)}), f32[16,32,128]{2,1,0:T(8,128)S(1)}, u32[]{:S(2)}, u32[]{:S(2)}) async-start(f32[16,32,128]{2,1,0:T(8,128)} %get-tuple-element.40), calls=%async_computation.3 | async-start | bytes 524288 | tf_op jit(solution)/shard_map/all_to_all | solution.py:457
  136.8 1.3 collective-permute-start.15
  136.9 3.9 %collective-permute-start.14 = (f32[32,128]{1,0:T(8,128)S(1)}, f32[32,128]{1,0:T(8,128)S(1)}, u32[]{:S(2)}, u32[]{:S(2)}) collective-permute-start(f32[32,128]{1,0:T(8,128)S(1)} %multiply_add_fusion.2), channel_id=1, source_target_pairs={{0,1},{1,0},{2,3},{3,2},{4,5},{5,4},{6,7},{7,6},{8,9},{9,8},{10,11... | collective-permute-start | bytes 49160 | tf_op jit(solution)/shard_map/ppermute | solution.py:398
  138.1 3.7 %collective-permute-start.18 = (f32[8,128]{1,0:T(8,128)S(1)}, f32[8,128]{1,0:T(8,128)S(1)}, u32[]{:S(2)}, u32[]{:S(2)}) collective-permute-start(f32[8,128]{1,0:T(8,128)S(1)} %get-tuple-element.51), channel_id=1, source_target_pairs={{0,96},{32,0},{64,32},{96,64},{1,97},{33,1},{65,33},{97,65},{2,98}... | collective-permute-start | bytes 12296 | tf_op jit(solution)/shard_map/ppermute | solution.py:476
  139.6 5.1 %collective-permute-start.17 = (f32[8,128]{1,0:T(8,128)S(1)}, f32[8,128]{1,0:T(8,128)S(1)}, u32[]{:S(2)}, u32[]{:S(2)}) collective-permute-start(f32[8,128]{1,0:T(8,128)S(1)} %get-tuple-element.52), channel_id=1, source_target_pairs={{0,64},{32,96},{64,0},{96,32},{1,65},{33,97},{65,1},{97,33},{2,66}... | collective-permute-start | bytes 12296 | tf_op jit(solution)/shard_map/ppermute | solution.py:476
  139.6 5.2 %collective-permute-start.16 = (f32[8,128]{1,0:T(8,128)S(1)}, f32[8,128]{1,0:T(8,128)S(1)}, u32[]{:S(2)}, u32[]{:S(2)}) collective-permute-start(f32[8,128]{1,0:T(8,128)S(1)} %get-tuple-element.53), channel_id=1, source_target_pairs={{0,32},{32,64},{64,96},{96,0},{1,33},{33,65},{65,97},{97,1},{2,34}... | collective-permute-start | bytes 12296 | tf_op jit(solution)/shard_map/ppermute | solution.py:476

commit v3 on v2

--- a/solution.py
+++ b/solution.py
@@ -21,6 +21,9 @@
 GROUP = 32
 EXTRA = 16
 LEFT, RIGHT = 0, 1
+FIRST, ROWS, COLUMNS = 0, 1, 2
+PARTS = 4
+LONG = 1024 * 1024
 HEAD = 8
 STRIDE = 64
 
@@ -44,7 +47,7 @@
     return copies
 
 
-def plan_kernel(half_ref, near_ref, far_ref, col_ref, row_ref, lists, sizes):
+def plan_kernel(half_ref, near_ref, far_ref, col_hbm, row_hbm, col_ref, row_ref, lists, sizes, sems):
     halves = near_ref.shape[1] // 2
     slots = 2 * GROUP
     first = half_ref[0] * halves
@@ -62,35 +65,41 @@
         tiles = jnp.int32(0)
         for group, ref in enumerate((near_ref, far_ref)):
             count = ref[KG, first + b]
-            named = [ref[k, first + b] + group * GROUP for k in range(KG)]
-            for k in range(KG):
-                col_ref[at + tiles + k] = named[k]
-            named = [slot if k < 2 else jnp.where(k < count, slot, slots) for k, slot in enumerate(named)]
-            known = [sizes[slot] for slot in named]
-            for slot, size in zip(named, known):
-                lists[slot * STRIDE + size] = b
-            for slot, size in zip(named, known):
-                sizes[slot] = size + 1
+
+            def some(start, stop, ref=ref, group=group, tiles=tiles, count=count):
+                named = [ref[k, first + b] + group * GROUP for k in range(start, stop)]
+                for k, slot in enumerate(named, start):
+                    col_ref[at + tiles + k] = slot
+                if start >= 2:
+                    named = [jnp.where(k < count, slot, slots) for k, slot in enumerate(named, start)]
+                known = [sizes[slot] for slot in named]
+                for slot, size in zip(named, known):
+                    lists[slot * STRIDE + size] = b
+                for slot, size in zip(named, known):
+                    sizes[slot] = size + 1
+
+            some(0, 2)
+            pl.when(count > 2)(functools.partial(some, 2, KG))
             tiles = tiles + count
         col_ref[at + tiles] = slots
         for k in range(KG):
             col_ref[HEAD + position + k] = b
         return position + (tiles + 1) // 2
 
-    def finish(ref, right, pairs, none):
+    def finish(ref, right, pairs, last, none):
         tails = (pairs + TAIL - 1) // TAIL
         ref[0] = tails // (PAIRS // TAIL)
         ref[1] = tails % (PAIRS // TAIL)
 
         def pad(k, carry):
-            ref[HEAD + pairs + k] = 0
+            ref[HEAD + pairs + k] = last
             ref[right + 2 * (pairs + k)] = none
             ref[right + 2 * (pairs + k) + 1] = none
             return carry
 
         lax.fori_loop(0, tails * TAIL - pairs, pad, 0)
 
-    finish(col_ref, col_right, lax.fori_loop(0, halves, one_block, jnp.int32(0)), slots)
+    finish(col_ref, col_right, lax.fori_loop(0, halves, one_block, jnp.int32(0)), halves - 1, slots)
 
     def one_slot(q, position):
         size = sizes[q]
@@ -103,26 +112,41 @@
                 row_ref[row_right + 2 * (position + k) + j] = lists[q * STRIDE + 2 * k + j]
             return carry
 
-        for k in range(4):
-            one_pair(k, 0)
-        lax.fori_loop(4, pairs, one_pair, 0)
+        def more():
+            for k in range(1, 4):
+                one_pair(k, 0)
+            lax.fori_loop(4, pairs, one_pair, 0)
+
+        one_pair(0, 0)
+        pl.when(pairs > 1)(more)
         return position + pairs
 
-    finish(row_ref, row_right, lax.fori_loop(0, slots, one_slot, jnp.int32(0)), halves)
+    finish(row_ref, row_right, lax.fori_loop(0, slots, one_slot, jnp.int32(0)), slots - 1, halves)
+    pairs = [(ref, hbm.at[pl.ds(0, ref.shape[0])]) for ref, hbm in ((col_ref, col_hbm), (row_ref, row_hbm))]
+    for copy in start_copies(pairs, sems):
+        copy.wait()
+
+
+def list_shape(halves):
+    room = HEAD + 3 * (halves * KG + 2 * GROUP + PAIRS + KG)
+    return ((room + 1023) // 1024 * 1024,)
 
 
 def plan(half, near, far):
-    halves = near.shape[1] // 2
-    room = halves * KG + 2 * GROUP + PAIRS + KG
+    dims = list_shape(near.shape[1] // 2)
     return pl.pallas_call(
         plan_kernel,
-        out_shape=[shape((HEAD + 3 * room,), jnp.int32)] * 2,
+        out_shape=[shape((LONG,), jnp.int32)] * 2,
         in_specs=[SMEM] * 3,
-        out_specs=[SMEM] * 2,
+        out_specs=[HBM] * 2,
         scratch_shapes=[
+            pltpu.SMEM(dims, jnp.int32),
+            pltpu.SMEM(dims, jnp.int32),
             pltpu.SMEM(((2 * GROUP + 1) * STRIDE,), jnp.int32),
             pltpu.SMEM((2 * GROUP + 1,), jnp.int32),
+            pltpu.SemaphoreType.DMA((2,)),
         ],
+        compiler_params=PREPARE,
     )(half.reshape(1), near, far)
 
 
@@ -134,16 +158,21 @@
     return high, middle, low
 
 
+def whole(parts):
+    high, middle, low = [part.astype(jnp.float32) for part in parts]
+    return high + middle + low
+
+
 def log_sum(values):
     top = functools.reduce(jnp.maximum, values)
     return top + jnp.log2(sum(jnp.exp2(value - top) for value in values))
 
 
 def pack_kernel(place_ref, *refs):
-    *ids_refs, points_hbm, potential_hbm, logmass_hbm, out_ref, points, potential, logmass, sems = refs
-    copies = start_copies(
-        [(potential_hbm, potential), (logmass_hbm, logmass), (points_hbm, points)], sems
-    )
+    count = (len(refs) - 2) // 2
+    remotes, (out_ref, *locals_, sems) = refs[:count], refs[count:]
+    *ids_refs, points, potential, logmass = locals_
+    copies = start_copies(list(zip(remotes, locals_)), sems)
     place = place_ref[0]
     peers, per_peer = ids_refs[0].shape
     for copy in copies:
@@ -167,67 +196,30 @@
         lax.fori_loop(0, per_peer, one_block, 0, unroll=8)
 
 
-def pack(place, ids, points, potential, logmass):
-    count = ids[0].size
+def pack(place, ids, *values):
+    remotes = [*ids, *values]
     return pl.pallas_call(
         pack_kernel,
-        out_shape=shape((count, D + EXTRA, BLOCK), jnp.bfloat16),
-        in_specs=[SMEM] * (1 + len(ids)) + [HBM] * 3,
+        out_shape=shape((ids[0].size, D + EXTRA, BLOCK), jnp.bfloat16),
+        in_specs=[SMEM] + [HBM] * len(remotes),
         out_specs=VMEM,
-        scratch_shapes=[
-            pltpu.VMEM(points.shape, points.dtype),
-            pltpu.VMEM(potential.shape, potential.dtype),
-            pltpu.VMEM(logmass.shape, logmass.dtype),
-            pltpu.SemaphoreType.DMA((3,)),
-        ],
+        scratch_shapes=[pltpu.SMEM(value.shape, value.dtype) for value in ids]
+        + [pltpu.VMEM(value.shape, value.dtype) for value in values]
+        + [pltpu.SemaphoreType.DMA((len(remotes),))],
         compiler_params=PREPARE,
-    )(place.reshape(1), *ids, points, potential, logmass)
-
-
-def unpack_kernel(group, in_ref, *refs):
-    outs, (blocks, start, mass, sems) = refs[-7:-4], refs[-4:]
-
-    def one_block(q, carry):
-        block = in_ref[q, :D, :]
-        both = jnp.concatenate([block, block], axis=0)
-        blocks[RIGHT, q] = both
-        blocks[LEFT, q] = both.T
-        rows = in_ref[q, D:, :].astype(jnp.float32)
-        start[pl.ds(q, 1), :] = rows[0:1] + rows[1:2] + rows[2:3]
-        mass[pl.ds(q, 1), :] = rows[3:4] + rows[4:5] + rows[5:6]
-        return carry
-
-    lax.fori_loop(0, GROUP, one_block, 0, unroll=8)
-    own = pl.ds(group * GROUP, GROUP)
-    pairs = [(blocks, outs[0].at[:, own]), (start, outs[1].at[own]), (mass, outs[2].at[own])]
+    )(place.reshape(1), *remotes)
+
+
+def source_kernel(half_ref, points_hbm, logmass_hbm, blocks_hbm, norm_ref, points, logmass, blocks, sems):
+    halves = blocks.shape[1] - 1
+    rows = pl.ds(pl.multiple_of(half_ref[0] * halves, halves), halves)
+    at = pl.multiple_of(half_ref[0] * (halves * BLOCK), halves * BLOCK)
+    pairs = [(points_hbm.at[:, pl.ds(at, halves * BLOCK)], points), (logmass_hbm.at[rows], logmass)]
     for copy in start_copies(pairs, sems):
         copy.wait()
-
-
-def unpack(group, fetched, before):
-    return pl.pallas_call(
-        functools.partial(unpack_kernel, group),
-        out_shape=[shape((2, 2 * GROUP, BLOCK, BLOCK), jnp.bfloat16)]
-        + [shape((2 * GROUP, BLOCK))] * 2,
-        in_specs=[VMEM] + [HBM] * len(before),
-        out_specs=[HBM] * 3,
-        scratch_shapes=[
-            pltpu.VMEM((2, GROUP, BLOCK, BLOCK), jnp.bfloat16),
-            pltpu.VMEM((GROUP, BLOCK), jnp.float32),
-            pltpu.VMEM((GROUP, BLOCK), jnp.float32),
-            pltpu.SemaphoreType.DMA((3,)),
-        ],
-        input_output_aliases={1 + k: k for k in range(len(before))},
-        compiler_params=PREPARE,
-    )(fetched, *before)
-
-
-def source_kernel(half_ref, points_hbm, blocks_hbm, norm_ref, points, blocks, sems):
-    halves = blocks.shape[1]
-    at = pl.multiple_of(half_ref[0] * (halves * BLOCK), halves * BLOCK)
-    copy = pltpu.make_async_copy(points_hbm.at[:, pl.ds(at, halves * BLOCK)], points, sems.at[0])
-    copy.start()
-    copy.wait()
+    parts = split3(LOG2E * logmass[...])
+    blocks[LEFT, halves] = jnp.concatenate([*parts, jnp.zeros_like(parts[0])], axis=0)
+    blocks[RIGHT, halves] = jnp.zeros((BLOCK, BLOCK), jnp.bfloat16)
 
     def one_block(b, carry):
         wide = points[:, pl.ds(pl.multiple_of(b * BLOCK, BLOCK), BLOCK)].astype(jnp.float32)
@@ -241,37 +233,37 @@
         return carry
 
     lax.fori_loop(0, halves, one_block, 0, unroll=4)
-    copy = pltpu.make_async_copy(blocks, blocks_hbm, sems.at[1])
+    copy = pltpu.make_async_copy(blocks, blocks_hbm, sems.at[0])
     copy.start()
     copy.wait()
 
 
-def source(half, halves, points):
-    blocks = (2, halves, BLOCK, BLOCK)
+def source(half, halves, points, logmass):
+    blocks = (2, halves + 1, BLOCK, BLOCK)
     return pl.pallas_call(
         source_kernel,
         out_shape=[shape(blocks, jnp.bfloat16), shape((halves, BLOCK))],
-        in_specs=[SMEM, HBM],
+        in_specs=[SMEM, HBM, HBM],
         out_specs=[HBM, VMEM],
         scratch_shapes=[
             pltpu.VMEM((D, halves * BLOCK), jnp.bfloat16),
+            pltpu.VMEM((halves, BLOCK), jnp.float32),
             pltpu.VMEM(blocks, jnp.bfloat16),
             pltpu.SemaphoreType.DMA((2,)),
         ],
         compiler_params=PREPARE,
-    )(half.reshape(1), points)
-
-
-def start_bias(start_ref):
-    return start_ref[...]
+    )(half.reshape(1), points, logmass)
 
 
 def field_bias(mass_ref, parts_ref):
-    return mass_ref[...] - log_sum([parts_ref[k] for k in range(parts_ref.shape[0])])
+    rows = parts_ref.shape[1]
+    mass = whole([mass_ref[k * rows : (k + 1) * rows, :] for k in range(3)])
+    return mass - log_sum([parts_ref[k] for k in range(parts_ref.shape[0])])
 
 
 def potential_bias(mass_ref, chosen_ref, *refs):
     dot = functools.partial(jnp.dot, preferred_element_type=jnp.float32)
+    mass = whole([mass_ref[0, : 2 * GROUP, :], mass_ref[0, 2 * GROUP :, :], mass_ref[1, : 2 * GROUP, :]])
     out = []
     for group in range(2):
         own = slice(group * GROUP, (group + 1) * GROUP)
@@ -281,29 +273,66 @@
         known = dot(chosen, jnp.ones_like(chosen)) > 0.5
         parts = jnp.where(known, parts, LOWEST)
         merged = log_sum([parts[k * GROUP : (k + 1) * GROUP] for k in range(len(refs))])
-        out.append(mass_ref[own, :] - merged)
+        out.append(mass[own, :] - merged)
     return jnp.concatenate(out, axis=0)
 
 
-def pass_kernel(bias_of, fixed_count, parts_count, *refs):
-    remote_count = 3 + fixed_count
-    remotes, refs = refs[:remote_count], refs[remote_count:]
-    bias_parts, refs = refs[:parts_count], refs[parts_count:]
-    out_ref, bias_ref, columns, peaks, masses, sems = refs[:6]
-    locals_ = refs[6:]
-    list_ref, left_ref, right_ref, *fixed = locals_
-    sources = [remotes[0], remotes[1].at[LEFT], remotes[2].at[RIGHT], *remotes[3:]]
-    copies = start_copies(list(zip(sources, locals_))[::-1], sems)
-    lefts, rights = left_ref.shape[0], right_ref.shape[0]
+def unpack(raw, left, start_ref, mass_ref):
+    def one_block(q, carry):
+        block = raw[q, :D, :]
+        left[q] = jnp.concatenate([block, block], axis=0).T
+        rows = raw[q, D:, :].astype(jnp.float32)
+        start_ref[pl.ds(q, 1), :] = rows[0:1] + rows[1:2] + rows[2:3]
+        mass_ref[pl.ds(q, 1), :] = rows[3:4] + rows[4:5] + rows[5:6]
+        return carry
+
+    return lambda group: lax.fori_loop(group * GROUP, (group + 1) * GROUP, one_block, 0, unroll=8)
+
+
+def pass_kernel(kind, *refs):
+    columns, peaks, masses, list_ref, left_ref, right_ref, sems = refs[-7:]
+    lefts, rights = columns.shape[0], right_ref.shape[0]
+    part = lefts // PARTS
+    left_parts = []
+    if kind == FIRST:
+        list_hbm, near_hbm, far_hbm, points_hbm, out_ref, left_hbm, mass_ref, bias_ref, raw = refs[:-7]
+        early = [(near_hbm, raw.at[pl.ds(0, GROUP)]), (far_hbm, raw.at[pl.ds(GROUP, GROUP)])]
+        late = [(points_hbm.at[RIGHT, pl.ds(0, rights)], right_ref)]
+    elif kind == ROWS:
+        list_hbm, left_hbm, points_hbm, chosen_hbm = refs[:4]
+        *col_parts, out_ref, bias_ref, mass, chosen = refs[4:-7]
+        early = [(left_hbm.at[pl.ds(lefts, 2)], mass), (chosen_hbm, chosen)]
+        late = [(points_hbm.at[RIGHT, pl.ds(0, rights)], right_ref)]
+        left_parts = [left_hbm.at[pl.ds(k * part, part)] for k in range(PARTS)]
+    else:
+        list_hbm, near_hbm, far_hbm, points_hbm, rows_ref, out_ref, bias_ref, mass = refs[:-7]
+        early = [(points_hbm.at[LEFT, lefts], mass)]
+        late = [(near_hbm, right_ref.at[pl.ds(0, GROUP)]), (far_hbm, right_ref.at[pl.ds(GROUP, GROUP)])]
+        left_parts = [points_hbm.at[LEFT, pl.ds(k * part, part)] for k in range(PARTS)]
+    late.append((list_hbm.at[pl.ds(0, list_ref.shape[0])], list_ref))
+    pairs = early + late + [(ref, left_ref.at[pl.ds(k * part, part)]) for k, ref in enumerate(left_parts)]
+    copies = start_copies(pairs, sems)
+    peaks[...] = jnp.full_like(peaks, LOWEST)
+    masses[...] = jnp.zeros_like(masses)
+    for copy in copies[: len(early)]:
+        copy.wait()
+    if kind == FIRST:
+        unpack_group = unpack(raw, left_ref, bias_ref, mass_ref)
+        for group in range(2):
+            unpack_group(group)
+        high, middle, low = split3(mass_ref[...])
+        left_ref[lefts] = jnp.concatenate([high, middle], axis=0)
+        left_ref[lefts + 1] = jnp.concatenate([low, jnp.zeros_like(low)], axis=0)
+        hand_on = pltpu.make_async_copy(left_ref, left_hbm, sems.at[len(pairs)])
+        hand_on.start()
+    elif kind == ROWS:
+        bias_ref[...] = potential_bias(mass, chosen, *col_parts)
+    else:
+        bias_ref[...] = field_bias(mass, rows_ref)
     square = (BLOCK, BLOCK)
     lane = lax.broadcasted_iota(jnp.int32, square, 1)
     eye = jnp.where(lane == lax.broadcasted_iota(jnp.int32, square, 0), 1.0, 0.0).astype(jnp.bfloat16)
     lane = jnp.where(lane < 3 * GROUP, lane % GROUP, -1)
-    peaks[...] = jnp.full_like(peaks, LOWEST)
-    masses[...] = jnp.zeros_like(masses)
-    for copy in copies[:fixed_count]:
-        copy.wait()
-    bias_ref[...] = bias_of(*fixed, *bias_parts)
     for group in range(lefts // GROUP):
         high, middle, low = split3(bias_ref[group * GROUP : (group + 1) * GROUP, :])
         parts = jnp.concatenate([high, middle, low, jnp.zeros_like(high)], axis=0)
@@ -316,7 +345,7 @@
             return carry
 
         lax.fori_loop(0, GROUP, fill, 0, unroll=4)
-    for copy in copies[fixed_count:]:
+    for copy in copies[len(early) : len(early) + len(late)]:
         copy.wait()
     rights_at = HEAD + (list_ref.shape[0] - HEAD) // 3
     ones = jnp.ones((BLOCK, 2 * BLOCK), jnp.bfloat16)
@@ -330,9 +359,27 @@
         peaks[copy, r] = top
 
     def right_block(r):
-        return right_ref[jnp.minimum(r, rights - 1)]
-
-    def step(start, count, t, carry):
+        r = jnp.minimum(r, rights - 1)
+        if kind != COLUMNS:
+            return right_ref[r]
+        block = right_ref[r, :D, :]
+        return jnp.concatenate([block, block], axis=0)
+
+    def wait_for(known, needed):
+        if not left_parts:
+            return known
+
+        def wait(k, carry):
+            at = pl.ds(k * part, part)
+            source = left_hbm.at[at] if kind == ROWS else points_hbm.at[LEFT, at]
+            pltpu.make_async_copy(source, left_ref.at[at], sems.at[len(early) + len(late) + k]).wait()
+            return carry
+
+        lax.fori_loop(known, needed, wait, 0)
+        return jnp.maximum(known, needed)
+
+    def step(start, count, t, known):
+        known = wait_for(known, list_ref[HEAD + start + t * count + count - 1] // part + 1)
         for u in range(count):
             i = start + t * count + u
             l = list_ref[HEAD + i]
@@ -344,10 +391,11 @@
             )
             fold((2 * u) % COPIES, first, scores[:, :BLOCK])
             fold((2 * u + 1) % COPIES, second, scores[:, BLOCK:])
-        return carry
-
-    lax.fori_loop(0, list_ref[0], functools.partial(step, 0, PAIRS), 0)
-    lax.fori_loop(0, list_ref[1], functools.partial(step, list_ref[0] * PAIRS, TAIL), 0)
+        return known
+
+    known = lax.fori_loop(0, list_ref[0], functools.partial(step, 0, PAIRS), jnp.int32(0))
+    known = lax.fori_loop(0, list_ref[1], functools.partial(step, list_ref[0] * PAIRS, TAIL), known)
+    wait_for(known, PARTS)
 
     def finish(octet, carry):
         rows = []
@@ -363,28 +411,42 @@
     lax.fori_loop(0, rights // 8, finish, 0)
     for k in range(1, out_ref.shape[0]):
         out_ref[k] = out_ref[0]
-
-
-def log_sums(pairs, left, right, bias_of, fixed, parts, copies):
-    lefts, rights = left.shape[1], right.shape[1]
-    remotes = [pairs, left, right, *fixed]
+    if kind == FIRST:
+        hand_on.wait()
+
+
+def log_sums(kind, pairs, halves, remotes, parts, copies):
+    slots = 2 * GROUP
+    lefts, rights = (halves, slots) if kind == COLUMNS else (slots, halves)
+    rows = D + EXTRA if kind == COLUMNS else BLOCK
+    held = lefts
+    outs, bias = [shape((copies, rights, BLOCK))], pltpu.VMEM((lefts, BLOCK), jnp.float32)
+    if kind == FIRST:
+        held = lefts + 2
+        outs.append(shape((held, BLOCK, BLOCK), jnp.bfloat16))
+        scratch = [bias, bias, pltpu.VMEM((slots, D + EXTRA, BLOCK), jnp.bfloat16)]
+    elif kind == ROWS:
+        scratch = [bias, pltpu.VMEM((2, BLOCK, BLOCK), jnp.bfloat16), pltpu.VMEM(remotes[-1].shape, jnp.bfloat16)]
+    else:
+        outs.append(shape((lefts, BLOCK)))
+        scratch = [pltpu.VMEM((BLOCK, BLOCK), jnp.bfloat16)]
     return pl.pallas_call(
-        functools.partial(pass_kernel, bias_of, len(fixed), len(parts)),
-        out_shape=[shape((copies, rights, BLOCK)), shape((lefts, BLOCK))],
-        in_specs=[HBM] * len(remotes) + [VMEM] * len(parts),
-        out_specs=[VMEM, VMEM],
-        scratch_shapes=[
+        functools.partial(pass_kernel, kind),
+        out_shape=outs,
+        in_specs=[HBM] * (1 + len(remotes)) + [VMEM] * len(parts),
+        out_specs=[VMEM, HBM] if kind == FIRST else [VMEM] * len(outs),
+        scratch_shapes=scratch
+        + [
             pltpu.VMEM((lefts, BLOCK, BLOCK), jnp.bfloat16),
             pltpu.VMEM((COPIES, rights + 1, 8, BLOCK), jnp.float32),
             pltpu.VMEM((COPIES, rights + 1, 8, BLOCK), jnp.float32),
-            pltpu.SemaphoreType.DMA((len(remotes),)),
-            pltpu.SMEM(pairs.shape, pairs.dtype),
-            pltpu.VMEM(left.shape[1:], left.dtype),
-            pltpu.VMEM(right.shape[1:], right.dtype),
-        ]
-        + [pltpu.VMEM(value.shape, value.dtype) for value in fixed],
-        compiler_params=PASS,
-    )(*remotes, *parts)
+            pltpu.SMEM(list_shape(halves), jnp.int32),
+            pltpu.VMEM((held, BLOCK, BLOCK), jnp.bfloat16),
+            pltpu.VMEM((rights, rows, BLOCK), jnp.bfloat16),
+            pltpu.SemaphoreType.DMA((5 + PARTS,)),
+        ],
+        compiler_params=PREPARE if kind == FIRST else PASS,
+    )(pairs, *remotes, *parts)
 
 
 def ring(values, axis, size, stride=1):
@@ -433,13 +495,11 @@
     ids = jnp.stack(ids)
     col_pairs, row_pairs = plan(half, tiles, swap(tiles))
     fetched = lax.all_to_all(packed, "src", split_axis=0, concat_axis=0, tiled=True)
-    points, source_half = source(half, halves, source_points.T)
+    points, source_half = source(
+        half, halves, source_points.T, source_logmass.reshape(blocks, BLOCK)
+    )
     fetched, points, col_pairs, row_pairs = lax.optimization_barrier((fetched, points, col_pairs, row_pairs))
-    targets, potentials, slot_mass = unpack(1, swap(fetched), unpack(0, fetched, []))
-    source_mass = LOG2E * lax.dynamic_slice(
-        source_logmass.reshape(blocks, BLOCK), (half * halves, 0), (halves, BLOCK)
-    )
-
+    both = [fetched, swap(fetched)]
     all_ids = jnp.stack([ids, swap(ids)])
     same = all_ids[:, :, :, None, :] == all_ids[:, :1, :, :, None]
     same = same[:, :, :, :, None, :] & jnp.eye(peers, dtype=bool)[:, None, :, None]
@@ -450,14 +510,14 @@
     same_core = [list(range(core, groups, 2)) for core in range(2)]
     for sweep_index in range(ITERS):
         if sweep_index == 0:
-            bias_of, fixed, parts = start_bias, [potentials], []
+            rows, targets = log_sums(FIRST, row_pairs, halves, [*both, points], [], groups // 2)
         else:
-            bias_of, fixed, parts = potential_bias, [slot_mass, chosen], col_parts
-        rows, _ = log_sums(row_pairs, targets, points, bias_of, fixed, parts, groups // 2)
+            remotes = [targets, points, chosen]
+            (rows,) = log_sums(ROWS, row_pairs, halves, remotes, col_parts, groups // 2)
         rows = lax.all_to_all(
             rows, "grp", split_axis=0, concat_axis=0, tiled=True, axis_index_groups=same_core
         )
-        cols, field = log_sums(col_pairs, points, targets, field_bias, [source_mass], [rows], 1)
+        cols, field = log_sums(COLUMNS, col_pairs, halves, [*both, points], [rows], 1)
         cols = cols[0]
         if sweep_index < ITERS - 1:
             other = swap(cols)

time: 147 us -> 142 us (0.966); the launches traced: 146 us -> 143 us
  Pallas kernels: 47.1 us -> 39.8 us
  starting transfers between devices: 40.5 us -> 47.2 us
  local copies, waits for them, and re-layouts: 5.14 us -> 3.06 us
    pallas_call x10 -> x8, Pallas kernels: 43.3 us -> 35.9 us  [the longest x6 27 us: log_sums(): pl.pallas_call(functools.partial(pass_kernel, kind), out_shape=outs, in_s...]
    ppermute x3, starting transfers between devices: 2.62 us -> 6.44 us  [shards(): back.append(wanted if d == 0 else lax.ppermute(wanted, 'src', pairs))]
    unnamed x34 -> x16, local copies, waits for them, and re-layouts: 2.11 us -> 0.04 us
    all_to_all x2, starting transfers between devices: 15.9 us -> 17.4 us  [shards(): lax.all_to_all(rows, 'grp', split_axis=0, concat_axis=0, tiled=True, axis...]
  transfers between devices with their start and end apart: 22 -> 22, of which waited for: 14 -> 14; matrix products, arithmetic and copies ran while one was open for 6% -> 6% of each run, Pallas kernels for 9% -> 7%
where the time goes in v3:
time: 142 us; the launch traced here: 143 us
  starting transfers between devices  47.2 us (33%)
  Pallas kernels  39.8 us (28%)
  waiting for transfers between devices  31.1 us (22%)
  blocking collectives  14.3 us (10%)
  other arithmetic  6.12 us (4%)
  local copies, waits for them, and re-layouts  3.06 us (2%)
    pallas_call x6, Pallas kernels, log_sums(): pl.pallas_call(functools.partial(pass_kernel, kind), out_shape=outs, in_s...  27 us
    ppermute x16, starting transfers between devices, ring(): out.append(lax.ppermute(values, axis, pairs))  19.1 us
    all_to_all x2, starting transfers between devices, shards(): lax.all_to_all(rows, 'grp', split_axis=0, concat_axis=0, tiled=True, axis...  17.4 us
    all_to_all x2, waiting for transfers between devices, shards(): lax.all_to_all(rows, 'grp', split_axis=0, concat_axis=0, tiled=True, axis...  16.7 us
    all_to_all x1, blocking collectives, shards(): lax.all_to_all(rows, 'grp', split_axis=0, concat_axis=0, tiled=True, axis...  14.3 us
    ppermute x16, waiting for transfers between devices, ring(): out.append(lax.ppermute(values, axis, pairs))  10.6 us
    pallas_call x1, Pallas kernels, plan(): pl.pallas_call(plan_kernel, out_shape=[shape((LONG,), jnp.int32)] * 2, in...  6.65 us
    ppermute x3, starting transfers between devices, shards(): back.append(wanted if d == 0 else lax.ppermute(wanted, 'src', pairs))  6.44 us
  transfers between devices with their start and end apart: 22, of which 14 were waited for; matrix products, arithmetic and copies ran while one was open for 6% of the time, Pallas kernels for 7%

profile of v3, /device:TPU:0, one launch (start us, length us, event | category | flops | bytes accessed | tf_op | source)
XLA Modules:
  0.0 142.6 jit_solution(11022992425296778884)
XLA Ops:
  0.6 1.6 %collective-permute-start = (s32[4,8]{1,0:T(4,128)}, s32[4,8]{1,0:T(4,128)}, u32[]{:S(2)}, u32[]{:S(2)}) collective-permute-start(s32[4,8]{1,0:T(4,128)} %refs_0_.1), channel_id=1, source_target_pairs={{0,32},{32,64},{64,96},{96,0},{1,33},{33,65},{65,97},{97,1},{2,34}... | collective-permute-start | bytes 392 | tf_op jit(solution)/shard_map/ppermute | solution.py:460
  2.3 2.7 %collective-permute-start.1 = (s32[4,8]{1,0:T(4,128)}, s32[4,8]{1,0:T(4,128)}, u32[]{:S(2)}, u32[]{:S(2)}) collective-permute-start(s32[4,8]{1,0:T(4,128)} %refs_0_.1), channel_id=1, source_target_pairs={{0,64},{32,96},{64,0},{96,32},{1,65},{33,97},{65,1},{97,33},{2,66}... | collective-permute-start | bytes 392 | tf_op jit(solution)/shard_map/ppermute | solution.py:460
  5.0 1.4 %collective-permute-start.2 = (s32[4,8]{1,0:T(4,128)}, s32[4,8]{1,0:T(4,128)}, u32[]{:S(2)}, u32[]{:S(2)}) collective-permute-start(s32[4,8]{1,0:T(4,128)} %refs_0_.1), channel_id=1, source_target_pairs={{0,96},{32,0},{64,32},{96,64},{1,97},{33,1},{65,33},{97,65},{2,98}... | collective-permute-start | bytes 392 | tf_op jit(solution)/shard_map/ppermute | solution.py:460
  6.4 1.2 collective-permute-done.1.refs_2_
  7.7 1.1 collective-permute-done.2.refs_3_
  8.8 2.3 %shard_map.95 = bf16[32,80,128]{2,1,0:T(8,128)(2,1)} custom-call(s32[1]{0:T(128)} %bitcast.place_ref, s32[4,8]{1,0:T(4,128)} %refs_0_.1, s32[4,8]{1,0:T(4,128)} %collective-permute-done.refs_1_, s32[4,8]{1,0:T(4,128)} %collective-permute-done.1.refs_2_, s32[4,8]{1,0:T(4,128)} %collective-permute-done.2.refs_3_, bf16[64,4096]{1,0:T(8,128)(2,1)} %bitcast.152, ...), custom_call_target="tpu_custom_call" | custom-call | tf_op jit(solution)/shard_map/pallas_call | solution.py:201
  11.0 4.2 %all-to-all-start = ((bf16[32,80,128]{2,1,0:T(8,128)(2,1)}), bf16[32,80,128]{2,1,0:T(8,128)(2,1)}, u32[]{:S(2)}, u32[]{:S(2)}) async-start(bf16[32,80,128]{2,1,0:T(8,128)(2,1)} %shard_map.95), calls=%async_computation | async-start | bytes 1310720 | tf_op jit(solution)/shard_map/all_to_all | solution.py:497
  15.2 1.3 pad_add_fusion.1.near_ref
  16.5 3.8 %shard_map.96 = (bf16[2,33,128,128]{3,2,1,0:T(8,128)(2,1)}, f32[32,128]{1,0:T(8,128)}) custom-call(s32[1]{0:T(128)} %bitcast.4.half_ref, bf16[64,8192]{1,0:T(8,128)(2,1)} %bitcast.153, f32[64,128]{1,0:T(8,128)} %bitcast.155), custom_call_target="tpu_custom_call" | custom-call | tf_op jit(solution)/shard_map/pallas_call | solution.py:243
  20.4 6.7 %shard_map.97 = (s32[1048576]{0:T(1024)}, s32[1048576]{0:T(1024)}) custom-call(s32[1]{0:T(128)} %bitcast.4.half_ref, s32[9,64]{1,0:T(8,128)} %pad_add_fusion.1.near_ref, s32[9,64]{1,0:T(8,128)} %collective-permute-done.3.far_ref), custom_call_target="tpu_custom_call" | custom-call | tf_op jit(solution)/shard_map/pallas_call | solution.py:137
  27.0 0.6 collective-permute-start.4
  27.6 0.7 pad_add_fusion.2
  28.5 0.7 and.70
  29.3 0.7 and.76
  30.1 0.6 pad_add_fusion
  30.7 5.7 %shard_map.98 = (f32[16,32,128]{2,1,0:T(8,128)}, bf16[66,128,128]{2,1,0:T(8,128)(2,1)}) custom-call(s32[1048576]{0:T(1024)} %get-tuple-element.22.refs_0_, bf16[32,80,128]{2,1,0:T(8,128)(2,1)} %all-to-all-done.refs_1_, bf16[32,80,128]{2,1,0:T(8,128)(2,1)} %collective-permute-done.4.refs_2_, bf16[2,33,128,128]{3,2,1,0:T(8,128)(2,1)} %get-tuple-element.21.refs_3_.refs_2_), custom_call_target="tpu_custom_call" | custom-call | tf_op jit(solution)/shard_map/pallas_call | solution.py:433
  36.4 10.0 %all-to-all-start.1 = ((f32[16,32,128]{2,1,0:T(8,128)}), f32[16,32,128]{2,1,0:T(8,128)S(1)}, u32[]{:S(2)}, u32[]{:S(2)}) async-start(f32[16,32,128]{2,1,0:T(8,128)} %get-tuple-element.24), calls=%async_computation.1 | async-start | bytes 524288 | tf_op jit(solution)/shard_map/all_to_all | solution.py:517
  46.4 0.7 fusion.33
  47.1 0.8 broadcast_compare_fusion
  48.2 8.0 %all-to-all-done.1.refs_4_ = f32[16,32,128]{2,1,0:T(8,128)S(1)} async-done(((f32[16,32,128]{2,1,0:T(8,128)}), f32[16,32,128]{2,1,0:T(8,128)S(1)}, u32[]{:S(2)}, u32[]{:S(2)}) %all-to-all-start.1) | async-done | bytes 262176 | tf_op jit(solution)/shard_map/all_to_all | solution.py:517
  56.3 4.5 %shard_map.99 = (f32[1,64,128]{2,1,0:T(8,128)S(1)}, f32[32,128]{1,0:T(8,128)}) custom-call(s32[1048576]{0:T(1024)} %get-tuple-element.19.refs_0_, bf16[32,80,128]{2,1,0:T(8,128)(2,1)} %all-to-all-done.refs_1_, bf16[32,80,128]{2,1,0:T(8,128)(2,1)} %collective-permute-done.4.refs_2_, bf16[2,33,128,128]{3,2,1,0:T(8,128)(2,1)} %get-tuple-element.21.refs_3_.refs_2_, ...), custom_call_target="tpu_custom_call" | custom-call | tf_op jit(solution)/shard_map/pallas_call | solution.py:433
  61.2 0.8 collective-permute-done.6
  62.1 1.4 collective-permute-start.7
  63.5 3.6 %collective-permute-start.8 = (f32[64,128]{1,0:T(8,128)S(1)}, f32[64,128]{1,0:T(8,128)S(1)}, u32[]{:S(2)}, u32[]{:S(2)}) collective-permute-start(f32[64,128]{1,0:T(8,128)S(1)} %multiply_add_fusion.1.refs_4_), channel_id=1, source_target_pairs={{0,64},{32,96},{64,0},{96,32},{1,65},{33,97},{65,1},{97,33},{2,66}... | collective-permute-start | bytes 98312 | tf_op jit(solution)/shard_map/ppermute | solution.py:460
  67.1 0.4 collective-permute-done.7.refs_5_
  67.5 1.8 %collective-permute-done.8.refs_6_ = f32[64,128]{1,0:T(8,128)S(1)} collective-permute-done((f32[64,128]{1,0:T(8,128)S(1)}, f32[64,128]{1,0:T(8,128)S(1)}, u32[]{:S(2)}, u32[]{:S(2)}) %collective-permute-start.8) | collective-permute-done | bytes 32800 | tf_op jit(solution)/shard_map/ppermute | solution.py:460
  69.3 1.7 %collective-permute-done.9.refs_7_ = f32[64,128]{1,0:T(8,128)S(1)} collective-permute-done((f32[64,128]{1,0:T(8,128)S(1)}, f32[64,128]{1,0:T(8,128)S(1)}, u32[]{:S(2)}, u32[]{:S(2)}) %collective-permute-start.9) | collective-permute-done | bytes 32800 | tf_op jit(solution)/shard_map/ppermute | solution.py:460
  71.0 3.8 %shard_map.100 = f32[16,32,128]{2,1,0:T(8,128)S(1)} custom-call(s32[1048576]{0:T(1024)} %get-tuple-element.22.refs_0_, bf16[66,128,128]{2,1,0:T(8,128)(2,1)} %get-tuple-element.23.refs_1_, bf16[2,33,128,128]{3,2,1,0:T(8,128)(2,1)} %get-tuple-element.21.refs_3_.refs_2_, bf16[2,128,128]{2,1,0:T(8,128)(2,1)S(1)} %and_convert_fusion.refs_3_, ...), custom_call_target="tpu_custom_call" | custom-call | tf_op jit(solution)/shard_map/pallas_call | solution.py:433
  74.9 14.3 %all_to_all.20.refs_4_ = f32[16,32,128]{2,1,0:T(8,128)S(1)} all-to-all(f32[16,32,128]{2,1,0:T(8,128)S(1)} %shard_map.100), channel_id=1, replica_groups={{0,2,4,6,8,10,12,14,16,18,20,22,24,26,28,30},{1,3,5,7,9,11,13,15,17,19,..., dimensions={0} | all-to-all | bytes 524288 | tf_op jit(solution)/shard_map/all_to_all | solution.py:517
  89.2 4.6 %shard_map.101 = (f32[1,64,128]{2,1,0:T(8,128)S(1)}, f32[32,128]{1,0:T(8,128)}) custom-call(s32[1048576]{0:T(1024)} %get-tuple-element.19.refs_0_, bf16[32,80,128]{2,1,0:T(8,128)(2,1)} %all-to-all-done.refs_1_, bf16[32,80,128]{2,1,0:T(8,128)(2,1)} %collective-permute-done.4.refs_2_, bf16[2,33,128,128]{3,2,1,0:T(8,128)(2,1)} %get-tuple-element.21.refs_3_.refs_2_, ...), custom_call_target="tpu_custom_call" | custom-call | tf_op jit(solution)/shard_map/pallas_call | solution.py:433
  94.0 1.0 collective-permute-done.10
  95.1 4.0 %collective-permute-start.11 = (f32[64,128]{1,0:T(8,128)S(1)}, f32[64,128]{1,0:T(8,128)S(1)}, u32[]{:S(2)}, u32[]{:S(2)}) collective-permute-start(f32[64,128]{1,0:T(8,128)S(1)} %multiply_add_fusion.refs_4_), channel_id=1, source_target_pairs={{0,32},{32,64},{64,96},{96,0},{1,33},{33,65},{65,97},{97,1},{2,34}... | collective-permute-start | bytes 98312 | tf_op jit(solution)/shard_map/ppermute | solution.py:460
  99.1 1.6 %collective-permute-start.12 = (f32[64,128]{1,0:T(8,128)S(1)}, f32[64,128]{1,0:T(8,128)S(1)}, u32[]{:S(2)}, u32[]{:S(2)}) collective-permute-start(f32[64,128]{1,0:T(8,128)S(1)} %multiply_add_fusion.refs_4_), channel_id=1, source_target_pairs={{0,64},{32,96},{64,0},{96,32},{1,65},{33,97},{65,1},{97,33},{2,66}... | collective-permute-start | bytes 98312 | tf_op jit(solution)/shard_map/ppermute | solution.py:460
  100.7 1.1 collective-permute-start.13
  101.9 0.7 fusion.34
  102.6 2.0 %collective-permute-done.12.refs_6_ = f32[64,128]{1,0:T(8,128)S(1)} collective-permute-done((f32[64,128]{1,0:T(8,128)S(1)}, f32[64,128]{1,0:T(8,128)S(1)}, u32[]{:S(2)}, u32[]{:S(2)}) %collective-permute-start.12) | collective-permute-done | bytes 32800 | tf_op jit(solution)/shard_map/ppermute | solution.py:460
  104.6 4.5 %shard_map.102 = f32[16,32,128]{2,1,0:T(8,128)} custom-call(s32[1048576]{0:T(1024)} %get-tuple-element.22.refs_0_, bf16[66,128,128]{2,1,0:T(8,128)(2,1)} %get-tuple-element.23.refs_1_, bf16[2,33,128,128]{3,2,1,0:T(8,128)(2,1)} %get-tuple-element.21.refs_3_.refs_2_, bf16[2,128,128]{2,1,0:T(8,128)(2,1)S(1)} %and_convert_fusion.refs_3_, ...), custom_call_target="tpu_custom_call" | custom-call | tf_op jit(solution)/shard_map/pallas_call | solution.py:433
  109.2 7.4 %all-to-all-start.3 = ((f32[16,32,128]{2,1,0:T(8,128)}), f32[16,32,128]{2,1,0:T(8,128)S(1)}, u32[]{:S(2)}, u32[]{:S(2)}) async-start(f32[16,32,128]{2,1,0:T(8,128)} %shard_map.102), calls=%async_computation.3 | async-start | bytes 524288 | tf_op jit(solution)/shard_map/all_to_all | solution.py:517
  116.7 8.6 %all-to-all-done.3.refs_4_ = f32[16,32,128]{2,1,0:T(8,128)S(1)} async-done(((f32[16,32,128]{2,1,0:T(8,128)}), f32[16,32,128]{2,1,0:T(8,128)S(1)}, u32[]{:S(2)}, u32[]{:S(2)}) %all-to-all-start.3) | async-done | bytes 262176 | tf_op jit(solution)/shard_map/all_to_all | solution.py:517
  125.3 3.9 %shard_map.103 = (f32[1,64,128]{2,1,0:T(8,128)S(1)}, f32[32,128]{1,0:T(8,128)S(1)}) custom-call(s32[1048576]{0:T(1024)} %get-tuple-element.19.refs_0_, bf16[32,80,128]{2,1,0:T(8,128)(2,1)} %all-to-all-done.refs_1_, bf16[32,80,128]{2,1,0:T(8,128)(2,1)} %collective-permute-done.4.refs_2_, bf16[2,33,128,128]{3,2,1,0:T(8,128)(2,1)} %get-tuple-element.21.refs_3_.refs_2_, ...), custom_call_target="tpu_custom_call" | custom-call | tf_op jit(solution)/shard_map/pallas_call | solution.py:433
  129.4 0.6 collective-permute-start.14
  129.9 0.6 collective-permute-done.15
  130.6 4.5 %collective-permute-start.18 = (f32[8,128]{1,0:T(8,128)S(1)}, f32[8,128]{1,0:T(8,128)S(1)}, u32[]{:S(2)}, u32[]{:S(2)}) collective-permute-start(f32[8,128]{1,0:T(8,128)S(1)} %get-tuple-element.37), channel_id=1, source_target_pairs={{0,96},{32,0},{64,32},{96,64},{1,97},{33,1},{65,33},{97,65},{2,98}... | collective-permute-start | bytes 12296 | tf_op jit(solution)/shard_map/ppermute | solution.py:536
  135.1 1.9 %collective-permute-start.17 = (f32[8,128]{1,0:T(8,128)S(1)}, f32[8,128]{1,0:T(8,128)S(1)}, u32[]{:S(2)}, u32[]{:S(2)}) collective-permute-start(f32[8,128]{1,0:T(8,128)S(1)} %get-tuple-element.38), channel_id=1, source_target_pairs={{0,64},{32,96},{64,0},{96,32},{1,65},{33,97},{65,1},{97,33},{2,66}... | collective-permute-start | bytes 12296 | tf_op jit(solution)/shard_map/ppermute | solution.py:536
  137.2 0.6 maximum_bitcast_fusion
  137.9 2.3 %collective-permute-done.17 = f32[8,128]{1,0:T(8,128)S(1)} collective-permute-done((f32[8,128]{1,0:T(8,128)S(1)}, f32[8,128]{1,0:T(8,128)S(1)}, u32[]{:S(2)}, u32[]{:S(2)}) %collective-permute-start.17) | collective-permute-done | bytes 4128 | tf_op jit(solution)/shard_map/ppermute | solution.py:536
  140.3 1.5 %collective-permute-done.16 = f32[8,128]{1,0:T(8,128)S(1)} collective-permute-done((f32[8,128]{1,0:T(8,128)S(1)}, f32[8,128]{1,0:T(8,128)S(1)}, u32[]{:S(2)}, u32[]{:S(2)}) %collective-permute-start.16) | collective-permute-done | bytes 4128 | tf_op jit(solution)/shard_map/ppermute | solution.py:536
  142.0 0.6 fusion.12
  (57 shorter events, 2.2 us)
Async XLA Ops:
  0.6 5.8 %collective-permute-start = (s32[4,8]{1,0:T(4,128)}, s32[4,8]{1,0:T(4,128)}, u32[]{:S(2)}, u32[]{:S(2)}) collective-permute-start(s32[4,8]{1,0:T(4,128)} %refs_0_.1), channel_id=1, source_target_pairs={{0,32},{32,64},{64,96},{96,0},{1,33},{33,65},{65,97},{97,1},{2,34}... | collective-permute-start | bytes 392 | tf_op jit(solution)/shard_map/ppermute | solution.py:460
  2.3 5.4 %collective-permute-start.1 = (s32[4,8]{1,0:T(4,128)}, s32[4,8]{1,0:T(4,128)}, u32[]{:S(2)}, u32[]{:S(2)}) collective-permute-start(s32[4,8]{1,0:T(4,128)} %refs_0_.1), channel_id=1, source_target_pairs={{0,64},{32,96},{64,0},{96,32},{1,65},{33,97},{65,1},{97,33},{2,66}... | collective-permute-start | bytes 392 | tf_op jit(solution)/shard_map/ppermute | solution.py:460
  5.0 3.7 %collective-permute-start.2 = (s32[4,8]{1,0:T(4,128)}, s32[4,8]{1,0:T(4,128)}, u32[]{:S(2)}, u32[]{:S(2)}) collective-permute-start(s32[4,8]{1,0:T(4,128)} %refs_0_.1), channel_id=1, source_target_pairs={{0,96},{32,0},{64,32},{96,64},{1,97},{33,1},{65,33},{97,65},{2,98}... | collective-permute-start | bytes 392 | tf_op jit(solution)/shard_map/ppermute | solution.py:460
  11.0 16.0 %all-to-all-start = ((bf16[32,80,128]{2,1,0:T(8,128)(2,1)}), bf16[32,80,128]{2,1,0:T(8,128)(2,1)}, u32[]{:S(2)}, u32[]{:S(2)}) async-start(bf16[32,80,128]{2,1,0:T(8,128)(2,1)} %shard_map.95), calls=%async_computation | async-start | bytes 1310720 | tf_op jit(solution)/shard_map/all_to_all | solution.py:497
  16.5 3.8 %collective-permute-start.3 = (s32[9,64]{1,0:T(8,128)}, s32[9,64]{1,0:T(8,128)}, u32[]{:S(2)}, u32[]{:S(2)}) collective-permute-start(s32[9,64]{1,0:T(8,128)} %pad_add_fusion.1.near_ref), channel_id=1, source_target_pairs={{0,1},{1,0},{2,3},{3,2},{4,5},{5,4},{6,7},{7,6},{8,9},{9,8},{10,11... | collective-permute-start | bytes 6920 | tf_op jit(solution)/shard_map/ppermute | solution.py:460
  27.0 3.6 %collective-permute-start.4 = (bf16[32,80,128]{2,1,0:T(8,128)(2,1)}, bf16[32,80,128]{2,1,0:T(8,128)(2,1)}, u32[]{:S(2)}, u32[]{:S(2)}) collective-permute-start(bf16[32,80,128]{2,1,0:T(8,128)(2,1)} %all-to-all-done.refs_1_), channel_id=1, source_target_pairs={{0,1},{1,0},{2,3},{3,2},{4,5},{5,4},{6,7},{7,6},{8,9},{9,8},{10,11... | collective-permute-start | bytes 1966088 | tf_op jit(solution)/shard_map/ppermute | solution.py:460
  28.3 1.7 %copy-start.1 = (s32[1,4,4,8]{3,2,1,0:T(4,128)}, s32[1,4,4,8]{3,2,1,0:T(4,128)S(1)}, u32[]{:S(2)}) copy-start(s32[1,4,4,8]{3,2,1,0:T(4,128)S(1)} %get-tuple-element.45) | copy-start | bytes 1540
  28.3 2.4 %copy-start.7 = (s32[4,4,8]{2,1,0:T(4,128)}, s32[4,4,8]{2,1,0:T(4,128)S(1)}, u32[]{:S(2)}) copy-start(s32[4,4,8]{2,1,0:T(4,128)S(1)} %get-tuple-element.44) | copy-start | bytes 1540
  28.3 1.7 %collective-permute-start.5 = (s32[4,4,8]{2,1,0:T(4,128)S(1)}, s32[4,4,8]{2,1,0:T(4,128)S(1)}, u32[]{:S(2)}, u32[]{:S(2)}) collective-permute-start(s32[4,4,8]{2,1,0:T(4,128)S(1)} %get-tuple-element.44), channel_id=1, source_target_pairs={{0,1},{1,0},{2,3},{3,2},{4,5},{5,4},{6,7},{7,6},{8,9},{9,8},{10,11... | collective-permute-start | bytes 1544 | tf_op jit(solution)/shard_map/ppermute | solution.py:460
  30.1 0.6 copy-start.4
  36.4 19.9 %all-to-all-start.1 = ((f32[16,32,128]{2,1,0:T(8,128)}), f32[16,32,128]{2,1,0:T(8,128)S(1)}, u32[]{:S(2)}, u32[]{:S(2)}) async-start(f32[16,32,128]{2,1,0:T(8,128)} %get-tuple-element.24), calls=%async_computation.1 | async-start | bytes 524288 | tf_op jit(solution)/shard_map/all_to_all | solution.py:517
  46.4 14.5 %copy-start.6 = (pred[32,32]{1,0:T(8,128)(4,1)S(1)}, pred[32,32]{1,0:T(8,128)(4,1)}, u32[]{:S(2)}) copy-start(pred[32,32]{1,0:T(8,128)(4,1)} %and.70) | copy-start | bytes 3076
  48.2 18.9 %copy-start.3 = (pred[128,128]{1,0:T(8,128)(4,1)S(1)}, pred[128,128]{1,0:T(8,128)(4,1)}, u32[]{:S(2)}) copy-start(pred[128,128]{1,0:T(8,128)(4,1)} %and.76) | copy-start | bytes 49156
  60.8 1.3 collective-permute-start.6
  62.1 5.5 %collective-permute-start.7 = (f32[64,128]{1,0:T(8,128)S(1)}, f32[64,128]{1,0:T(8,128)S(1)}, u32[]{:S(2)}, u32[]{:S(2)}) collective-permute-start(f32[64,128]{1,0:T(8,128)S(1)} %multiply_add_fusion.1.refs_4_), channel_id=1, source_target_pairs={{0,32},{32,64},{64,96},{96,0},{1,33},{33,65},{65,97},{97,1},{2,34}... | collective-permute-start | bytes 98312 | tf_op jit(solution)/shard_map/ppermute | solution.py:460
  63.5 5.9 %collective-permute-start.8 = (f32[64,128]{1,0:T(8,128)S(1)}, f32[64,128]{1,0:T(8,128)S(1)}, u32[]{:S(2)}, u32[]{:S(2)}) collective-permute-start(f32[64,128]{1,0:T(8,128)S(1)} %multiply_add_fusion.1.refs_4_), channel_id=1, source_target_pairs={{0,64},{32,96},{64,0},{96,32},{1,65},{33,97},{65,1},{97,33},{2,66}... | collective-permute-start | bytes 98312 | tf_op jit(solution)/shard_map/ppermute | solution.py:460
  67.1 3.9 %collective-permute-start.9 = (f32[64,128]{1,0:T(8,128)S(1)}, f32[64,128]{1,0:T(8,128)S(1)}, u32[]{:S(2)}, u32[]{:S(2)}) collective-permute-start(f32[64,128]{1,0:T(8,128)S(1)} %multiply_add_fusion.1.refs_4_), channel_id=1, source_target_pairs={{0,96},{32,0},{64,32},{96,64},{1,97},{33,1},{65,33},{97,65},{2,98}... | collective-permute-start | bytes 98312 | tf_op jit(solution)/shard_map/ppermute | solution.py:460
  74.9 19.0 %copy-start = (bf16[4096,64]{0,1:T(8,128)(2,1)S(1)}, bf16[4096,64]{0,1:T(8,128)(2,1)}, u32[]{:S(2)}) copy-start(bf16[4096,64]{0,1:T(8,128)(2,1)} %param.10) | copy-start | bytes 1572868
  93.7 1.3 collective-permute-start.10
  95.1 7.5 %collective-permute-start.11 = (f32[64,128]{1,0:T(8,128)S(1)}, f32[64,128]{1,0:T(8,128)S(1)}, u32[]{:S(2)}, u32[]{:S(2)}) collective-permute-start(f32[64,128]{1,0:T(8,128)S(1)} %multiply_add_fusion.refs_4_), channel_id=1, source_target_pairs={{0,32},{32,64},{64,96},{96,0},{1,33},{33,65},{65,97},{97,1},{2,34}... | collective-permute-start | bytes 98312 | tf_op jit(solution)/shard_map/ppermute | solution.py:460
  99.1 5.4 %collective-permute-start.12 = (f32[64,128]{1,0:T(8,128)S(1)}, f32[64,128]{1,0:T(8,128)S(1)}, u32[]{:S(2)}, u32[]{:S(2)}) collective-permute-start(f32[64,128]{1,0:T(8,128)S(1)} %multiply_add_fusion.refs_4_), channel_id=1, source_target_pairs={{0,64},{32,96},{64,0},{96,32},{1,65},{33,97},{65,1},{97,33},{2,66}... | collective-permute-start | bytes 98312 | tf_op jit(solution)/shard_map/ppermute | solution.py:460
  100.7 3.9 %collective-permute-start.13 = (f32[64,128]{1,0:T(8,128)S(1)}, f32[64,128]{1,0:T(8,128)S(1)}, u32[]{:S(2)}, u32[]{:S(2)}) collective-permute-start(f32[64,128]{1,0:T(8,128)S(1)} %multiply_add_fusion.refs_4_), channel_id=1, source_target_pairs={{0,96},{32,0},{64,32},{96,64},{1,97},{33,1},{65,33},{97,65},{2,98}... | collective-permute-start | bytes 98312 | tf_op jit(solution)/shard_map/ppermute | solution.py:460
  109.2 20.2 %copy-start.5 = (f32[32,128]{1,0:T(8,128)S(1)}, f32[32,128]{1,0:T(8,128)}, u32[]{:S(2)}) copy-start(f32[32,128]{1,0:T(8,128)} %get-tuple-element.28) | copy-start | bytes 49156
  109.2 16.1 %all-to-all-start.3 = ((f32[16,32,128]{2,1,0:T(8,128)}), f32[16,32,128]{2,1,0:T(8,128)S(1)}, u32[]{:S(2)}, u32[]{:S(2)}) async-start(f32[16,32,128]{2,1,0:T(8,128)} %shard_map.102), calls=%async_computation.3 | async-start | bytes 524288 | tf_op jit(solution)/shard_map/all_to_all | solution.py:517
  116.6 25.3 %copy-start.2 = (f32[4096]{0:T(1024)S(1)}, f32[4096]{0:T(1024)}, u32[]{:S(2)}) copy-start(f32[4096]{0:T(1024)} %param.11) | copy-start | bytes 49156
  129.3 1.3 collective-permute-start.15
  129.4 7.8 %collective-permute-start.14 = (f32[32,128]{1,0:T(8,128)S(1)}, f32[32,128]{1,0:T(8,128)S(1)}, u32[]{:S(2)}, u32[]{:S(2)}) collective-permute-start(f32[32,128]{1,0:T(8,128)S(1)} %multiply_add_fusion.2), channel_id=1, source_target_pairs={{0,1},{1,0},{2,3},{3,2},{4,5},{5,4},{6,7},{7,6},{8,9},{9,8},{10,11... | collective-permute-start | bytes 49160 | tf_op jit(solution)/shard_map/ppermute | solution.py:460
  130.6 7.2 %collective-permute-start.18 = (f32[8,128]{1,0:T(8,128)S(1)}, f32[8,128]{1,0:T(8,128)S(1)}, u32[]{:S(2)}, u32[]{:S(2)}) collective-permute-start(f32[8,128]{1,0:T(8,128)S(1)} %get-tuple-element.37), channel_id=1, source_target_pairs={{0,96},{32,0},{64,32},{96,64},{1,97},{33,1},{65,33},{97,65},{2,98}... | collective-permute-start | bytes 12296 | tf_op jit(solution)/shard_map/ppermute | solution.py:536
  135.1 5.1 %collective-permute-start.17 = (f32[8,128]{1,0:T(8,128)S(1)}, f32[8,128]{1,0:T(8,128)S(1)}, u32[]{:S(2)}, u32[]{:S(2)}) collective-permute-start(f32[8,128]{1,0:T(8,128)S(1)} %get-tuple-element.38), channel_id=1, source_target_pairs={{0,64},{32,96},{64,0},{96,32},{1,65},{33,97},{65,1},{97,33},{2,66}... | collective-permute-start | bytes 12296 | tf_op jit(solution)/shard_map/ppermute | solution.py:536
  137.0 4.8 %collective-permute-start.16 = (f32[8,128]{1,0:T(8,128)S(1)}, f32[8,128]{1,0:T(8,128)S(1)}, u32[]{:S(2)}, u32[]{:S(2)}) collective-permute-start(f32[8,128]{1,0:T(8,128)S(1)} %get-tuple-element.39), channel_id=1, source_target_pairs={{0,32},{32,64},{64,96},{96,0},{1,33},{33,65},{65,97},{97,1},{2,34}... | collective-permute-start | bytes 12296 | tf_op jit(solution)/shard_map/ppermute | solution.py:536
